TPU v7x, 32 devices: a whole 2x2x4 slice. The times are simulated.
32 devices in a mesh: fsdp: 4 (over z), sp: 8 (over y, x, core).
Axes of the slice: x: 2, y: 2, z: 4, core: 2. Of those that a mesh axis runs over, the one named last changes fastest.
Arguments:
- tokens: bfloat16 [4, 4096, 2048], P('fsdp', 'sp'), may hold values from -6 to 6
- cotangent: bfloat16 [4, 4096, 2048], P('fsdp', 'sp'), may hold values from -6 to 6
- first_gain: bfloat16 [2048], P(('fsdp', 'sp')), may hold values from 0.5 to 1.5
- first_shift: bfloat16 [2048], P(('fsdp', 'sp')), may hold values from -1.1953125 to 1.1953125
- joint_weight: bfloat16 [2048, 6144], P(('fsdp', 'sp')), may hold values from -0.125 to 0.125
- joint_bias: bfloat16 [6144], P(('fsdp', 'sp')), may hold values from -0.29882812 to 0.29882812
- out_weight: bfloat16 [2048, 2048], P(('fsdp', 'sp')), may hold values from -1 to 1
- second_gain: bfloat16 [2048], P(('fsdp', 'sp')), may hold values from 0.5 to 1.5
- second_shift: bfloat16 [2048], P(('fsdp', 'sp')), may hold values from -1.1953125 to 1.1953125
- gate_weight: bfloat16 [2048, 5632], P(('fsdp', 'sp')), may hold values from -0.125 to 0.125
- up_weight: bfloat16 [2048, 5632], P(('fsdp', 'sp')), may hold values from -0.125 to 0.125
- down_weight: bfloat16 [5632, 2048], P(('fsdp', 'sp')), may hold values from -0.15625 to 0.15625
Outputs:
- output: bfloat16 [4, 4096, 2048], P('fsdp', 'sp')
- tokens_grad: float32 [4, 4096, 2048], P('fsdp', 'sp')
- first_gain_grad: float32 [2048], P(('fsdp', 'sp'))
- first_shift_grad: float32 [2048], P(('fsdp', 'sp'))
- joint_weight_grad: float32 [2048, 6144], P(('fsdp', 'sp'))
- joint_bias_grad: float32 [6144], P(('fsdp', 'sp'))
- out_weight_grad: float32 [2048, 2048], P(('fsdp', 'sp'))
- second_gain_grad: float32 [2048], P(('fsdp', 'sp'))
- second_shift_grad: float32 [2048], P(('fsdp', 'sp'))
- gate_weight_grad: float32 [2048, 5632], P(('fsdp', 'sp'))
- up_weight_grad: float32 [2048, 5632], P(('fsdp', 'sp'))
- down_weight_grad: float32 [5632, 2048], P(('fsdp', 'sp'))
All inputs are finite; a program needn't handle non-finite values.
Results may differ from a plain program's by a relative error of at most 0.013.
Values may be sent and summed in bfloat16 or wider, within the bound.
No kernel may reach another device: no remote copies, remote signals or barrier semaphores. Data moves between devices by JAX's collectives and lax.ppermute only.
A program may use at most 448 MiB of HBM per device.

v0:
```python
import jax
import jax.numpy as jnp
from jax import lax
from jax.sharding import PartitionSpec as P

D = 2048
HEADS = 32
HEAD = 64
ROT = 16


epsilon = 1e-05
masked_value = -1e30


def layer_norm(values, gain_vec, shift_vec):
    center = values - jnp.mean(values, axis=-1, keepdims=True)
    spread = jnp.mean(center * center, axis=-1, keepdims=True)
    return center * lax.rsqrt(spread + epsilon) * gain_vec + shift_vec


def rotary_tables(positions):
    indices = jnp.arange(ROT // 2, dtype=jnp.float32)
    inverse = 1.0 / 10000.0 ** (indices * 2.0 / ROT)
    angles = positions[:, None] * inverse[None, :]
    angles = jnp.concatenate([angles, angles], axis=-1)
    return (jnp.cos(angles), jnp.sin(angles))


def rotate(vectors, cosine, sine_table):
    turned = vectors[..., :ROT]
    first_half = turned[..., : ROT // 2]
    second_half = turned[..., ROT // 2 :]
    flipped = jnp.concatenate([-second_half, first_half], axis=-1)
    rotated = turned * cosine[:, None, :] + flipped * sine_table[:, None, :]
    return jnp.concatenate([rotated, vectors[..., ROT:]], axis=-1)


def swish_product(gate_value, up_value):
    return gate_value * jax.nn.sigmoid(gate_value) * up_value


def block_layout(length):
    block_rows = min(512, length)
    block_count = length // block_rows
    starts = jnp.arange(block_count, dtype=jnp.int32) * block_rows
    return (block_rows, block_count, starts)


def attend(queries, all_keys, values):
    seq_count, length, head_count, head_size = queries.shape
    block_rows, block_count, starts = block_layout(length)
    factor = HEAD ** (-0.5)
    blocks = jnp.moveaxis(
        queries.reshape(seq_count, block_count, block_rows, head_count, head_size), 1, 0
    )
    col_ids = jnp.arange(length, dtype=jnp.int32)

    def one_block(entry):
        first_row, piece_rows = entry
        scores = (
            jnp.einsum("sqhe,skhe->shqk", piece_rows, all_keys, preferred_element_type=jnp.float32)
            * factor
        )
        row_ids = first_row + jnp.arange(block_rows, dtype=jnp.int32)
        allowed = col_ids[None, :] <= row_ids[:, None]
        scores = jnp.where(allowed, scores, masked_value)
        largest = jnp.max(scores, axis=-1, keepdims=True)
        raised = jnp.exp(scores - largest)
        totals = jnp.sum(raised, axis=-1, keepdims=True)
        probs_low = (raised / totals).astype(jnp.bfloat16)
        results = jnp.einsum(
            "shqk,skhe->sqhe", probs_low, values, preferred_element_type=jnp.float32
        )
        return (results.astype(jnp.bfloat16), largest + jnp.log(totals))

    results, logsum = lax.map(one_block, (starts, blocks))
    return (jnp.moveaxis(results, 0, 1).reshape(seq_count, length, head_count * head_size), logsum)


def attend_back(queries, all_keys, values, logsum, result_grad):
    seq_count, length, head_count, head_size = queries.shape
    block_rows, block_count, starts = block_layout(length)
    factor = HEAD ** (-0.5)
    blocks = jnp.moveaxis(
        queries.reshape(seq_count, block_count, block_rows, head_count, head_size), 1, 0
    )
    grad_blocks = jnp.moveaxis(
        result_grad.reshape(seq_count, block_count, block_rows, head_count, head_size), 1, 0
    )
    col_ids = jnp.arange(length, dtype=jnp.int32)

    def one_block(carry, entry):
        keys_sum, values_sum = carry
        first_row, piece_rows, piece_grad, piece_logsum = entry
        scores = (
            jnp.einsum("sqhe,skhe->shqk", piece_rows, all_keys, preferred_element_type=jnp.float32)
            * factor
        )
        row_ids = first_row + jnp.arange(block_rows, dtype=jnp.int32)
        allowed = col_ids[None, :] <= row_ids[:, None]
        attn_probs = jnp.where(allowed, jnp.exp(scores - piece_logsum), 0.0)
        probs_grad = jnp.einsum(
            "sqhe,skhe->shqk", piece_grad, values, preferred_element_type=jnp.float32
        )
        inner_sum = jnp.sum(attn_probs * probs_grad, axis=-1, keepdims=True)
        scores_grad = (attn_probs * (probs_grad - inner_sum)).astype(jnp.bfloat16)
        query_part = (
            jnp.einsum("shqk,skhe->sqhe", scores_grad, all_keys, preferred_element_type=jnp.float32)
            * factor
        )
        keys_sum = (
            keys_sum
            + jnp.einsum(
                "shqk,sqhe->skhe", scores_grad, piece_rows, preferred_element_type=jnp.float32
            )
            * factor
        )
        values_sum = values_sum + jnp.einsum(
            "shqk,sqhe->skhe",
            attn_probs.astype(jnp.bfloat16),
            piece_grad,
            preferred_element_type=jnp.float32,
        )
        return ((keys_sum, values_sum), query_part)

    zero_grid = jnp.zeros((seq_count, length, head_count, head_size), jnp.float32)
    (keys_sum, values_sum), query_parts = lax.scan(
        one_block, (zero_grid, zero_grid), (starts, blocks, grad_blocks, logsum)
    )
    query_sum = jnp.moveaxis(query_parts, 0, 1)
    flat_shape = (seq_count, length, head_count * head_size)
    return (
        query_sum.reshape(flat_shape).astype(jnp.bfloat16),
        keys_sum.reshape(flat_shape).astype(jnp.bfloat16),
        values_sum.reshape(flat_shape).astype(jnp.bfloat16),
    )


def per_device(
    tokens,
    cotangent,
    first_gain,
    first_shift,
    joint_weight,
    joint_bias,
    out_weight,
    second_gain,
    second_shift,
    gate_weight,
    up_weight,
    down_weight,
):
    sp_count = lax.axis_size("sp")
    seq_count = tokens.shape[0]
    span_rows = tokens.shape[1]
    row_count = seq_count * span_rows
    local_heads = HEADS // sp_count
    positions = (lax.axis_index("sp") * span_rows + jnp.arange(span_rows, dtype=jnp.int32)).astype(
        jnp.float32
    )
    cosine, sine_table = rotary_tables(positions)
    gain_one, shift_one, joint_full, joint_bias_full, out_full = (
        lax.all_gather(first_gain, ("fsdp", "sp"), axis=0, tiled=True),
        lax.all_gather(first_shift, ("fsdp", "sp"), axis=0, tiled=True),
        lax.all_gather(joint_weight, ("fsdp", "sp"), axis=0, tiled=True),
        lax.all_gather(joint_bias, ("fsdp", "sp"), axis=0, tiled=True),
        lax.all_gather(out_weight, ("fsdp", "sp"), axis=0, tiled=True),
    )
    inputs = tokens.astype(jnp.float32).reshape(row_count, D)
    normed, first_pull = jax.vjp(
        layer_norm, inputs, gain_one.astype(jnp.float32), shift_one.astype(jnp.float32)
    )
    normed_low = normed.astype(jnp.bfloat16)
    projected = jnp.dot(
        normed_low, joint_full, preferred_element_type=jnp.float32
    ) + joint_bias_full.astype(jnp.float32)
    projected = projected.reshape(seq_count, span_rows, 3, HEADS, HEAD)

    def turn_pair(query_pre, key_pre):
        return (rotate(query_pre, cosine, sine_table), rotate(key_pre, cosine, sine_table))

    (query_turned, key_turned), turn_pull = jax.vjp(
        turn_pair, projected[:, :, 0], projected[:, :, 1]
    )
    row_shape = (seq_count, span_rows, D)
    query_low = query_turned.astype(jnp.bfloat16).reshape(row_shape)
    key_low = key_turned.astype(jnp.bfloat16).reshape(row_shape)
    value_low = projected[:, :, 2].astype(jnp.bfloat16).reshape(row_shape)
    query_heads, key_heads, value_heads = (
        lax.all_to_all(query_low, "sp", split_axis=2, concat_axis=1, tiled=True),
        lax.all_to_all(key_low, "sp", split_axis=2, concat_axis=1, tiled=True),
        lax.all_to_all(value_low, "sp", split_axis=2, concat_axis=1, tiled=True),
    )
    length = query_heads.shape[1]
    head_shape = (seq_count, length, local_heads, HEAD)
    query_grid = query_heads.reshape(head_shape)
    key_grid = key_heads.reshape(head_shape)
    value_grid = value_heads.reshape(head_shape)
    attended_heads, logsum = attend(query_grid, key_grid, value_grid)
    attended_rows = lax.all_to_all(
        attended_heads, "sp", split_axis=1, concat_axis=2, tiled=True
    ).reshape(row_count, D)
    middle = inputs + jnp.dot(attended_rows, out_full, preferred_element_type=jnp.float32)
    gain_two, shift_two, gate_full, up_full, down_full = (
        lax.all_gather(second_gain, ("fsdp", "sp"), axis=0, tiled=True),
        lax.all_gather(second_shift, ("fsdp", "sp"), axis=0, tiled=True),
        lax.all_gather(gate_weight, ("fsdp", "sp"), axis=0, tiled=True),
        lax.all_gather(up_weight, ("fsdp", "sp"), axis=0, tiled=True),
        lax.all_gather(down_weight, ("fsdp", "sp"), axis=0, tiled=True),
    )
    normed_two, second_pull = jax.vjp(
        layer_norm, middle, gain_two.astype(jnp.float32), shift_two.astype(jnp.float32)
    )
    normed_two_low = normed_two.astype(jnp.bfloat16)
    gate_value = jnp.dot(normed_two_low, gate_full, preferred_element_type=jnp.float32)
    up_value = jnp.dot(normed_two_low, up_full, preferred_element_type=jnp.float32)
    hidden, swish_pull = jax.vjp(swish_product, gate_value, up_value)
    hidden_low = hidden.astype(jnp.bfloat16)
    output = (
        (middle + jnp.dot(hidden_low, down_full, preferred_element_type=jnp.float32))
        .astype(jnp.bfloat16)
        .reshape(row_shape)
    )
    grad_rows = cotangent.reshape(row_count, D)
    gate_back, up_back, down_back = (
        lax.all_gather(gate_weight, ("fsdp", "sp"), axis=0, tiled=True),
        lax.all_gather(up_weight, ("fsdp", "sp"), axis=0, tiled=True),
        lax.all_gather(down_weight, ("fsdp", "sp"), axis=0, tiled=True),
    )
    down_sum = jnp.einsum("rf,rd->fd", hidden_low, grad_rows, preferred_element_type=jnp.float32)
    hidden_grad = jnp.einsum("rd,fd->rf", grad_rows, down_back, preferred_element_type=jnp.float32)
    gate_grad, up_grad = swish_pull(hidden_grad)
    gate_grad_low = gate_grad.astype(jnp.bfloat16)
    up_grad_low = up_grad.astype(jnp.bfloat16)
    gate_sum = jnp.einsum(
        "rd,rf->df", normed_two_low, gate_grad_low, preferred_element_type=jnp.float32
    )
    up_sum = jnp.einsum(
        "rd,rf->df", normed_two_low, up_grad_low, preferred_element_type=jnp.float32
    )
    normed_two_grad = jnp.einsum(
        "rf,df->rd", gate_grad_low, gate_back, preferred_element_type=jnp.float32
    )
    normed_two_grad = normed_two_grad + jnp.einsum(
        "rf,df->rd", up_grad_low, up_back, preferred_element_type=jnp.float32
    )
    middle_norm_grad, gain_two_sum, shift_two_sum = second_pull(normed_two_grad)
    mlp_sums = (
        lax.psum_scatter(gain_two_sum, ("fsdp", "sp"), scatter_dimension=0, tiled=True),
        lax.psum_scatter(shift_two_sum, ("fsdp", "sp"), scatter_dimension=0, tiled=True),
        lax.psum_scatter(gate_sum, ("fsdp", "sp"), scatter_dimension=0, tiled=True),
        lax.psum_scatter(up_sum, ("fsdp", "sp"), scatter_dimension=0, tiled=True),
        lax.psum_scatter(down_sum, ("fsdp", "sp"), scatter_dimension=0, tiled=True),
    )
    middle_grad = grad_rows.astype(jnp.float32) + middle_norm_grad
    branch_grad = middle_grad.astype(jnp.bfloat16)
    joint_back, out_back = (
        lax.all_gather(joint_weight, ("fsdp", "sp"), axis=0, tiled=True),
        lax.all_gather(out_weight, ("fsdp", "sp"), axis=0, tiled=True),
    )
    out_sum = jnp.einsum(
        "rd,re->de", attended_rows, branch_grad, preferred_element_type=jnp.float32
    )
    attended_grad = (
        jnp.einsum("re,de->rd", branch_grad, out_back, preferred_element_type=jnp.float32)
        .astype(jnp.bfloat16)
        .reshape(row_shape)
    )
    attended_grad_heads = lax.all_to_all(
        attended_grad, "sp", split_axis=2, concat_axis=1, tiled=True
    ).reshape(head_shape)
    query_grad, key_grad, value_grad = attend_back(
        query_grid, key_grid, value_grid, logsum, attended_grad_heads
    )
    query_back, key_back, value_back = (
        lax.all_to_all(query_grad, "sp", split_axis=1, concat_axis=2, tiled=True),
        lax.all_to_all(key_grad, "sp", split_axis=1, concat_axis=2, tiled=True),
        lax.all_to_all(value_grad, "sp", split_axis=1, concat_axis=2, tiled=True),
    )
    grid_shape = (seq_count, span_rows, HEADS, HEAD)
    query_pre_grad, key_pre_grad = turn_pull(
        (
            query_back.astype(jnp.float32).reshape(grid_shape),
            key_back.astype(jnp.float32).reshape(grid_shape),
        )
    )
    projected_grad = jnp.stack(
        [query_pre_grad, key_pre_grad, value_back.astype(jnp.float32).reshape(grid_shape)], axis=2
    )
    projected_grad = projected_grad.reshape(row_count, 3 * D).astype(jnp.bfloat16)
    joint_bias_sum = jnp.sum(projected_grad.astype(jnp.float32), axis=0)
    joint_sum = jnp.einsum(
        "rd,re->de", normed_low, projected_grad, preferred_element_type=jnp.float32
    )
    normed_grad = jnp.einsum(
        "re,de->rd", projected_grad, joint_back, preferred_element_type=jnp.float32
    )
    inputs_norm_grad, gain_one_sum, shift_one_sum = first_pull(normed_grad)
    tokens_grad = (middle_grad + inputs_norm_grad).reshape(row_shape)
    attn_sums = (
        lax.psum_scatter(gain_one_sum, ("fsdp", "sp"), scatter_dimension=0, tiled=True),
        lax.psum_scatter(shift_one_sum, ("fsdp", "sp"), scatter_dimension=0, tiled=True),
        lax.psum_scatter(joint_sum, ("fsdp", "sp"), scatter_dimension=0, tiled=True),
        lax.psum_scatter(joint_bias_sum, ("fsdp", "sp"), scatter_dimension=0, tiled=True),
        lax.psum_scatter(out_sum, ("fsdp", "sp"), scatter_dimension=0, tiled=True),
    )
    return (
        output,
        tokens_grad,
        attn_sums[0],
        attn_sums[1],
        attn_sums[2],
        attn_sums[3],
        attn_sums[4],
        mlp_sums[0],
        mlp_sums[1],
        mlp_sums[2],
        mlp_sums[3],
        mlp_sums[4],
    )


def solution(mesh):
    return jax.shard_map(
        per_device,
        mesh=mesh,
        in_specs=(
            P("fsdp", "sp", None),
            P("fsdp", "sp", None),
            P(("fsdp", "sp")),
            P(("fsdp", "sp")),
            P(("fsdp", "sp"), None),
            P(("fsdp", "sp")),
            P(("fsdp", "sp"), None),
            P(("fsdp", "sp")),
            P(("fsdp", "sp")),
            P(("fsdp", "sp"), None),
            P(("fsdp", "sp"), None),
            P(("fsdp", "sp"), None),
        ),
        out_specs=(
            P("fsdp", "sp", None),
            P("fsdp", "sp", None),
            P(("fsdp", "sp")),
            P(("fsdp", "sp")),
            P(("fsdp", "sp"), None),
            P(("fsdp", "sp")),
            P(("fsdp", "sp"), None),
            P(("fsdp", "sp")),
            P(("fsdp", "sp")),
            P(("fsdp", "sp"), None),
            P(("fsdp", "sp"), None),
            P(("fsdp", "sp"), None),
        ),
        check_vma=False,
    )
```

profile of v0, /device:TPU:0, one launch (start us, length us, event | category | flops | bytes accessed | tf_op | source)
XLA Modules:
  0.0 4140.9 jit_solution(2290314971066373908)
XLA Ops:
  14.2 44.0 %all-reduce.19 = (bf16[6144]{0:T(1024)(128)(2,1)S(1)}, bf16[2048]{0:T(1024)(128)(2,1)S(1)}, bf16[2048]{0:T(1024)(128)(2,1)S(1)}, bf16[2048]{0:T(1024)(128)(2,1)}, bf16[2048]{0:T(1024)(128)(2,1)}) all-reduce(bf16[6144]{0:T(1024)(128)(2,1)S(1)} %dynamic-update-slice.2, ...), channel_id=1, replica_groups=mesh['fsdp'=4,'sp'=8] {'fsdp','sp'}, use_global_device_ids=true, to_apply=%add.10 | all-reduce | flops 14336 | bytes 57344
  59.6 110.0 %all-gather.6.cloned.1.call-done = bf16[2048,6144]{1,0:T(8,128)(2,1)} async-done(((bf16[64,6144]{1,0:T(8,128)(2,1)}), bf16[2048,6144]{1,0:T(8,128)(2,1)}) %all-gather.6.cloned.1.call-update) | async-done | bytes 25165840 | tf_op jit(solution)/shard_map/all_gather | solution.py:166
  410.1 412.8 %while.28 = (s32[]{:T(128)}, bf16[8,1,512,4,64]{2,4,3,1,0:T(8,128)(2,1)}, f32[8,1,4,512,1]{3,2,4,1,0:T(4,128)}, s32[8]{0:T(128)S(1)}, bf16[8,1,512,4,64]{2,4,3,1...) while((s32[]{:T(128)}, ...), condition=%wide.region_5.6_spmd.clone, body=%wide.region_2.5_spmd.clone.sunk | while | flops 2250373632 | bytes 122228888 | solution.py:77
  874.1 26.5 all-to-all-done.3
  963.9 26.7 multiply_convert_fusion.1
  1087.1 32.5 all-to-all-done.4
  1130.7 879.0 %while.29 = (s32[]{:T(128)}, f32[1,4096,4,64]{1,3,2,0:T(8,128)}, f32[1,4096,4,64]{1,3,2,0:T(8,128)}, bf16[8,1,512,4,64]{2,4,3,1,0:T(8,128)(2,1)}, bf16[8,1,512,4...) while((s32[]{:T(128)}, f32[1,4096,4,64]{1,3,2,0:T(8,128)}, ...), condition=%wide.region_12.13_spmd.clone, body=%wide.region_10.12_spmd.clone.sunk | while | flops 5502007808 | bytes 301527264 | solution.py:128
  1149.0 24.6 multiply_reduce_fusion.5
  1173.6 28.5 multiply_convert_fusion.4
  1258.1 24.7 multiply_reduce_fusion.5
  1282.8 27.7 multiply_convert_fusion.4
  1392.6 27.7 multiply_convert_fusion.4
  1502.4 27.7 multiply_convert_fusion.4
  1612.3 27.7 multiply_convert_fusion.4
  1722.1 27.7 multiply_convert_fusion.4
  1831.9 27.7 multiply_convert_fusion.4
  1941.7 27.7 multiply_convert_fusion.4
  2224.0 34.0 fusion.123
  2258.1 33.5 fusion.124
  2359.9 42.9 %all-reduce.18 = (f32[2048]{0:T(1024)S(1)}, f32[2048]{0:T(1024)S(1)}, f32[6144]{0:T(1024)S(1)}, f32[2048]{0:T(1024)S(1)}, f32[2048]{0:T(1024)S(1)}) all-reduce(f32[2048]{0:T(1024)S(1)} %get-tuple-element.189, f32[2048]{0:T(1024)S(1)} %get-tuple-element.192, ...), channel_id=2, replica_groups=mesh['fsdp'=4,'sp'=8] {'fsdp','sp'}, use_global_device_ids=true, to_apply=%region_16.17.clone | all-reduce | flops 14336 | bytes 114688
  2412.5 242.8 %reduce-scatter.6.cloned.1.call-done = f32[64,6144]{1,0:T(8,128)} async-done(((f32[2048,6144]{1,0:T(8,128)}), f32[64,6144]{1,0:T(8,128)}) %reduce-scatter.6.cloned.1.call-update) | async-done | bytes 1572880 | tf_op jit(solution)/shard_map/reduce_scatter | solution.py:304
  2655.2 486.9 %reduce-scatter.10.cloned.1.call-done = f32[64,5632]{1,0:T(8,128)} async-done(((f32[2048,5632]{1,0:T(8,128)}), f32[64,5632]{1,0:T(8,128)}) %reduce-scatter.10.cloned.1.call-update) | async-done | bytes 1441808 | tf_op jit(solution)/shard_map/reduce_scatter | solution.py:252
  3142.1 496.0 %reduce-scatter.12.cloned.1.call-done = f32[64,5632]{1,0:T(8,128)} async-done(((f32[2048,5632]{1,0:T(8,128)}), f32[64,5632]{1,0:T(8,128)}) %reduce-scatter.12.cloned.1.call-update) | async-done | bytes 1441808 | tf_op jit(solution)/shard_map/reduce_scatter | solution.py:253
  3638.1 495.8 %reduce-scatter.14.cloned.1.call-done = f32[176,2048]{1,0:T(8,128)} async-done(((f32[5632,2048]{1,0:T(8,128)}), f32[176,2048]{1,0:T(8,128)}) %reduce-scatter.14.cloned.1.call-update) | async-done | bytes 1441808 | tf_op jit(solution)/shard_map/reduce_scatter | solution.py:254
  (433 shorter events, 1781.5 us)
Async XLA Ops:
  7.2 162.5 %all-gather.6.cloned.1.call-start = ((), (), s32[]{:S(2)}) async-start(), calls=%async_computation.13 | async-start | bytes 25952256 | tf_op jit(solution)/shard_map/all_gather | solution.py:166
  7.9 905.0 %all-gather.8.cloned.1.call-start = ((), (), s32[]{:S(2)}) async-start(), calls=%async_computation.14 | async-start | bytes 8650752 | tf_op jit(solution)/shard_map/all_gather | solution.py:168
  8.7 914.9 %all-gather.10.cloned.1.call-start = ((), (), s32[]{:S(2)}) async-start(), calls=%async_computation.15 | async-start | bytes 23789568 | tf_op jit(solution)/shard_map/all_gather | solution.py:208
  9.4 934.5 %all-gather.12.cloned.1.call-start = ((), (), s32[]{:S(2)}) async-start(), calls=%async_computation.16 | async-start | bytes 23789568 | tf_op jit(solution)/shard_map/all_gather | solution.py:209
  58.3 132.2 %copy-start.41 = (f32[2048]{0:T(1024)}, f32[2048]{0:T(1024)S(1)}, u32[]{:S(2)}) copy-start(f32[2048]{0:T(1024)S(1)} %convert_element_type.268) | copy-start | bytes 24580
  58.3 132.2 %copy-start.28 = (f32[2048]{0:T(1024)}, f32[2048]{0:T(1024)S(1)}, u32[]{:S(2)}) copy-start(f32[2048]{0:T(1024)S(1)} %convert_element_type.267) | copy-start | bytes 24580
  58.5 149.7 %copy-start.23 = (f32[512,16]{0,1:T(8,128)}, f32[512,16]{0,1:T(8,128)S(1)}, u32[]{:S(2)}) copy-start(f32[512,16]{0,1:T(8,128)S(1)} %get-tuple-element.265) | copy-start | bytes 98308
  58.5 149.7 %copy-start.25 = (f32[512,16]{0,1:T(8,128)}, f32[512,16]{0,1:T(8,128)S(1)}, u32[]{:S(2)}) copy-start(f32[512,16]{0,1:T(8,128)S(1)} %get-tuple-element.266) | copy-start | bytes 98308
  58.9 131.6 %copy-start.30 = (f32[512]{0:T(512)}, f32[512]{0:T(512)S(1)}, u32[]{:S(2)}) copy-start(f32[512]{0:T(512)S(1)} %broadcast_multiply_fusion.2) | copy-start | bytes 6148
  59.6 130.9 %copy-start.37 = (f32[512]{0:T(512)}, f32[512]{0:T(512)S(1)}, u32[]{:S(2)}) copy-start(f32[512]{0:T(512)S(1)} %fusion.80) | copy-start | bytes 6148
  247.2 46.2 %all-to-all-start = ((bf16[8,2,65536]{2,1,0:T(2,128)(2,1)}), bf16[8,2,65536]{2,1,0:T(2,128)(2,1)S(1)}, u32[]{:S(2)}, u32[]{:S(2)}) async-start(bf16[8,2,65536]{2,1,0:T(2,128)(2,1)} %reshape.643), calls=%async_computation | async-start | bytes 4194304 | tf_op jit(solution)/shard_map/all_to_all | solution.py:191
  293.4 47.3 %all-to-all-start.1 = ((bf16[8,2,65536]{2,1,0:T(2,128)(2,1)}), bf16[8,2,65536]{2,1,0:T(2,128)(2,1)}, u32[]{:S(2)}, u32[]{:S(2)}) async-start(bf16[8,2,65536]{2,1,0:T(2,128)(2,1)} %reshape.645), calls=%async_computation.1 | async-start | bytes 4194304 | tf_op jit(solution)/shard_map/all_to_all | solution.py:192
  340.7 53.2 %all-to-all-start.2 = ((bf16[8,2,65536]{2,1,0:T(2,128)(2,1)}), bf16[8,2,65536]{2,1,0:T(2,128)(2,1)}, u32[]{:S(2)}, u32[]{:S(2)}) async-start(bf16[8,2,65536]{2,1,0:T(2,128)(2,1)} %reshape.647), calls=%async_computation.2 | async-start | bytes 4194304 | tf_op jit(solution)/shard_map/all_to_all | solution.py:193
  345.1 618.8 %all-gather.14.cloned.1.call-start = ((), (), s32[]{:S(2)}) async-start(), calls=%async_computation.17 | async-start | bytes 23789568 | tf_op jit(solution)/shard_map/all_gather | solution.py:210
  870.5 30.2 all-to-all-start.3
  1072.8 46.8 %all-to-all-start.4 = ((bf16[8,2,65536]{2,1,0:T(2,128)(2,1)}), bf16[8,2,65536]{2,1,0:T(2,128)(2,1)}, u32[]{:S(2)}, u32[]{:S(2)}) async-start(bf16[8,2,65536]{2,1,0:T(2,128)(2,1)} %reshape.651), calls=%async_computation.4 | async-start | bytes 4194304 | tf_op jit(solution)/shard_map/all_to_all | solution.py:270
  1077.2 1335.3 %reduce-scatter.8.cloned.1.call-start = ((), (), s32[]{:S(2)}) async-start(), calls=%async_computation.19 | async-start | bytes 17301504 | tf_op jit(solution)/shard_map/reduce_scatter | solution.py:306
  2044.3 54.6 %all-to-all-start.7 = ((bf16[8,2,65536]{2,1,0:T(2,128)(2,1)}), bf16[8,2,65536]{2,1,0:T(2,128)(2,1)S(1)}, u32[]{:S(2)}, u32[]{:S(2)}) async-start(bf16[8,2,65536]{2,1,0:T(2,128)(2,1)} %reshape.653), calls=%async_computation.7 | async-start | bytes 4194304 | tf_op jit(solution)/shard_map/all_to_all | solution.py:279
  2098.9 43.0 %all-to-all-start.5 = ((bf16[8,2,65536]{2,1,0:T(2,128)(2,1)}), bf16[8,2,65536]{2,1,0:T(2,128)(2,1)}, u32[]{:S(2)}, u32[]{:S(2)}) async-start(bf16[8,2,65536]{2,1,0:T(2,128)(2,1)} %reshape.657), calls=%async_computation.5 | async-start | bytes 4194304 | tf_op jit(solution)/shard_map/all_to_all | solution.py:277
  2141.8 31.0 all-to-all-start.6
  2146.2 509.1 %reduce-scatter.6.cloned.1.call-start = ((), (), s32[]{:S(2)}) async-start(), calls=%async_computation.18 | async-start | bytes 51904512 | tf_op jit(solution)/shard_map/reduce_scatter | solution.py:304
  2224.0 918.1 %reduce-scatter.10.cloned.1.call-start = ((), (), s32[]{:S(2)}) async-start(), calls=%async_computation.20 | async-start | bytes 47579136 | tf_op jit(solution)/shard_map/reduce_scatter | solution.py:252
  2258.0 1380.1 %reduce-scatter.12.cloned.1.call-start = ((), (), s32[]{:S(2)}) async-start(), calls=%async_computation.21 | async-start | bytes 47579136 | tf_op jit(solution)/shard_map/reduce_scatter | solution.py:253
  2291.6 1842.3 %reduce-scatter.14.cloned.1.call-start = ((), (), s32[]{:S(2)}) async-start(), calls=%async_computation.22 | async-start | bytes 47579136 | tf_op jit(solution)/shard_map/reduce_scatter | solution.py:254
  (62 other events, 837.9 us)
Sparse Core Ops, SparseCore 0:
  10.9 158.7 all-gather.5
  172.5 75.6 all-gather.7
  251.0 187.4 all-gather.9
  441.2 142.0 all-gather.11
  585.9 142.7 all-gather.13
  1087.2 189.7 reduce-scatter.7
  2224.1 431.0 reduce-scatter.5
  2658.1 483.9 reduce-scatter.9
  3145.0 493.0 reduce-scatter.11
  3640.8 493.0 reduce-scatter.13
where the time goes:
time: 4160 us; the launch traced here: 4140 us
  waiting for transfers between devices  1920 us (46%)
  matrix products  1200 us (29%)
  other arithmetic  563 us (14%)
  local copies, waits for them, and re-layouts  328 us (8%)
  blocking collectives  86.9 us (2%)
    reduce_scatter x1, waiting for transfers between devices, per_device(): lax.psum_scatter(up_sum, ('fsdp', 'sp'), scatter_dimension=0, tiled=True)  496 us
    reduce_scatter x1, waiting for transfers between devices, per_device(): lax.psum_scatter(down_sum, ('fsdp', 'sp'), scatter_dimension=0, tiled=True)  496 us
    reduce_scatter x1, waiting for transfers between devices, per_device(): lax.psum_scatter(gate_sum, ('fsdp', 'sp'), scatter_dimension=0, tiled=True)  487 us
    reduce_scatter x1, waiting for transfers between devices, per_device(): lax.psum_scatter(joint_sum, ('fsdp', 'sp'), scatter_dimension=0, tiled=True)  243 us
    dot_general x16, matrix products, one_block(): jnp.einsum('sqhe,skhe->shqk', piece_rows, all_keys, preferred_element_typ...  237 us
    convert_element_type x8, other arithmetic, one_block(): scores_grad = (attn_probs * (probs_grad - inner_sum)).astype(jnp.bfloat16)  222 us
    dot_general x8, matrix products, one_block(): jnp.einsum('sqhe,skhe->shqk', piece_grad, values, preferred_element_type=...  196 us
    unnamed x10, other arithmetic  150 us
  transfers between devices with their start and end apart: 18, of which 8 were waited for; matrix products, arithmetic and copies ran while one was open for 47% of the time, Pallas kernels for 0%

commit v1 on v0

v1 whole, which is shorter than its diff:
```python
import functools
import math

import jax
import jax.numpy as jnp
import numpy as np
from jax import lax
from jax.experimental import pallas as pl
from jax.experimental.pallas import tpu as pltpu
from jax.sharding import PartitionSpec as P

D = 2048
HEADS = 32
HEAD = 64
ROT = 16

epsilon = 1e-05
masked_value = -1e30
f32 = jnp.float32
bf16 = jnp.bfloat16
LOG2E_SCALE = math.log2(math.e) * HEAD**-0.5
NN = (((1,), (0,)), ((), ()))
NT = (((1,), (1,)), ((), ()))
TN = (((0,), (0,)), ((), ()))


def dot(a, b, dims):
    return lax.dot_general(a, b, dims, preferred_element_type=f32)


def params(mib=56):
    return pltpu.CompilerParams(vmem_limit_bytes=mib * 2**20)


class Plane:
    def __init__(self, count):
        outer = count // 4
        self.count = count
        self.outer = outer

        def spot(o, i, c):
            return ((o % outer) * 2 + i) * 2 + c

        def split(s):
            return s // 4, (s // 2) % 2, s % 2

        self.core = [(s, s ^ 1) for s in range(count)]
        first = []
        later = [[] for _ in range(outer - 1)]
        for s in range(count):
            o, i, c = split(s)
            swapped = outer == 2 and c == 1
            first.append((s, spot(o + 1, i, c) if swapped else spot(o, 1 - i, c)))
            for k in range(1, outer):
                later[k - 1].append((s, spot(o, 1 - i, c) if swapped else spot(o + k, i, c)))
        self.first = first
        self.later = later
        here = list(range(count))

        def moved(table, perm):
            out = [None] * count
            for a, b in perm:
                out[b] = table[a]
            return out

        blocks = [here, moved(here, first)]
        for perm in later:
            blocks += [moved(blocks[0], perm), moved(blocks[1], perm)]
        blocks += [moved(b, self.core) for b in blocks]
        self.table = np.array(blocks, np.int32).T
        self.half = 2 * outer

    @staticmethod
    def send(value, perm):
        return lax.ppermute(value, "sp", perm)

    @staticmethod
    def back(value, perm):
        return lax.ppermute(value, "sp", [(b, a) for a, b in perm])

    def gather(self, value):
        partner = self.send(value, self.core)
        one = self.send(value, self.first)
        blocks = [value, one]
        for perm in self.later:
            blocks += [self.send(value, perm), self.send(one, perm)]
        return blocks, [partner] + [self.send(b, self.core) for b in blocks[1:]]

    def reduce(self, part_of):
        half = self.half
        sums = [None] * half
        total = None
        for start in reversed(range(0, half, 2)):
            theirs = self.send(part_of(half + start, half + start + 2).astype(bf16), self.core)
            mine = part_of(start, start + 2) + theirs.astype(f32)
            if start:
                got = self.back(mine.astype(bf16), self.later[start // 2 - 1])
                total = got.astype(f32) if total is None else total + got.astype(f32)
            else:
                total = mine if total is None else mine + total
        return total[0] + self.back(total[1].astype(bf16), self.first).astype(f32)


def norm_kernel(x_ref, gain_ref, shift_ref, *rest):
    out_ref = rest[-1]
    values = x_ref[...].astype(f32)
    center = values - jnp.mean(values, axis=-1, keepdims=True)
    spread = jnp.mean(center * center, axis=-1, keepdims=True)
    out_ref[...] = (center * lax.rsqrt(spread + epsilon) * gain_ref[...] + shift_ref[...]).astype(bf16)


def norm_block(x, gain, shift, at, blocks, buffer):
    rows = x.shape[0]
    tile = min(256, rows)
    steps = rows // tile
    operands = [x, gain, shift]
    specs = [
        pl.BlockSpec((tile, D), lambda i: (i, 0)),
        pl.BlockSpec((1, D), lambda i: (0, 0)),
        pl.BlockSpec((1, D), lambda i: (0, 0)),
    ]
    aliases = {}
    if buffer is not None:
        operands.append(buffer)
        specs.append(pl.BlockSpec(memory_space=pl.ANY))
        aliases = {3: 0}
    return pl.pallas_call(
        norm_kernel,
        grid=(steps,),
        in_specs=specs,
        out_specs=pl.BlockSpec((tile, D), lambda i: (at * steps + i, 0)),
        out_shape=jax.ShapeDtypeStruct((blocks * rows, D), bf16),
        input_output_aliases=aliases,
        compiler_params=params(32),
        cost_estimate=pl.CostEstimate(flops=rows * D * 12, bytes_accessed=rows * D * 4, transcendentals=rows),
        name="first_norm",
    )(*operands)


def turn(values, cosine, sine_up, sine_down):
    width = values.shape[1]
    half = ROT // 2
    return (
        values * cosine
        + pltpu.roll(values, width - half, 1) * sine_up
        + pltpu.roll(values, half, 1) * sine_down
    )


def joint_kernel(width, table_ref, x_ref, w_ref, bias_ref, cos_ref, up_ref, down_ref, q_ref, k_ref, v_ref):
    projected = dot(x_ref[...], w_ref[...], NN) + bias_ref[...]
    tables = (cos_ref[...], up_ref[...], down_ref[...])
    q_ref[...] = turn(projected[:, :width], *tables).astype(bf16)
    k_ref[...] = turn(projected[:, width : 2 * width], *tables).astype(bf16)
    v_ref[...] = projected[:, 2 * width :].astype(bf16)


def joint_projection(table, normed, weight, bias, tables, span):
    length = normed.shape[0]
    width = weight.shape[1] // 3
    placed = pl.BlockSpec((span, width), lambda b, t: (t[b], 0))
    return pl.pallas_call(
        functools.partial(joint_kernel, width),
        grid_spec=pltpu.PrefetchScalarGridSpec(
            num_scalar_prefetch=1,
            grid=(length // span,),
            in_specs=[
                pl.BlockSpec((span, D), lambda b, t: (b, 0)),
                pl.BlockSpec((D, 3 * width), lambda b, t: (0, 0)),
                pl.BlockSpec((1, 3 * width), lambda b, t: (0, 0)),
                placed,
                placed,
                placed,
            ],
            out_specs=[placed] * 3,
        ),
        out_shape=[jax.ShapeDtypeStruct((length, width), bf16)] * 3,
        compiler_params=params(),
        cost_estimate=pl.CostEstimate(
            flops=2 * length * D * 3 * width, bytes_accessed=length * (D + 3 * width) * 2, transcendentals=0
        ),
        name="joint_projection",
    )(table, normed, weight, bias, *tables)


def attend_kernel(heads, bq, bk, q_ref, k_ref, v_ref, o_ref, lse_ref, qm, vt, acc, m_s, l_s):
    i = pl.program_id(0)
    length, width = k_ref.shape
    lane = lax.broadcasted_iota(jnp.int32, (1, width), 1) // HEAD

    @pl.when(i == 0)
    def _():
        def flip(b, carry):
            rows = pl.ds(pl.multiple_of(b * bk, bk), bk)
            vt[:, rows] = jnp.transpose(v_ref[rows, :])
            return carry

        lax.fori_loop(0, length // bk, flip, 0)

    q = q_ref[...]
    for h in range(heads):
        qm[h] = jnp.where(lane == h, q, jnp.zeros_like(q))
    acc[...] = jnp.zeros_like(acc)
    m_s[...] = jnp.full_like(m_s, masked_value)
    l_s[...] = jnp.zeros_like(l_s)

    def body(j, masked):
        rows = pl.ds(pl.multiple_of(j * bk, bk), bk)
        k = k_ref[rows, :]
        scores = [dot(k, qm[h], NT) for h in range(heads)]
        if masked:
            key_at = lax.broadcasted_iota(jnp.int32, scores[0].shape, 0) + j * bk
            query_at = lax.broadcasted_iota(jnp.int32, scores[0].shape, 1) + i * bq
            scores = [jnp.where(key_at <= query_at, s, masked_value) for s in scores]
        m0 = m_s[...]
        l0 = l_s[...]
        m1 = jnp.maximum(m0, jnp.concatenate([jnp.max(s, axis=0, keepdims=True) for s in scores] + [m0[heads:]], 0))
        m_s[...] = m1
        kept = jnp.exp2((m0 - m1) * LOG2E_SCALE)
        base = m1 * LOG2E_SCALE
        raised = [jnp.exp2(scores[h] * LOG2E_SCALE - base[h : h + 1]) for h in range(heads)]
        l_s[...] = l0 * kept + jnp.concatenate([jnp.sum(p, axis=0, keepdims=True) for p in raised] + [l0[heads:]], 0)
        for h in range(heads):
            part = slice(h * HEAD, (h + 1) * HEAD)
            acc[part, :] = acc[part, :] * kept[h : h + 1] + dot(vt[part, rows], raised[h].astype(bf16), NN)

    whole = (i * bq) // bk
    lax.fori_loop(0, whole, lambda j, c: (body(j, False), c)[1], 0)
    for d in range(max(1, bq // bk)):
        body(whole + d, True)
    for h in range(heads):
        part = slice(h * HEAD, (h + 1) * HEAD)
        acc[part, :] = acc[part, :] * (1.0 / l_s[h : h + 1])
    o_ref[...] = jnp.transpose(acc[...].astype(bf16))
    lse_ref[...] = m_s[...] * LOG2E_SCALE + jnp.log2(l_s[...])


def attend(q, k, v):
    length, width = q.shape
    heads = width // HEAD
    bq = bk = min(512, length)
    full = pl.BlockSpec((length, width), lambda i: (0, 0))
    return pl.pallas_call(
        functools.partial(attend_kernel, heads, bq, bk),
        grid=(length // bq,),
        in_specs=[pl.BlockSpec((bq, width), lambda i: (i, 0)), full, full],
        out_specs=[pl.BlockSpec((bq, width), lambda i: (i, 0)), pl.BlockSpec((8, bq), lambda i: (0, i))],
        out_shape=[jax.ShapeDtypeStruct((length, width), bf16), jax.ShapeDtypeStruct((8, length), f32)],
        scratch_shapes=[
            pltpu.VMEM((heads, bq, width), bf16),
            pltpu.VMEM((width, length), bf16),
            pltpu.VMEM((width, bq), f32),
            pltpu.VMEM((8, bq), f32),
            pltpu.VMEM((8, bq), f32),
        ],
        compiler_params=params(),
        cost_estimate=pl.CostEstimate(
            flops=8 * length * length * width,
            bytes_accessed=length * width * 8,
            transcendentals=length * length * heads // 2,
        ),
        name="attend",
    )(q, k, v)


def attend_back_kernel(
    heads, bq, bk, place_ref, q_ref, k_ref, v_ref, do_ref, o_ref, lse_ref, cos_ref, up_ref, down_ref, out_ref,
    dq_acc, dk_acc, dv_acc, delta,
):
    j = pl.program_id(0)
    length, width = q_ref.shape
    lane = lax.broadcasted_iota(jnp.int32, (1, width), 1) // HEAD

    @pl.when(j == 0)
    def _():
        dq_acc[...] = jnp.zeros_like(dq_acc)
        pick = (
            lax.broadcasted_iota(jnp.int32, (8, width), 0) == lax.broadcasted_iota(jnp.int32, (8, width), 1) // HEAD
        ).astype(f32)

        def sums(b, carry):
            rows = pl.ds(pl.multiple_of(b * bq, bq), bq)
            both = do_ref[rows, :].astype(f32) * o_ref[rows, :].astype(f32)
            delta[:, rows] = lax.dot_general(
                pick, both, NT, precision=lax.Precision.HIGHEST, preferred_element_type=f32
            )
            return carry

        lax.fori_loop(0, length // bq, sums, 0)

    key_rows = pl.ds(pl.multiple_of(j * bk, bk), bk)
    k = k_ref[key_rows, :]
    v = v_ref[key_rows, :]
    kt = jnp.transpose(k)
    dk_acc[...] = jnp.zeros_like(dk_acc)
    dv_acc[...] = jnp.zeros_like(dv_acc)

    def body(i, masked):
        rows = pl.ds(pl.multiple_of(i * bq, bq), bq)
        q = q_ref[rows, :]
        do = do_ref[rows, :]
        probs, grads, queries, results = [], [], [], []
        for h in range(heads):
            qh = jnp.where(lane == h, q, jnp.zeros_like(q))
            doh = jnp.where(lane == h, do, jnp.zeros_like(do))
            s = dot(k, qh, NT)
            p = jnp.exp2(s * LOG2E_SCALE - lse_ref[h : h + 1, rows])
            if masked:
                key_at = lax.broadcasted_iota(jnp.int32, s.shape, 0) + j * bk
                query_at = lax.broadcasted_iota(jnp.int32, s.shape, 1) + i * bq
                p = jnp.where(key_at <= query_at, p, 0.0)
            dp = dot(v, doh, NT)
            ds = p * (dp - delta[h : h + 1, rows])
            probs.append(p.astype(bf16))
            grads.append(ds.astype(bf16))
            queries.append(qh)
            results.append(doh)
        dv_acc[...] += dot(jnp.concatenate(probs, 1), jnp.concatenate(results, 0), NN)
        dk_acc[...] += dot(jnp.concatenate(grads, 1), jnp.concatenate(queries, 0), NN)
        for h in range(heads):
            part = slice(h * HEAD, (h + 1) * HEAD)
            dq_acc[part, rows] += dot(kt[part], grads[h], NN)

    first = (j * bk) // bq
    near = max(1, bk // bq)
    for d in range(near):
        body(first + d, True)
    lax.fori_loop(first + near, length // bq, lambda i, c: (body(i, False), c)[1], 0)
    scale = HEAD**-0.5
    tables = (cos_ref[...], -up_ref[...], -down_ref[...])
    dq = (jnp.transpose(dq_acc[:, key_rows]) * scale).astype(bf16).astype(f32)
    dk = (dk_acc[...] * scale).astype(bf16).astype(f32)
    out_ref[:, :width] = turn(dq, *tables).astype(bf16)
    out_ref[:, width : 2 * width] = turn(dk, *tables).astype(bf16)
    out_ref[:, 2 * width :] = dv_acc[...].astype(bf16)


def attend_back(place, q, k, v, do, o, lse, tables, span):
    length, width = q.shape
    heads = width // HEAD
    bq = min(512, length)
    bk = span
    full = pl.BlockSpec((length, width), lambda i, t: (0, 0))
    block = pl.BlockSpec((bk, width), lambda i, t: (i, 0))
    return pl.pallas_call(
        functools.partial(attend_back_kernel, heads, bq, bk),
        grid_spec=pltpu.PrefetchScalarGridSpec(
            num_scalar_prefetch=1,
            grid=(length // bk,),
            in_specs=[full] * 5 + [pl.BlockSpec((8, length), lambda i, t: (0, 0))] + [block] * 3,
            out_specs=pl.BlockSpec((bk, 3 * width), lambda i, t: (t[i], 0)),
            scratch_shapes=[
                pltpu.VMEM((width, length), f32),
                pltpu.VMEM((bk, width), f32),
                pltpu.VMEM((bk, width), f32),
                pltpu.VMEM((8, length), f32),
            ],
        ),
        out_shape=jax.ShapeDtypeStruct((length, 3 * width), bf16),
        compiler_params=params(60),
        cost_estimate=pl.CostEstimate(
            flops=12 * length * length * width,
            bytes_accessed=length * width * 16,
            transcendentals=length * length * heads // 2,
        ),
        name="attend_back",
    )(place, q, k, v, do, o, lse, *tables)


def feed_kernel(ff, x0, x1, c0, c1, wgu_ref, wd_ref, *rest):
    hidden_ref, grad_ref, x_ref, c_ref = rest[-4:]
    which = pl.program_id(0)

    @pl.when(which == 0)
    def _():
        x_ref[...] = x0[...]
        c_ref[...] = c0[...]

    @pl.when(which == 1)
    def _():
        x_ref[...] = x1[...]
        c_ref[...] = c1[...]

    both = dot(x_ref[...], wgu_ref[...], NN)
    hidden_grad = dot(c_ref[...], wd_ref[...], NT)
    gate = both[:, :ff]
    up = both[:, ff:]
    open_ = jax.nn.sigmoid(gate)
    swished = gate * open_
    hidden_ref[...] = (swished * up).astype(bf16)
    grad_ref[:, :ff] = (hidden_grad * up * open_ * (1.0 + gate * (1.0 - open_))).astype(bf16)
    grad_ref[:, ff:] = (hidden_grad * swished).astype(bf16)


def feed_block(pair, cot_pair, gate_up, down, at, half, buffers):
    rows = pair[0].shape[0]
    ff = down.shape[0]
    tile = min(256, rows)
    steps = rows // tile
    length = 2 * half * rows
    early = pl.BlockSpec((tile, D), lambda p, i: (jnp.where(p == 0, i, steps - 1), 0))
    late = pl.BlockSpec((tile, D), lambda p, i: (jnp.where(p == 0, 0, i), 0))
    operands = [pair[0], pair[1], cot_pair[0], cot_pair[1], gate_up, down]
    specs = [
        early,
        late,
        early,
        late,
        pl.BlockSpec((D, 2 * ff), lambda p, i: (0, 0)),
        pl.BlockSpec((ff, D), lambda p, i: (0, 0)),
    ]
    aliases = {}
    if buffers is not None:
        aliases = {len(operands) + n: n for n in range(4)}
        operands += list(buffers)
        specs += [pl.BlockSpec(memory_space=pl.ANY)] * 4

    def place(p, i):
        return ((p * half + at) * steps + i, 0)

    return pl.pallas_call(
        functools.partial(feed_kernel, ff),
        grid=(2, steps),
        in_specs=specs,
        out_specs=[
            pl.BlockSpec((tile, ff), place),
            pl.BlockSpec((tile, 2 * ff), place),
            pl.BlockSpec((tile, D), place),
            pl.BlockSpec((tile, D), place),
        ],
        out_shape=[
            jax.ShapeDtypeStruct((length, ff), bf16),
            jax.ShapeDtypeStruct((length, 2 * ff), bf16),
            jax.ShapeDtypeStruct((length, D), bf16),
            jax.ShapeDtypeStruct((length, D), bf16),
        ],
        input_output_aliases=aliases,
        compiler_params=params(),
        cost_estimate=pl.CostEstimate(
            flops=12 * rows * D * ff, bytes_accessed=6 * D * ff + rows * D * 16, transcendentals=2 * rows * ff
        ),
        name="feed_forward",
    )(*operands)


def rotary_columns(length, width):
    half = ROT // 2
    indices = jnp.arange(half, dtype=f32)
    inverse = 1.0 / 10000.0 ** (indices * 2.0 / ROT)
    angles = jnp.arange(length, dtype=jnp.int32).astype(f32)[:, None] * inverse[None, :]
    cosine, sine = jnp.cos(angles), jnp.sin(angles)
    rest = jnp.zeros((length, HEAD - ROT), f32)
    none = jnp.zeros((length, half), f32)
    one_head = (
        jnp.concatenate([cosine, cosine, rest + 1.0], -1),
        jnp.concatenate([-sine, none, rest], -1),
        jnp.concatenate([none, sine, rest], -1),
    )
    return tuple(jnp.tile(t, (1, width // HEAD)) for t in one_head)


def norm_parts(values):
    center = values - jnp.mean(values, axis=-1, keepdims=True)
    spread = jnp.mean(center * center, axis=-1, keepdims=True)
    inverse = lax.rsqrt(spread + epsilon)
    return center * inverse, inverse


def norm_back(grad, xhat, inverse, gain):
    scaled = grad * gain
    middle = jnp.mean(scaled, axis=-1, keepdims=True)
    along = jnp.mean(scaled * xhat, axis=-1, keepdims=True)
    return (
        inverse * (scaled - middle - xhat * along),
        jnp.sum(grad * xhat, axis=0),
        jnp.sum(grad, axis=0),
    )


def swap_sp(value):
    return lax.all_to_all(value, "sp", split_axis=0, concat_axis=0, tiled=True)


def per_device(
    tokens, cotangent, first_gain, first_shift, joint_weight, joint_bias, out_weight, second_gain, second_shift,
    gate_weight, up_weight, down_weight,
):
    n_sp = lax.axis_size("sp")
    n_z = lax.axis_size("fsdp")
    n_all = n_sp * n_z
    plane = Plane(n_sp)
    half = plane.half
    me = lax.axis_index("sp")
    span = tokens.shape[1]
    length = n_sp * span
    width = D // n_sp
    depth = joint_weight.shape[0]
    ff_rows = down_weight.shape[0]
    unit = max(16, 128 // n_z)
    ff_pad = -(-ff_rows // unit) * unit
    ff = n_z * ff_pad

    order = jnp.asarray(plane.table)[me]
    place = jnp.asarray(np.argsort(plane.table, axis=1).astype(np.int32))[me]

    small = jnp.concatenate([first_gain, first_shift, second_gain, second_shift, joint_bias])
    small = jnp.broadcast_to(small[None], (n_all, small.shape[0]))
    small = lax.all_to_all(small, ("fsdp", "sp"), split_axis=0, concat_axis=0, tiled=True).astype(f32)
    n_gain = first_gain.shape[0]
    gain_one, shift_one, gain_two, shift_two = (
        small[:, i * n_gain : (i + 1) * n_gain].reshape(1, D) for i in range(4)
    )
    bias_all = small[:, 4 * n_gain :].reshape(3, n_sp, width)
    bias = lax.dynamic_index_in_dim(bias_all, me, axis=1, keepdims=False).reshape(1, 3 * width)

    x = tokens.reshape(span, D)
    blocks, partners = plane.gather(x)
    joint_cols = joint_weight.reshape(depth, 3, n_sp, width).transpose(2, 0, 1, 3).reshape(n_sp * depth, 3 * width)
    joint_mine = lax.all_gather(swap_sp(joint_cols), "fsdp", axis=0, tiled=True)

    def by_columns(weight):
        cut = weight.reshape(depth, n_z, n_sp, ff_rows)
        cut = jnp.pad(cut, ((0, 0), (0, 0), (0, 0), (0, ff_pad - ff_rows)))
        return cut.transpose(2, 0, 1, 3).reshape(n_sp * depth, ff)

    gate_up_cols = jnp.concatenate([by_columns(gate_weight), by_columns(up_weight)], axis=1)
    down_rows = jnp.pad(down_weight, ((0, ff_pad - ff_rows), (0, 0)))

    out_full = lax.all_gather(out_weight, ("fsdp", "sp"), axis=0, tiled=True)
    gate_up = lax.all_gather(swap_sp(gate_up_cols), "fsdp", axis=0, tiled=True)
    down = lax.all_gather(down_rows, "fsdp", axis=0, tiled=True)

    normed = None
    for t, block in enumerate(blocks + partners):
        normed = norm_block(block, gain_one, shift_one, t, n_sp, normed)
    tables = rotary_columns(length, width)
    q, k, v = joint_projection(order, normed, joint_mine, bias, tables, span)
    cot_blocks, cot_partners = plane.gather(cotangent.reshape(span, D))
    o, lse = attend(q, k, v)

    attended = swap_sp(o).reshape(n_sp, span, width)
    out_groups = out_full.reshape(n_sp, width, D)
    inputs = x.astype(f32)
    middle = inputs + jnp.einsum("jrc,jce->re", attended, out_groups, preferred_element_type=f32)
    xhat_two, inverse_two = norm_parts(middle)
    normed_two = (xhat_two * gain_two + shift_two).astype(bf16)

    two_blocks, two_partners = plane.gather(normed_two)
    feed = None
    for t in range(half):
        feed = feed_block(
            (two_blocks[t], two_partners[t]), (cot_blocks[t], cot_partners[t]), gate_up, down, t, half, feed
        )
    hidden, gate_up_grad, two_all, cot_all = feed

    def two_part(start, stop):
        rows = gate_up_grad[start * span : stop * span]
        return dot(rows, gate_up, NT).reshape(stop - start, span, D)

    two_grad = plane.reduce(two_part)

    def out_part(start, stop):
        rows = hidden[start * span : stop * span]
        return dot(rows, down, NN).reshape(stop - start, span, D)

    output = (middle + plane.reduce(out_part)).astype(bf16)

    down_sum = dot(hidden, cot_all, TN).astype(bf16)
    gate_up_sum = dot(two_all, gate_up_grad, TN).astype(bf16)
    down_grad = lax.psum_scatter(down_sum, "fsdp", scatter_dimension=0, tiled=True)[:ff_rows].astype(f32)
    gate_up_own = swap_sp(lax.psum_scatter(gate_up_sum, "fsdp", scatter_dimension=0, tiled=True))
    gate_up_own = gate_up_own.reshape(n_sp, depth, 2, n_z, ff_pad)[..., :ff_rows].transpose(2, 1, 3, 0, 4)
    gate_up_own = gate_up_own.reshape(2, depth, n_z * n_sp * ff_rows).astype(f32)

    two_input_grad, gain_two_sum, shift_two_sum = norm_back(two_grad, xhat_two, inverse_two, gain_two)
    middle_grad = cotangent.reshape(span, D).astype(f32) + two_input_grad
    branch_grad = middle_grad.astype(bf16)
    attended_grad = jnp.einsum("re,jce->jrc", branch_grad, out_groups, preferred_element_type=f32).astype(bf16)
    do = swap_sp(attended_grad.reshape(n_sp * span, width))
    out_sum = jnp.einsum("jrc,re->jce", attended, branch_grad, preferred_element_type=f32).reshape(D, D)
    out_grad = lax.psum_scatter(out_sum.astype(bf16), ("fsdp", "sp"), scatter_dimension=0, tiled=True).astype(f32)

    joint_grad_rows = attend_back(place, q, k, v, do, o, lse, tables, span)

    def normed_part(start, stop):
        rows = joint_grad_rows[start * span : stop * span]
        return dot(rows, joint_mine, NT).reshape(stop - start, span, D)

    normed_grad = plane.reduce(normed_part)
    joint_sum = dot(normed, joint_grad_rows, TN).astype(bf16)
    joint_own = swap_sp(lax.psum_scatter(joint_sum, "fsdp", scatter_dimension=0, tiled=True))
    joint_grad = joint_own.reshape(n_sp, depth, 3, width).transpose(1, 2, 0, 3).reshape(depth, 3 * D).astype(f32)
    bias_sum = jnp.sum(joint_grad_rows.astype(f32), axis=0).reshape(3, 1, width)
    bias_sum = lax.dynamic_update_slice(jnp.zeros((3, n_sp, width), f32), bias_sum, (0, me, 0))

    xhat_one, inverse_one = norm_parts(inputs)
    input_grad, gain_one_sum, shift_one_sum = norm_back(normed_grad, xhat_one, inverse_one, gain_one)
    tokens_grad = (middle_grad + input_grad).reshape(tokens.shape)

    sums = [gain_one_sum, shift_one_sum, gain_two_sum, shift_two_sum]
    sums = jnp.concatenate([s.reshape(n_all, n_gain) for s in sums] + [bias_sum.reshape(n_all, -1)], axis=1)
    sums = jnp.sum(lax.all_to_all(sums, ("fsdp", "sp"), split_axis=0, concat_axis=0, tiled=True), axis=0)
    gain_one_grad, shift_one_grad, gain_two_grad, shift_two_grad = (
        sums[i * n_gain : (i + 1) * n_gain] for i in range(4)
    )
    return (
        output.reshape(tokens.shape),
        tokens_grad,
        gain_one_grad,
        shift_one_grad,
        joint_grad,
        sums[4 * n_gain :],
        out_grad,
        gain_two_grad,
        shift_two_grad,
        gate_up_own[0],
        gate_up_own[1],
        down_grad,
    )


def solution(mesh):
    rows = P("fsdp", "sp", None)
    vector = P(("fsdp", "sp"))
    matrix = P(("fsdp", "sp"), None)
    return jax.shard_map(
        per_device,
        mesh=mesh,
        in_specs=(rows, rows, vector, vector, matrix, vector, matrix, vector, vector, matrix, matrix, matrix),
        out_specs=(rows, rows, vector, vector, matrix, vector, matrix, vector, vector, matrix, matrix, matrix),
        check_vma=False,
    )
```

time: 4160 us -> 1230 us (0.30)
  waiting for transfers between devices: 1920 us -> 407 us
  matrix products: 1200 us -> 196 us
  other arithmetic: 563 us -> 97.8 us
  Pallas kernels: 0 us -> 314 us
  local copies, waits for them, and re-layouts: 328 us -> 111 us
  blocking collectives: 86.9 us -> 17.8 us
    reduce_scatter x5 -> x4, waiting for transfers between devices: 1720 us -> 0.01 us  [the longest x1 0.01 us: per_device(): lax.psum_scatter(gate_up_sum, 'fsdp', scatter_dimension=0, tiled=True)]
    dot_general x71 -> x18, matrix products: 1200 us -> 196 us  [the longest x15 170 us: dot(): return lax.dot_general(a, b, dims, preferred_element_type=f32)]
    pallas_call x0 -> x15, Pallas kernels: none -> 314 us  [the longest x1 118 us: attend_back(): pl.pallas_call(functools.partial(attend_back_kernel, heads, bq, bk), grid...]
    ppermute x0 -> x33, waiting for transfers between devices: none -> 312 us  [the longest x27 180 us: send(): return lax.ppermute(value, 'sp', perm)]
    convert_element_type x20 -> x8, other arithmetic: 233 us -> 31.6 us  [the longest x3 22.6 us: reduce(): got = self.back(mine.astype(bf16), self.later[start // 2 - 1])]
    unnamed x10 -> x2, other arithmetic: 150 us -> 0.01 us
    reduce_sum x14 -> x7, other arithmetic: 128 us -> 14.4 us  [the longest x2 9.03 us: norm_back(): jnp.sum(grad * xhat, axis=0)]
    all_gather x5 -> x4, waiting for transfers between devices: 110 us -> 0.02 us  [the longest x1 0.02 us: per_device(): gate_up = lax.all_gather(swap_sp(gate_up_cols), 'fsdp', axis=0, tiled=True)]
  transfers between devices with their start and end apart: 18 -> 48, of which waited for: 8 -> 16; matrix products, arithmetic and copies ran while one was open for 47% -> 28% of each run, Pallas kernels for 0% -> 24%
where the time goes in v1:
time: 1230 us; the launch traced here: 1220 us
  waiting for transfers between devices  407 us (33%)
  Pallas kernels  314 us (26%)
  matrix products  196 us (16%)
  local copies, waits for them, and re-layouts  111 us (9%)
  other arithmetic  97.8 us (8%)
  starting transfers between devices  58 us (5%)
  blocking collectives  17.8 us (1%)
  between operations  15.2 us (1%)
    ppermute x27, waiting for transfers between devices, send(): return lax.ppermute(value, 'sp', perm)  180 us
    dot_general x15, matrix products, dot(): return lax.dot_general(a, b, dims, preferred_element_type=f32)  170 us
    ppermute x6, waiting for transfers between devices, back(): return lax.ppermute(value, 'sp', [(b, a) for a, b in perm])  133 us
    pallas_call x1, Pallas kernels, attend_back(): pl.pallas_call(functools.partial(attend_back_kernel, heads, bq, bk), grid...  118 us
    all_to_all x5, waiting for transfers between devices, swap_sp(): return lax.all_to_all(value, 'sp', split_axis=0, concat_axis=0, tiled=True)  92.7 us
    pallas_call x1, Pallas kernels, attend(): pl.pallas_call(functools.partial(attend_kernel, heads, bq, bk), grid=(len...  81.2 us
    pallas_call x4, Pallas kernels, feed_block(): pl.pallas_call(functools.partial(feed_kernel, ff), grid=(2, steps), in_sp...  72.3 us
    add x3, other arithmetic, reduce(): total = mine if total is None else mine + total  34.9 us
  transfers between devices with their start and end apart: 48, of which 16 were waited for; matrix products, arithmetic and copies ran while one was open for 28% of the time, Pallas kernels for 24%

profile of v1, /device:TPU:0, one launch (start us, length us, event | category | flops | bytes accessed | tf_op | source)
XLA Modules:
  0.0 1216.8 jit_solution(11042452779009239456)
XLA Ops:
  10.8 17.8 %all_to_all.71 = bf16[8,64,768]{2,1,0:T(8,128)(2,1)} all-to-all(bf16[8,64,768]{2,1,0:T(8,128)(2,1)} %all_to_all.48), channel_id=1, replica_groups=mesh['fsdp'=4,'sp'=8] {'sp'}, dimensions={0} | all-to-all | bytes 1572864 | tf_op jit(solution)/shard_map/all_to_all | solution.py:481
  30.7 46.0 %collective-permute-done.x_ref = bf16[512,2048]{1,0:T(8,128)(2,1)} collective-permute-done((bf16[512,2048]{1,0:T(8,128)(2,1)S(1)}, bf16[512,2048]{1,0:T(8,128)(2,1)}, u32[]{:S(2)}, u32[]{:S(2)}) %collective-permute-start) | collective-permute-done | bytes 2097184 | tf_op jit(solution)/shard_map/ppermute | solution.py:75
  88.3 15.1 %collective-permute-done.1.x_ref = bf16[512,2048]{1,0:T(8,128)(2,1)} collective-permute-done((bf16[512,2048]{1,0:T(8,128)(2,1)}, bf16[512,2048]{1,0:T(8,128)(2,1)}, u32[]{:S(2)}, u32[]{:S(2)}) %collective-permute-start.1) | collective-permute-done | bytes 2097184 | tf_op jit(solution)/shard_map/ppermute | solution.py:75
  191.5 21.6 %joint_projection.1 = (bf16[4096,256]{1,0:T(8,128)(2,1)}, bf16[4096,256]{1,0:T(8,128)(2,1)}, bf16[4096,256]{1,0:T(8,128)(2,1)}) custom-call(s32[8]{0:T(128)} %fusion.46.table_ref, bf16[4096,2048]{1,0:T(8,128)(2,1)} %copy-done.2, bf16[2048,768]{1,0:T(8,128)(2,1)} %all-gather.5.cloned.1.call-done.w_ref, f32[1,768]{1,0:T(1,128)} %bitcast.177, ...), custom_call_target="tpu_custom_call" | custom-call | flops 12884901888 | bytes 23068672 | tf_op jit(solution)/shard_map/joint_projection/pallas_call | solution.py:162
  213.2 81.2 %attend.1 = (bf16[4096,256]{1,0:T(8,128)(2,1)}, f32[8,4096]{1,0:T(8,128)}) custom-call(bf16[4096,256]{1,0:T(8,128)(2,1)} %get-tuple-element.33.q_ref, bf16[4096,256]{1,0:T(8,128)(2,1)} %get-tuple-element.34.k_ref, bf16[4096,256]{1,0:T(8,128)(2,1)} %get-tuple-element.35.v_ref), custom_call_target="tpu_custom_call" | custom-call | flops 34359738368 | bytes 8388608 | tf_op jit(solution)/shard_map/attend/pallas_call | solution.py:243
  302.4 23.5 %all-to-all-done.2 = bf16[8,512,256]{2,1,0:T(8,128)(2,1)} async-done(((bf16[8,512,256]{2,1,0:T(8,128)(2,1)}), bf16[8,512,256]{2,1,0:T(8,128)(2,1)}, u32[]{:S(2)}, u32[]{:S(2)}) %all-to-all-start.2) | async-done | bytes 2097184 | tf_op jit(solution)/shard_map/all_to_all | solution.py:481
  336.5 32.9 %collective-permute-done.10.c0 = bf16[512,2048]{1,0:T(8,128)(2,1)} collective-permute-done((bf16[512,2048]{1,0:T(8,128)(2,1)}, bf16[512,2048]{1,0:T(8,128)(2,1)}, u32[]{:S(2)}, u32[]{:S(2)}) %collective-permute-start.10) | collective-permute-done | bytes 2097184 | tf_op jit(solution)/shard_map/ppermute | solution.py:75
  372.0 38.8 %collective-permute-done.7.x0 = bf16[512,2048]{1,0:T(8,128)(2,1)} collective-permute-done((bf16[512,2048]{1,0:T(8,128)(2,1)S(1)}, bf16[512,2048]{1,0:T(8,128)(2,1)}, u32[]{:S(2)}, u32[]{:S(2)}) %collective-permute-start.7) | collective-permute-done | bytes 2097184 | tf_op jit(solution)/shard_map/ppermute | solution.py:75
  414.7 22.6 %collective-permute-done.13.x0 = bf16[512,2048]{1,0:T(8,128)(2,1)} collective-permute-done((bf16[512,2048]{1,0:T(8,128)(2,1)S(1)}, bf16[512,2048]{1,0:T(8,128)(2,1)}, u32[]{:S(2)}, u32[]{:S(2)}) %collective-permute-start.13) | collective-permute-done | bytes 2097184 | tf_op jit(solution)/shard_map/ppermute | solution.py:75
  437.9 21.9 %collective-permute-done.8.x0 = bf16[512,2048]{1,0:T(8,128)(2,1)} collective-permute-done((bf16[512,2048]{1,0:T(8,128)(2,1)}, bf16[512,2048]{1,0:T(8,128)(2,1)}, u32[]{:S(2)}, u32[]{:S(2)}) %collective-permute-start.8) | collective-permute-done | bytes 2097184 | tf_op jit(solution)/shard_map/ppermute | solution.py:75
  459.8 18.0 %feed_forward.4 = (bf16[4096,768]{1,0:T(8,128)(2,1)}, bf16[4096,1536]{1,0:T(8,128)(2,1)}, bf16[4096,2048]{1,0:T(8,128)(2,1)}, bf16[4096,2048]{1,0:T(8,128)(2,1)}) custom-call(bf16[512,2048]{1,0:T(8,128)(2,1)} %copy-done.15, bf16[512,2048]{1,0:T(8,128)(2,1)} %copy-done.33, bf16[512,2048]{1,0:T(8,128)(2,1)} %bitcast.170, ...), custom_call_target="tpu_custom_call" | custom-call | flops 9663676416 | bytes 26214400 | tf_op jit(solution)/shard_map/feed_forward/pallas_call | solution.py:421
  477.8 18.1 %feed_forward.5 = (bf16[4096,768]{1,0:T(8,128)(2,1)}, bf16[4096,1536]{1,0:T(8,128)(2,1)}, bf16[4096,2048]{1,0:T(8,128)(2,1)}, bf16[4096,2048]{1,0:T(8,128)(2,1)}) custom-call(bf16[512,2048]{1,0:T(8,128)(2,1)} %collective-permute-done.7.x0, ...), custom_call_target="tpu_custom_call", output_to_operand_aliasing={{0}: (6, {}), {1}: (7, {}), {2}: (8, {}), {3}: (9, {})} | custom-call | flops 9663676416 | bytes 26214400 | tf_op jit(solution)/shard_map/feed_forward/pallas_call | solution.py:421
  495.9 18.0 %feed_forward.6 = (bf16[4096,768]{1,0:T(8,128)(2,1)}, bf16[4096,1536]{1,0:T(8,128)(2,1)}, bf16[4096,2048]{1,0:T(8,128)(2,1)}, bf16[4096,2048]{1,0:T(8,128)(2,1)}) custom-call(bf16[512,2048]{1,0:T(8,128)(2,1)} %collective-permute-done.13.x0, ...), custom_call_target="tpu_custom_call", output_to_operand_aliasing={{0}: (6, {}), {1}: (7, {}), {2}: (8, {}), {3}: (9, {})} | custom-call | flops 9663676416 | bytes 26214400 | tf_op jit(solution)/shard_map/feed_forward/pallas_call | solution.py:421
  513.9 18.2 %feed_forward.7 = (bf16[4096,768]{1,0:T(8,128)(2,1)}, bf16[4096,1536]{1,0:T(8,128)(2,1)}, bf16[4096,2048]{1,0:T(8,128)(2,1)}, bf16[4096,2048]{1,0:T(8,128)(2,1)}) custom-call(bf16[512,2048]{1,0:T(8,128)(2,1)} %collective-permute-done.8.x0, ...), custom_call_target="tpu_custom_call", output_to_operand_aliasing={{0}: (6, {}), {1}: (7, {}), {2}: (8, {}), {3}: (9, {})} | custom-call | flops 9663676416 | bytes 26214400 | tf_op jit(solution)/shard_map/feed_forward/pallas_call | solution.py:421
  532.2 34.0 %convolution_convert_fusion.1 = bf16[2048,1536]{1,0:T(8,128)(2,1)} fusion(bf16[4096,2048]{1,0:T(8,128)(2,1)} %get-tuple-element.52, bf16[4096,1536]{1,0:T(8,128)(2,1)} %get-tuple-element.50), kind=kOutput, calls=%fused_computation.8 | convolution fusion | flops 25772949504 | bytes 35651584 | tf_op jit(solution)/shard_map/dot_general | solution.py:28
  667.3 11.7 convert_add_fusion.1
  683.0 51.7 %collective-permute-done.23 = bf16[2,512,2048]{2,1,0:T(8,128)(2,1)} collective-permute-done((bf16[2,512,2048]{2,1,0:T(8,128)(2,1)}, bf16[2,512,2048]{2,1,0:T(8,128)(2,1)}, u32[]{:S(2)}, u32[]{:S(2)}) %collective-permute-start.23) | collective-permute-done | bytes 4194336 | tf_op jit(solution)/shard_map/ppermute | solution.py:79
  756.5 18.5 %collective-permute-done.24 = bf16[512,2048]{1,0:T(8,128)(2,1)S(1)} collective-permute-done((bf16[512,2048]{1,0:T(8,128)(2,1)S(1)}, bf16[512,2048]{1,0:T(8,128)(2,1)S(1)}, u32[]{:S(2)}, u32[]{:S(2)}) %collective-permute-start.24) | collective-permute-done | bytes 2097184 | tf_op jit(solution)/shard_map/ppermute | solution.py:79
  795.2 20.1 %convolution_convert_fusion.8 = bf16[768,2048]{1,0:T(8,128)(2,1)} fusion(bf16[4096,768]{1,0:T(8,128)(2,1)} %get-tuple-element.49, bf16[4096,2048]{1,0:T(8,128)(2,1)} %get-tuple-element.53), kind=kOutput, calls=%fused_computation.50 | convolution fusion | flops 12886474752 | bytes 26214400 | tf_op jit(solution)/shard_map/dot_general | solution.py:28
  823.0 117.7 %attend_back.1 = bf16[4096,768]{1,0:T(8,128)(2,1)} custom-call(s32[8]{0:T(128)} %fusion.47.place_ref, bf16[4096,256]{1,0:T(8,128)(2,1)} %get-tuple-element.33.q_ref, bf16[4096,256]{1,0:T(8,128)(2,1)} %get-tuple-element.34.k_ref, bf16[4096,256]{1,0:T(8,128)(2,1)} %get-tuple-element.35.v_ref, bf16[4096,256]{1,0:T(8,128)(2,1)} %bitcast.165, ...), custom_call_target="tpu_custom_call" | custom-call | flops 51539607552 | bytes 16777216 | tf_op jit(solution)/shard_map/attend_back/pallas_call | solution.py:345
  940.7 20.3 %convolution_convert_fusion.9 = bf16[2048,768]{1,0:T(8,128)(2,1)} fusion(bf16[4096,2048]{1,0:T(8,128)(2,1)} %copy-done.2, bf16[4096,768]{1,0:T(8,128)(2,1)} %attend_back.1), kind=kOutput, calls=%fused_computation.51 | convolution fusion | flops 12886474752 | bytes 26214400 | tf_op jit(solution)/shard_map/dot_general | solution.py:28
  1015.3 53.0 %collective-permute-done.31 = bf16[2,512,2048]{2,1,0:T(8,128)(2,1)} collective-permute-done((bf16[2,512,2048]{2,1,0:T(8,128)(2,1)}, bf16[2,512,2048]{2,1,0:T(8,128)(2,1)}, u32[]{:S(2)}, u32[]{:S(2)}) %collective-permute-start.31) | collective-permute-done | bytes 4194336 | tf_op jit(solution)/shard_map/ppermute | solution.py:79
  1092.5 42.0 %all-to-all-done.7 = bf16[8,64,1536]{2,1,0:T(8,128)(2,1)} async-done(((bf16[8,64,1536]{2,1,0:T(8,128)(2,1)}), bf16[8,64,1536]{2,1,0:T(8,128)(2,1)}, u32[]{:S(2)}, u32[]{:S(2)}) %all-to-all-start.7) | async-done | bytes 1572896 | tf_op jit(solution)/shard_map/all_to_all | solution.py:481
  1162.3 20.9 %all-to-all-done.6 = bf16[8,64,768]{2,1,0:T(8,128)(2,1)S(1)} async-done(((bf16[8,64,768]{2,1,0:T(8,128)(2,1)}), bf16[8,64,768]{2,1,0:T(8,128)(2,1)S(1)}, u32[]{:S(2)}, u32[]{:S(2)}) %all-to-all-start.6) | async-done | bytes 786464 | tf_op jit(solution)/shard_map/all_to_all | solution.py:481
  (290 shorter events, 418.1 us)
Async XLA Ops:
  7.2 184.4 %all-gather.5.cloned.1.call-start = ((), (), s32[]{:S(2)}) async-start(), calls=%async_computation.12 | async-start | bytes 3932160 | tf_op jit(solution)/shard_map/all_gather | solution.py:519
  28.7 297.2 %all-gather.7.cloned.1.call-start = ((), (), s32[]{:S(2)}) async-start(), calls=%async_computation.13 | async-start | bytes 8650752 | tf_op jit(solution)/shard_map/all_gather | solution.py:529
  29.4 430.3 %all-gather.11.cloned.1.call-start = ((), (), s32[]{:S(2)}) async-start(), calls=%async_computation.15 | async-start | bytes 3932160 | tf_op jit(solution)/shard_map/all_gather | solution.py:531
  80.8 93.8 %collective-permute-start.6 = (bf16[512,2048]{1,0:T(8,128)(2,1)S(1)}, bf16[512,2048]{1,0:T(8,128)(2,1)}, u32[]{:S(2)}, u32[]{:S(2)}) collective-permute-start(bf16[512,2048]{1,0:T(8,128)(2,1)S(1)} %bitcast.143), channel_id=1, source_target_pairs={{0,1},{1,0},{2,3},{3,2},{4,5},{5,4},{6,7},{7,6},{8,9},{9,8},{10,11... | collective-permute-start | bytes 6291464 | tf_op jit(solution)/shard_map/ppermute | solution.py:75
  87.7 89.7 %collective-permute-start.5 = (bf16[512,2048]{1,0:T(8,128)(2,1)}, bf16[512,2048]{1,0:T(8,128)(2,1)}, u32[]{:S(2)}, u32[]{:S(2)}) collective-permute-start(bf16[512,2048]{1,0:T(8,128)(2,1)} %collective-permute-done.x_ref), channel_id=1, source_target_pairs={{0,1},{1,0},{2,3},{3,2},{4,5},{5,4},{6,7},{7,6},{8,9},{9,8},{10,11... | collective-permute-start | bytes 6291464 | tf_op jit(solution)/shard_map/ppermute | solution.py:75
  87.9 92.2 %collective-permute-start.4 = (bf16[512,2048]{1,0:T(8,128)(2,1)}, bf16[512,2048]{1,0:T(8,128)(2,1)}, u32[]{:S(2)}, u32[]{:S(2)}) collective-permute-start(bf16[512,2048]{1,0:T(8,128)(2,1)} %collective-permute-done.3.x_ref), channel_id=1, source_target_pairs={{0,1},{1,0},{2,3},{3,2},{4,5},{5,4},{6,7},{7,6},{8,9},{9,8},{10,11... | collective-permute-start | bytes 6291464 | tf_op jit(solution)/shard_map/ppermute | solution.py:75
  103.3 79.6 %collective-permute-start.2 = (bf16[512,2048]{1,0:T(8,128)(2,1)}, bf16[512,2048]{1,0:T(8,128)(2,1)}, u32[]{:S(2)}, u32[]{:S(2)}) collective-permute-start(bf16[512,2048]{1,0:T(8,128)(2,1)} %collective-permute-done.1.x_ref), channel_id=1, source_target_pairs={{0,1},{1,0},{2,3},{3,2},{4,5},{5,4},{6,7},{7,6},{8,9},{9,8},{10,11... | collective-permute-start | bytes 6291464 | tf_op jit(solution)/shard_map/ppermute | solution.py:75
  122.1 337.7 %all-gather.9.cloned.1.call-start = ((), (), s32[]{:S(2)}) async-start(), calls=%async_computation.14 | async-start | bytes 7864320 | tf_op jit(solution)/shard_map/all_gather | solution.py:530
  298.7 712.1 %reduce-scatter.9.cloned.1.call-start = ((), (), s32[]{:S(2)}) async-start(), calls=%async_computation.18 | async-start | bytes 7864320 | tf_op jit(solution)/shard_map/reduce_scatter | solution.py:571
  298.7 72.2 %collective-permute-start.20 = (bf16[512,2048]{1,0:T(8,128)(2,1)}, bf16[512,2048]{1,0:T(8,128)(2,1)}, u32[]{:S(2)}, u32[]{:S(2)}) collective-permute-start(bf16[512,2048]{1,0:T(8,128)(2,1)} %bitcast.167), channel_id=1, source_target_pairs={{0,1},{1,0},{2,3},{3,2},{4,5},{5,4},{6,7},{7,6},{8,9},{9,8},{10,11... | collective-permute-start | bytes 6291464 | tf_op jit(solution)/shard_map/ppermute | solution.py:75
  299.2 70.2 %collective-permute-start.10 = (bf16[512,2048]{1,0:T(8,128)(2,1)}, bf16[512,2048]{1,0:T(8,128)(2,1)}, u32[]{:S(2)}, u32[]{:S(2)}) collective-permute-start(bf16[512,2048]{1,0:T(8,128)(2,1)} %bitcast.168), channel_id=1, source_target_pairs={{0,2},{1,5},{2,0},{3,7},{4,6},{5,1},{6,4},{7,3},{8,10},{9,13},{10,... | collective-permute-start | bytes 6291464 | tf_op jit(solution)/shard_map/ppermute | solution.py:75
  300.7 71.3 %collective-permute-start.15 = (bf16[512,2048]{1,0:T(8,128)(2,1)}, bf16[512,2048]{1,0:T(8,128)(2,1)}, u32[]{:S(2)}, u32[]{:S(2)}) collective-permute-start(bf16[512,2048]{1,0:T(8,128)(2,1)} %bitcast.169), channel_id=1, source_target_pairs={{0,4},{1,3},{2,6},{3,1},{4,0},{5,7},{6,2},{7,5},{8,12},{9,11},{10,... | collective-permute-start | bytes 6291464 | tf_op jit(solution)/shard_map/ppermute | solution.py:75
  336.0 74.8 %collective-permute-start.7 = (bf16[512,2048]{1,0:T(8,128)(2,1)S(1)}, bf16[512,2048]{1,0:T(8,128)(2,1)}, u32[]{:S(2)}, u32[]{:S(2)}) collective-permute-start(bf16[512,2048]{1,0:T(8,128)(2,1)S(1)} %add_convert_fusion.3.x0), channel_id=1, source_target_pairs={{0,2},{1,5},{2,0},{3,7},{4,6},{5,1},{6,4},{7,3},{8,10},{9,13},{10,... | collective-permute-start | bytes 6291464 | tf_op jit(solution)/shard_map/ppermute | solution.py:75
  414.7 81.2 %collective-permute-start.16 = (bf16[512,2048]{1,0:T(8,128)(2,1)}, bf16[512,2048]{1,0:T(8,128)(2,1)}, u32[]{:S(2)}, u32[]{:S(2)}) collective-permute-start(bf16[512,2048]{1,0:T(8,128)(2,1)} %collective-permute-done.15.c0), channel_id=1, source_target_pairs={{0,1},{1,0},{2,3},{3,2},{4,5},{5,4},{6,7},{7,6},{8,9},{9,8},{10,11... | collective-permute-start | bytes 6291464 | tf_op jit(solution)/shard_map/ppermute | solution.py:75
  437.3 76.6 %collective-permute-start.12 = (bf16[512,2048]{1,0:T(8,128)(2,1)S(1)}, bf16[512,2048]{1,0:T(8,128)(2,1)}, u32[]{:S(2)}, u32[]{:S(2)}) collective-permute-start(bf16[512,2048]{1,0:T(8,128)(2,1)S(1)} %collective-permute-done.11.c0), channel_id=1, source_target_pairs={{0,1},{1,0},{2,3},{3,2},{4,5},{5,4},{6,7},{7,6},{8,9},{9,8},{10,11... | collective-permute-start | bytes 6291464 | tf_op jit(solution)/shard_map/ppermute | solution.py:75
  592.1 90.9 %collective-permute-start.21 = (bf16[2,512,2048]{2,1,0:T(8,128)(2,1)}, bf16[2,512,2048]{2,1,0:T(8,128)(2,1)}, u32[]{:S(2)}, u32[]{:S(2)}) collective-permute-start(bf16[2,512,2048]{2,1,0:T(8,128)(2,1)} %bitcast.16), channel_id=1, source_target_pairs={{0,1},{1,0},{2,3},{3,2},{4,5},{5,4},{6,7},{7,6},{8,9},{9,8},{10,11... | collective-permute-start | bytes 12582920 | tf_op jit(solution)/shard_map/ppermute | solution.py:75
  637.2 97.5 %collective-permute-start.23 = (bf16[2,512,2048]{2,1,0:T(8,128)(2,1)}, bf16[2,512,2048]{2,1,0:T(8,128)(2,1)}, u32[]{:S(2)}, u32[]{:S(2)}) collective-permute-start(bf16[2,512,2048]{2,1,0:T(8,128)(2,1)} %add_convert_fusion.2), channel_id=1, source_target_pairs={{4,0},{3,1},{6,2},{1,3},{0,4},{7,5},{2,6},{5,7},{12,8},{11,9},{14,... | collective-permute-start | bytes 12582920 | tf_op jit(solution)/shard_map/ppermute | solution.py:79
  681.5 70.1 %collective-permute-start.28 = (bf16[512,2048]{1,0:T(8,128)(2,1)S(1)}, bf16[512,2048]{1,0:T(8,128)(2,1)S(1)}, u32[]{:S(2)}, u32[]{:S(2)}) collective-permute-start(bf16[512,2048]{1,0:T(8,128)(2,1)S(1)} %fusion.25), channel_id=1, source_target_pairs={{2,0},{5,1},{0,2},{7,3},{6,4},{1,5},{4,6},{3,7},{10,8},{13,9},{8,1... | collective-permute-start | bytes 6291464 | tf_op jit(solution)/shard_map/ppermute | solution.py:79
  795.1 291.0 %reduce-scatter.11.cloned.1.call-start = ((), (), s32[]{:S(2)}) async-start(), calls=%async_computation.19 | async-start | bytes 3932160 | tf_op jit(solution)/shard_map/reduce_scatter | solution.py:570
  815.3 324.8 %reduce-scatter.5.cloned.1.call-start = ((), (), s32[]{:S(2)}) async-start(), calls=%async_computation.16 | async-start | bytes 3932160 | tf_op jit(solution)/shard_map/reduce_scatter | solution.py:591
  961.1 247.0 %reduce-scatter.7.cloned.1.call-start = ((), (), s32[]{:S(2)}) async-start(), calls=%async_computation.17 | async-start | bytes 8650752 | tf_op jit(solution)/shard_map/reduce_scatter | solution.py:581
  1000.2 68.1 %collective-permute-start.31 = (bf16[2,512,2048]{2,1,0:T(8,128)(2,1)}, bf16[2,512,2048]{2,1,0:T(8,128)(2,1)}, u32[]{:S(2)}, u32[]{:S(2)}) collective-permute-start(bf16[2,512,2048]{2,1,0:T(8,128)(2,1)} %add_convert_fusion), channel_id=1, source_target_pairs={{4,0},{3,1},{6,2},{1,3},{0,4},{7,5},{2,6},{5,7},{12,8},{11,9},{14,... | collective-permute-start | bytes 12582920 | tf_op jit(solution)/shard_map/ppermute | solution.py:79
  1010.8 123.7 %all-to-all-start.7 = ((bf16[8,64,1536]{2,1,0:T(8,128)(2,1)}), bf16[8,64,1536]{2,1,0:T(8,128)(2,1)}, u32[]{:S(2)}, u32[]{:S(2)}) async-start(bf16[8,64,1536]{2,1,0:T(8,128)(2,1)} %bitcast.171), calls=%async_computation.10 | async-start | bytes 3145728 | tf_op jit(solution)/shard_map/all_to_all | solution.py:481
  1083.9 105.3 %collective-permute-start.32 = (bf16[512,2048]{1,0:T(8,128)(2,1)}, bf16[512,2048]{1,0:T(8,128)(2,1)}, u32[]{:S(2)}, u32[]{:S(2)}) collective-permute-start(bf16[512,2048]{1,0:T(8,128)(2,1)} %fusion.26), channel_id=1, source_target_pairs={{2,0},{5,1},{0,2},{7,3},{6,4},{1,5},{4,6},{3,7},{10,8},{13,9},{8,1... | collective-permute-start | bytes 6291464 | tf_op jit(solution)/shard_map/ppermute | solution.py:79
  (63 other events, 1988.8 us)
Sparse Core Ops, SparseCore 0:
  28.8 63.4 all-gather.4
  95.1 80.2 all-gather.6
  177.6 61.0 all-gather.10
  240.2 113.9 all-gather.8
  566.3 111.9 reduce-scatter.8
  815.4 62.6 reduce-scatter.10
  961.2 60.9 reduce-scatter.4
  1024.5 159.0 reduce-scatter.6

commit v2 on v1

--- a/solution.py
+++ b/solution.py
@@ -78,27 +78,131 @@
     def back(value, perm):
         return lax.ppermute(value, "sp", [(b, a) for a, b in perm])
 
-    def gather(self, value):
-        partner = self.send(value, self.core)
-        one = self.send(value, self.first)
-        blocks = [value, one]
-        for perm in self.later:
-            blocks += [self.send(value, perm), self.send(one, perm)]
-        return blocks, [partner] + [self.send(b, self.core) for b in blocks[1:]]
-
-    def reduce(self, part_of):
-        half = self.half
-        sums = [None] * half
-        total = None
-        for start in reversed(range(0, half, 2)):
-            theirs = self.send(part_of(half + start, half + start + 2).astype(bf16), self.core)
-            mine = part_of(start, start + 2) + theirs.astype(f32)
-            if start:
-                got = self.back(mine.astype(bf16), self.later[start // 2 - 1])
-                total = got.astype(f32) if total is None else total + got.astype(f32)
-            else:
-                total = mine if total is None else mine + total
-        return total[0] + self.back(total[1].astype(bf16), self.first).astype(f32)
+    def gather_first(self, value):
+        return (
+            self.send(value, self.core),
+            self.send(value, self.first),
+            [self.send(value, perm) for perm in self.later],
+        )
+
+    def gather_second(self, one, twos):
+        return (
+            self.send(one, self.core),
+            [self.send(two, self.core) for two in twos],
+            [self.send(one, perm) for perm in self.later],
+        )
+
+    def gather_third(self, threes):
+        return [self.send(three, self.core) for three in threes]
+
+
+    def reduce_far(self, product, deps=()):
+        sent = []
+        for start in reversed(range(2, self.half, 2)):
+            theirs = self.send(product(self.half + start, self.half + start + 2, (), bf16, deps), self.core)
+            mine = product(start, start + 2, ((theirs, 0),), bf16)
+            sent.append(self.back(mine, self.later[start // 2 - 1]))
+        return sent
+
+    def reduce_near(self, product, deps=()):
+        return self.send(product(self.half, self.half + 2, (), bf16, deps), self.core)
+
+    def reduce_next(self, product, got, theirs, deps=()):
+        one = product(1, 2, tuple((t, 1) for t in [theirs] + got), bf16, deps)
+        return self.back(one, self.first)
+
+    def reduce_own(self, product, got, theirs, last, dtype=bf16):
+        return product(0, 1, tuple((t, 0) for t in [theirs] + got + [last]), dtype)[0]
+
+
+def launch(
+    kernel, operands, in_specs, outs, out_specs, *, grid, name, cost, scratch=(), deps=(), aliases=None, prefetch=0, mib=60
+):
+    deps = jax.tree.leaves(deps)
+    count = len(operands)
+
+    def body(*refs):
+        kernel(*refs[:count], *refs[count + len(deps) :])
+
+    flops, moved, transcendentals = cost
+    return pl.pallas_call(
+        body,
+        grid_spec=pltpu.PrefetchScalarGridSpec(
+            num_scalar_prefetch=prefetch,
+            grid=grid,
+            in_specs=list(in_specs) + [pl.BlockSpec(memory_space=pl.ANY)] * len(deps),
+            out_specs=list(out_specs),
+            scratch_shapes=list(scratch),
+        ),
+        out_shape=list(outs),
+        input_output_aliases=aliases or {},
+        compiler_params=pltpu.CompilerParams(vmem_limit_bytes=mib * 2**20),
+        cost_estimate=pl.CostEstimate(flops=int(flops), bytes_accessed=int(moved), transcendentals=int(transcendentals)),
+        name=name,
+    )(*operands, *deps)
+
+
+ANYWHERE = pl.BlockSpec(memory_space=pl.ANY)
+
+
+def held(value, deps):
+    return launch(
+        lambda *refs: None, [value], [ANYWHERE], [shape_of(value.shape, value.dtype)], [ANYWHERE],
+        grid=(1,), aliases={0: 0}, deps=deps, cost=(0, 0, 0), name="held",
+    )[0]
+
+
+def whole(shape):
+    return pl.BlockSpec(shape, lambda *_: (0,) * len(shape))
+
+
+def shape_of(shape, dtype):
+    return jax.ShapeDtypeStruct(shape, dtype)
+
+
+def product_kernel(terms, dims, *refs):
+    out_ref = refs[-1]
+    count, rows, width = out_ref.shape
+    total = dot(refs[0][...], refs[terms][...], dims)
+    for t in range(1, terms):
+        total += dot(refs[t][...], refs[terms + t][...], dims)
+    for ref in refs[2 * terms : -1]:
+        total += ref[...].astype(f32).reshape(count * rows, width)
+    out_ref[...] = total.astype(out_ref.dtype).reshape(count, rows, width)
+
+
+def product_of(lefts, right, dims, span):
+    tile = 512
+    depth = sum(left.shape[1] for left in lefts)
+
+    def right_at(at, left):
+        if dims is NT:
+            return pl.BlockSpec((tile, left.shape[1]), lambda i: (i, at))
+        return pl.BlockSpec((left.shape[1], tile), lambda i: (at, i))
+
+    def product(start, stop, addends, dtype, deps=()):
+        count = stop - start
+        assert start % count == 0 and all(at % count == 0 for _, at in addends)
+
+        def columns(at):
+            return pl.BlockSpec((count, span, tile), lambda i: (at // count, 0, i))
+
+        return launch(
+            functools.partial(product_kernel, len(lefts), dims),
+            [*lefts, *[right] * len(lefts), *(value for value, _ in addends)],
+            [pl.BlockSpec((count * span, a.shape[1]), lambda i: (start // count, 0)) for a in lefts]
+            + [right_at(t, left) for t, left in enumerate(lefts)]
+            + [columns(at) for _, at in addends],
+            [shape_of((count, span, D), dtype)],
+            [columns(0)],
+            grid=(D // tile,),
+            deps=deps,
+            mib=60,
+            cost=(2 * count * span * D * depth, 2 * depth * (D + count * span) + 4 * count * span * D, 0),
+            name="block_product",
+        )[0]
+
+    return product
 
 
 def norm_kernel(x_ref, gain_ref, shift_ref, *rest):
@@ -109,32 +213,197 @@
     out_ref[...] = (center * lax.rsqrt(spread + epsilon) * gain_ref[...] + shift_ref[...]).astype(bf16)
 
 
-def norm_block(x, gain, shift, at, blocks, buffer):
+def norm_block(x, gain, shift, at, blocks, buffer, deps=()):
     rows = x.shape[0]
     tile = min(256, rows)
     steps = rows // tile
-    operands = [x, gain, shift]
-    specs = [
-        pl.BlockSpec((tile, D), lambda i: (i, 0)),
-        pl.BlockSpec((1, D), lambda i: (0, 0)),
-        pl.BlockSpec((1, D), lambda i: (0, 0)),
-    ]
-    aliases = {}
-    if buffer is not None:
-        operands.append(buffer)
-        specs.append(pl.BlockSpec(memory_space=pl.ANY))
-        aliases = {3: 0}
-    return pl.pallas_call(
+    row = pl.BlockSpec((1, D), lambda i: (0, 0))
+    held = [] if buffer is None else [buffer]
+    return launch(
         norm_kernel,
+        [x, gain, shift, *held],
+        [pl.BlockSpec((tile, D), lambda i: (i, 0)), row, row, *[ANYWHERE] * len(held)],
+        [shape_of((blocks * rows, D), bf16)],
+        [pl.BlockSpec((tile, D), lambda i: (at * steps + i, 0))],
         grid=(steps,),
-        in_specs=specs,
-        out_specs=pl.BlockSpec((tile, D), lambda i: (at * steps + i, 0)),
-        out_shape=jax.ShapeDtypeStruct((blocks * rows, D), bf16),
-        input_output_aliases=aliases,
-        compiler_params=params(32),
-        cost_estimate=pl.CostEstimate(flops=rows * D * 12, bytes_accessed=rows * D * 4, transcendentals=rows),
+        aliases={3: 0} if held else {},
+        deps=deps,
+        mib=60,
+        cost=(rows * D * 12, rows * D * 4, rows),
         name="first_norm",
-    )(*operands)
+    )[0]
+
+
+def cut_joint_kernel(n_sp, groups, group, in_ref, out_ref):
+    for j in range(n_sp):
+        for g in range(groups):
+            for m in range(3):
+                to = (g * 3 + m) * group
+                start = m * D + (j * groups + g) * group
+                out_ref[j, :, to : to + group] = in_ref[:, start : start + group]
+
+
+def cut_joint(weight, n_sp, groups):
+    depth = weight.shape[0]
+    width = D // n_sp
+    return launch(
+        functools.partial(cut_joint_kernel, n_sp, groups, width // groups),
+        [weight], [whole(weight.shape)], [shape_of((n_sp, depth, 3 * width), bf16)], [whole((n_sp, depth, 3 * width))],
+        grid=(1,), cost=(0, weight.size * 4, 0), name="cut_joint",
+    )[0]
+
+
+def join_joint_kernel(n_sp, groups, group, *refs):
+    out_ref = refs[-1]
+    for j in range(n_sp):
+        for g in range(groups):
+            for m in range(3):
+                start = m * D + (j * groups + g) * group
+                out_ref[:, start : start + group] = refs[g][j, :, m * group : (m + 1) * group].astype(f32)
+
+
+def join_joint(parts, n_sp):
+    groups = len(parts)
+    depth = parts[0].shape[1]
+    return launch(
+        functools.partial(join_joint_kernel, n_sp, groups, parts[0].shape[2] // 3),
+        parts, [whole(p.shape) for p in parts], [shape_of((depth, 3 * D), f32)], [whole((depth, 3 * D))],
+        grid=(1,), cost=(0, depth * D * 18, 0), name="join_joint",
+    )[0]
+
+
+def cut_feed_kernel(n_sp, n_z, size, padded, gate_ref, up_ref, out_ref):
+    out_ref[...] = jnp.zeros_like(out_ref)
+    for j in range(n_sp):
+        for p, ref in enumerate((gate_ref, up_ref)):
+            for z in range(n_z):
+                start = (z * n_sp + j) * size
+                to = (p * n_z + z) * padded
+                out_ref[j, :, to : to + size] = ref[:, start : start + size]
+
+
+def cut_feed(gate_weight, up_weight, n_sp, n_z, padded, deps):
+    depth, total = gate_weight.shape
+    size = total // (n_sp * n_z)
+    shape = (n_sp, depth, 2 * n_z * padded)
+    return launch(
+        functools.partial(cut_feed_kernel, n_sp, n_z, size, padded),
+        [gate_weight, up_weight], [whole(gate_weight.shape)] * 2, [shape_of(shape, bf16)], [whole(shape)],
+        grid=(1,), cost=(0, gate_weight.size * 8, 0), name="cut_feed", deps=deps,
+    )[0]
+
+
+def join_feed_kernel(n_sp, n_z, size, padded, in_ref, gate_ref, up_ref):
+    for p, ref in enumerate((gate_ref, up_ref)):
+        for z in range(n_z):
+            for j in range(n_sp):
+                start = (z * n_sp + j) * size
+                to = (p * n_z + z) * padded
+                ref[:, start : start + size] = in_ref[j, :, to : to + size].astype(f32)
+
+
+def join_feed(value, n_z, size, padded):
+    n_sp, depth, _ = value.shape
+    shape = (depth, n_sp * n_z * size)
+    return launch(
+        functools.partial(join_feed_kernel, n_sp, n_z, size, padded),
+        [value], [whole(value.shape)], [shape_of(shape, f32)] * 2, [whole(shape)] * 2,
+        grid=(1,), cost=(0, value.size * 6, 0), name="join_feed",
+    )
+
+
+def norm_back_kernel(steps, n_parts, *refs):
+    grad_ref, x_ref, gain_ref, beside_ref = refs[:4]
+    weights = refs[4 : 4 + n_parts]
+    outs = refs[4 + n_parts :]
+    result_ref, sums_ref = outs[0], outs[1]
+    values = x_ref[...].astype(f32)
+    center = values - jnp.mean(values, axis=-1, keepdims=True)
+    spread = jnp.mean(center * center, axis=-1, keepdims=True)
+    inverse = lax.rsqrt(spread + epsilon)
+    xhat = center * inverse
+    grad = grad_ref[...].astype(f32)
+    scaled = grad * gain_ref[...]
+    level = jnp.mean(scaled, axis=-1, keepdims=True)
+    along = jnp.mean(scaled * xhat, axis=-1, keepdims=True)
+    result = beside_ref[...].astype(f32) + inverse * (scaled - level - xhat * along)
+    result_ref[...] = result
+
+    @pl.when(pl.program_id(0) == 0)
+    def _():
+        sums_ref[...] = jnp.zeros_like(sums_ref)
+
+    sums_ref[0:1] += jnp.sum(grad * xhat, axis=0, keepdims=True)
+    sums_ref[1:2] += jnp.sum(grad, axis=0, keepdims=True)
+    if n_parts:
+        branch = result.astype(bf16)
+        outs[2][...] = branch
+        parts = outs[3:]
+        group = parts[0].shape[2]
+        full = dot(branch, weights[0][...], NT).astype(bf16)
+        for j in range(parts[0].shape[0]):
+            for g, part in enumerate(parts):
+                start = (j * len(parts) + g) * group
+                part[j] = full[:, start : start + group]
+
+
+def norm_back(grad, x, gain, beside, weight=None, n_sp=0, groups=0):
+    rows = x.shape[0]
+    tile = min(128, rows)
+    row = pl.BlockSpec((1, D), lambda i: (0, 0))
+    block = pl.BlockSpec((tile, D), lambda i: (i, 0))
+    outs = [shape_of((rows, D), f32), shape_of((8, D), f32)]
+    out_specs = [block, whole((8, D))]
+    extra, specs = [], []
+    if weight is not None:
+        group = D // n_sp // groups
+        extra, specs = [weight], [whole((D, D))]
+        outs += [shape_of((rows, D), bf16)] + [shape_of((n_sp, rows, group), bf16)] * groups
+        out_specs += [block] + [pl.BlockSpec((n_sp, tile, group), lambda i: (0, i, 0))] * groups
+    return launch(
+        functools.partial(norm_back_kernel, rows // tile, len(extra)),
+        [grad, x, gain, beside, *extra],
+        [block, block, row, block, *specs],
+        outs,
+        out_specs,
+        grid=(rows // tile,),
+        cost=(rows * D * (20 + 2 * D * len(extra)), rows * D * 16 + 2 * D * D * len(extra), rows),
+        name="norm_back",
+    )
+
+
+def middle_kernel(groups, n_sp, *refs):
+    parts, (out_w, x_ref, gain_ref, shift_ref) = refs[:groups], refs[groups : groups + 4]
+    middle_ref, normed_ref, attended_ref = refs[groups + 4 :]
+    group = parts[0].shape[2]
+    for j in range(n_sp):
+        for g in range(groups):
+            start = (j * groups + g) * group
+            attended_ref[:, start : start + group] = parts[g][j]
+    values = x_ref[...].astype(f32) + dot(attended_ref[...], out_w[...], NN)
+    middle_ref[...] = values
+    center = values - jnp.mean(values, axis=-1, keepdims=True)
+    spread = jnp.mean(center * center, axis=-1, keepdims=True)
+    normed_ref[...] = (center * lax.rsqrt(spread + epsilon) * gain_ref[...] + shift_ref[...]).astype(bf16)
+
+
+def middle_of(parts, out_w, x, gain, shift, deps=()):
+    n_sp, rows, group = parts[0].shape
+    tile = min(128, rows)
+    row = pl.BlockSpec((1, D), lambda i: (0, 0))
+    block = pl.BlockSpec((tile, D), lambda i: (i, 0))
+    return launch(
+        functools.partial(middle_kernel, len(parts), n_sp),
+        [*parts, out_w, x, gain, shift],
+        [pl.BlockSpec((n_sp, tile, group), lambda i: (0, i, 0))] * len(parts)
+        + [pl.BlockSpec((D, D), lambda i: (0, 0)), block, row, row],
+        [shape_of((rows, D), f32), shape_of((rows, D), bf16), shape_of((rows, D), bf16)],
+        [block] * 3,
+        grid=(rows // tile,),
+        deps=deps,
+        cost=(2 * rows * D * D, 2 * D * D + rows * D * 12, rows),
+        name="middle",
+    )
 
 
 def turn(values, cosine, sine_up, sine_down):
@@ -147,17 +416,20 @@
     )
 
 
-def joint_kernel(width, table_ref, x_ref, w_ref, bias_ref, cos_ref, up_ref, down_ref, q_ref, k_ref, v_ref):
+def joint_kernel(width, table_ref, x_ref, w_ref, bias_ref, cos_ref, up_ref, down_ref, *outs):
     projected = dot(x_ref[...], w_ref[...], NN) + bias_ref[...]
     tables = (cos_ref[...], up_ref[...], down_ref[...])
-    q_ref[...] = turn(projected[:, :width], *tables).astype(bf16)
-    k_ref[...] = turn(projected[:, width : 2 * width], *tables).astype(bf16)
-    v_ref[...] = projected[:, 2 * width :].astype(bf16)
-
-
-def joint_projection(table, normed, weight, bias, tables, span):
+    for g in range(len(outs) // 3):
+        part = projected[:, 3 * g * width : 3 * (g + 1) * width]
+        outs[3 * g][...] = turn(part[:, :width], *tables).astype(bf16)
+        outs[3 * g + 1][...] = turn(part[:, width : 2 * width], *tables).astype(bf16)
+        outs[3 * g + 2][...] = part[:, 2 * width :].astype(bf16)
+
+
+def joint_projection(table, normed, weight, bias, tables, span, groups):
     length = normed.shape[0]
-    width = weight.shape[1] // 3
+    total = weight.shape[1]
+    width = total // 3 // groups
     placed = pl.BlockSpec((span, width), lambda b, t: (t[b], 0))
     return pl.pallas_call(
         functools.partial(joint_kernel, width),
@@ -166,24 +438,25 @@
             grid=(length // span,),
             in_specs=[
                 pl.BlockSpec((span, D), lambda b, t: (b, 0)),
-                pl.BlockSpec((D, 3 * width), lambda b, t: (0, 0)),
-                pl.BlockSpec((1, 3 * width), lambda b, t: (0, 0)),
+                pl.BlockSpec((D, total), lambda b, t: (0, 0)),
+                pl.BlockSpec((1, total), lambda b, t: (0, 0)),
                 placed,
                 placed,
                 placed,
             ],
-            out_specs=[placed] * 3,
+            out_specs=[placed] * (3 * groups),
         ),
-        out_shape=[jax.ShapeDtypeStruct((length, width), bf16)] * 3,
+        out_shape=[jax.ShapeDtypeStruct((length, width), bf16)] * (3 * groups),
         compiler_params=params(),
         cost_estimate=pl.CostEstimate(
-            flops=2 * length * D * 3 * width, bytes_accessed=length * (D + 3 * width) * 2, transcendentals=0
+            flops=2 * length * D * total, bytes_accessed=length * (D + total) * 2, transcendentals=0
         ),
         name="joint_projection",
     )(table, normed, weight, bias, *tables)
 
 
-def attend_kernel(heads, bq, bk, q_ref, k_ref, v_ref, o_ref, lse_ref, qm, vt, acc, m_s, l_s):
+def attend_kernel(heads, bq, bk, q_ref, k_ref, v_ref, *rest):
+    o_ref, lse_ref, qm, vt, acc, m_s, l_s = rest[-7:]
     i = pl.program_id(0)
     length, width = k_ref.shape
     lane = lax.broadcasted_iota(jnp.int32, (1, width), 1) // HEAD
@@ -235,7 +508,8 @@
     lse_ref[...] = m_s[...] * LOG2E_SCALE + jnp.log2(l_s[...])
 
 
-def attend(q, k, v):
+def attend(q, k, v, deps=()):
+    deps = jax.tree.leaves(deps)
     length, width = q.shape
     heads = width // HEAD
     bq = bk = min(512, length)
@@ -243,7 +517,8 @@
     return pl.pallas_call(
         functools.partial(attend_kernel, heads, bq, bk),
         grid=(length // bq,),
-        in_specs=[pl.BlockSpec((bq, width), lambda i: (i, 0)), full, full],
+        in_specs=[pl.BlockSpec((bq, width), lambda i: (i, 0)), full, full]
+        + [pl.BlockSpec(memory_space=pl.ANY)] * len(deps),
         out_specs=[pl.BlockSpec((bq, width), lambda i: (i, 0)), pl.BlockSpec((8, bq), lambda i: (0, i))],
         out_shape=[jax.ShapeDtypeStruct((length, width), bf16), jax.ShapeDtypeStruct((8, length), f32)],
         scratch_shapes=[
@@ -260,13 +535,13 @@
             transcendentals=length * length * heads // 2,
         ),
         name="attend",
-    )(q, k, v)
+    )(q, k, v, *deps)
 
 
 def attend_back_kernel(
-    heads, bq, bk, place_ref, q_ref, k_ref, v_ref, do_ref, o_ref, lse_ref, cos_ref, up_ref, down_ref, out_ref,
-    dq_acc, dk_acc, dv_acc, delta,
+    heads, bq, bk, place_ref, q_ref, k_ref, v_ref, do_ref, o_ref, lse_ref, cos_ref, up_ref, down_ref, *rest
 ):
+    out_ref, dq_acc, dk_acc, dv_acc, delta = rest[-5:]
     j = pl.program_id(0)
     length, width = q_ref.shape
     lane = lax.broadcasted_iota(jnp.int32, (1, width), 1) // HEAD
@@ -335,7 +610,8 @@
     out_ref[:, 2 * width :] = dv_acc[...].astype(bf16)
 
 
-def attend_back(place, q, k, v, do, o, lse, tables, span):
+def attend_back(place, q, k, v, do, o, lse, tables, span, deps=()):
+    deps = jax.tree.leaves(deps)
     length, width = q.shape
     heads = width // HEAD
     bq = min(512, length)
@@ -347,7 +623,8 @@
         grid_spec=pltpu.PrefetchScalarGridSpec(
             num_scalar_prefetch=1,
             grid=(length // bk,),
-            in_specs=[full] * 5 + [pl.BlockSpec((8, length), lambda i, t: (0, 0))] + [block] * 3,
+            in_specs=[full] * 5 + [pl.BlockSpec((8, length), lambda i, t: (0, 0))] + [block] * 3
+            + [pl.BlockSpec(memory_space=pl.ANY)] * len(deps),
             out_specs=pl.BlockSpec((bk, 3 * width), lambda i, t: (t[i], 0)),
             scratch_shapes=[
                 pltpu.VMEM((width, length), f32),
@@ -364,7 +641,7 @@
             transcendentals=length * length * heads // 2,
         ),
         name="attend_back",
-    )(place, q, k, v, do, o, lse, *tables)
+    )(place, q, k, v, do, o, lse, *tables, *deps)
 
 
 def feed_kernel(ff, x0, x1, c0, c1, wgu_ref, wd_ref, *rest):
@@ -392,7 +669,7 @@
     grad_ref[:, ff:] = (hidden_grad * swished).astype(bf16)
 
 
-def feed_block(pair, cot_pair, gate_up, down, at, half, buffers):
+def feed_block(pair, cot_pair, gate_up, down, at, half, buffers, deps=()):
     rows = pair[0].shape[0]
     ff = down.shape[0]
     tile = min(256, rows)
@@ -418,63 +695,44 @@
     def place(p, i):
         return ((p * half + at) * steps + i, 0)
 
-    return pl.pallas_call(
+    return launch(
         functools.partial(feed_kernel, ff),
-        grid=(2, steps),
-        in_specs=specs,
-        out_specs=[
+        operands,
+        specs,
+        [
+            shape_of((length, ff), bf16),
+            shape_of((length, 2 * ff), bf16),
+            shape_of((length, D), bf16),
+            shape_of((length, D), bf16),
+        ],
+        [
             pl.BlockSpec((tile, ff), place),
             pl.BlockSpec((tile, 2 * ff), place),
             pl.BlockSpec((tile, D), place),
             pl.BlockSpec((tile, D), place),
         ],
-        out_shape=[
-            jax.ShapeDtypeStruct((length, ff), bf16),
-            jax.ShapeDtypeStruct((length, 2 * ff), bf16),
-            jax.ShapeDtypeStruct((length, D), bf16),
-            jax.ShapeDtypeStruct((length, D), bf16),
-        ],
-        input_output_aliases=aliases,
-        compiler_params=params(),
-        cost_estimate=pl.CostEstimate(
-            flops=12 * rows * D * ff, bytes_accessed=6 * D * ff + rows * D * 16, transcendentals=2 * rows * ff
-        ),
+        grid=(2, steps),
+        aliases=aliases,
+        deps=deps,
+        cost=(12 * rows * D * ff, 6 * D * ff + rows * D * 16, 2 * rows * ff),
         name="feed_forward",
-    )(*operands)
+    )
 
 
 def rotary_columns(length, width):
     half = ROT // 2
-    indices = jnp.arange(half, dtype=f32)
-    inverse = 1.0 / 10000.0 ** (indices * 2.0 / ROT)
-    angles = jnp.arange(length, dtype=jnp.int32).astype(f32)[:, None] * inverse[None, :]
-    cosine, sine = jnp.cos(angles), jnp.sin(angles)
-    rest = jnp.zeros((length, HEAD - ROT), f32)
-    none = jnp.zeros((length, half), f32)
+    indices = np.arange(half, dtype=np.float32)
+    inverse = np.float32(1.0) / np.float32(10000.0) ** (indices * np.float32(2.0 / ROT))
+    angles = np.arange(length, dtype=np.float32)[:, None] * inverse[None, :].astype(np.float32)
+    cosine, sine = np.cos(angles.astype(np.float64)), np.sin(angles.astype(np.float64))
+    rest = np.zeros((length, HEAD - ROT))
+    none = np.zeros((length, half))
     one_head = (
-        jnp.concatenate([cosine, cosine, rest + 1.0], -1),
-        jnp.concatenate([-sine, none, rest], -1),
-        jnp.concatenate([none, sine, rest], -1),
-    )
-    return tuple(jnp.tile(t, (1, width // HEAD)) for t in one_head)
-
-
-def norm_parts(values):
-    center = values - jnp.mean(values, axis=-1, keepdims=True)
-    spread = jnp.mean(center * center, axis=-1, keepdims=True)
-    inverse = lax.rsqrt(spread + epsilon)
-    return center * inverse, inverse
-
-
-def norm_back(grad, xhat, inverse, gain):
-    scaled = grad * gain
-    middle = jnp.mean(scaled, axis=-1, keepdims=True)
-    along = jnp.mean(scaled * xhat, axis=-1, keepdims=True)
-    return (
-        inverse * (scaled - middle - xhat * along),
-        jnp.sum(grad * xhat, axis=0),
-        jnp.sum(grad, axis=0),
-    )
+        np.concatenate([cosine, cosine, rest + 1.0], -1),
+        np.concatenate([-sine, none, rest], -1),
+        np.concatenate([none, sine, rest], -1),
+    )
+    return tuple(jnp.asarray(np.tile(t, (1, width // HEAD)).astype(np.float32)) for t in one_head)
 
 
 def swap_sp(value):
@@ -502,102 +760,167 @@
 
     order = jnp.asarray(plane.table)[me]
     place = jnp.asarray(np.argsort(plane.table, axis=1).astype(np.int32))[me]
+    groups = 2 if width % 256 == 0 else 1
+    group = width // groups
+    my_z = lax.axis_index("fsdp")
 
     small = jnp.concatenate([first_gain, first_shift, second_gain, second_shift, joint_bias])
     small = jnp.broadcast_to(small[None], (n_all, small.shape[0]))
-    small = lax.all_to_all(small, ("fsdp", "sp"), split_axis=0, concat_axis=0, tiled=True).astype(f32)
+    small_all = lax.all_to_all(small, ("fsdp", "sp"), split_axis=0, concat_axis=0, tiled=True)
+    small = small_all.astype(f32)
     n_gain = first_gain.shape[0]
     gain_one, shift_one, gain_two, shift_two = (
         small[:, i * n_gain : (i + 1) * n_gain].reshape(1, D) for i in range(4)
     )
     bias_all = small[:, 4 * n_gain :].reshape(3, n_sp, width)
-    bias = lax.dynamic_index_in_dim(bias_all, me, axis=1, keepdims=False).reshape(1, 3 * width)
+    bias = lax.dynamic_index_in_dim(bias_all, me, axis=1, keepdims=False)
+    bias = bias.reshape(3, groups, group).transpose(1, 0, 2).reshape(1, 3 * width)
+
+    joint_blocks = [swap_sp(cut_joint(joint_weight, n_sp, groups)).reshape(n_sp * depth, 3 * width)]
+    for _ in range(n_z - 1):
+        joint_blocks.append(lax.ppermute(joint_blocks[-1], "fsdp", [(i, (i + 1) % n_z) for i in range(n_z)]))
+    joint_mine = jnp.zeros((D, 3 * width), bf16)
+    for step, block in enumerate(joint_blocks):
+        at = lax.rem(my_z - step + n_z, n_z) * (n_sp * depth)
+        joint_mine = lax.dynamic_update_slice(joint_mine, block, (at, 0))
+
+    gate_up_cols = cut_feed(gate_weight, up_weight, n_sp, n_z, ff_pad, ())
+    down_rows = jnp.pad(down_weight, ((0, ff_pad - ff_rows), (0, 0)))
+    down = lax.all_gather(down_rows, "fsdp", axis=0, tiled=True)
 
     x = tokens.reshape(span, D)
-    blocks, partners = plane.gather(x)
-    joint_cols = joint_weight.reshape(depth, 3, n_sp, width).transpose(2, 0, 1, 3).reshape(n_sp * depth, 3 * width)
-    joint_mine = lax.all_gather(swap_sp(joint_cols), "fsdp", axis=0, tiled=True)
-
-    def by_columns(weight):
-        cut = weight.reshape(depth, n_z, n_sp, ff_rows)
-        cut = jnp.pad(cut, ((0, 0), (0, 0), (0, 0), (0, ff_pad - ff_rows)))
-        return cut.transpose(2, 0, 1, 3).reshape(n_sp * depth, ff)
-
-    gate_up_cols = jnp.concatenate([by_columns(gate_weight), by_columns(up_weight)], axis=1)
-    down_rows = jnp.pad(down_weight, ((0, ff_pad - ff_rows), (0, 0)))
-
-    out_full = lax.all_gather(out_weight, ("fsdp", "sp"), axis=0, tiled=True)
-    gate_up = lax.all_gather(swap_sp(gate_up_cols), "fsdp", axis=0, tiled=True)
-    down = lax.all_gather(down_rows, "fsdp", axis=0, tiled=True)
-
     normed = None
-    for t, block in enumerate(blocks + partners):
-        normed = norm_block(block, gain_one, shift_one, t, n_sp, normed)
-    tables = rotary_columns(length, width)
-    q, k, v = joint_projection(order, normed, joint_mine, bias, tables, span)
-    cot_blocks, cot_partners = plane.gather(cotangent.reshape(span, D))
-    o, lse = attend(q, k, v)
-
-    attended = swap_sp(o).reshape(n_sp, span, width)
-    out_groups = out_full.reshape(n_sp, width, D)
-    inputs = x.astype(f32)
-    middle = inputs + jnp.einsum("jrc,jce->re", attended, out_groups, preferred_element_type=f32)
-    xhat_two, inverse_two = norm_parts(middle)
-    normed_two = (xhat_two * gain_two + shift_two).astype(bf16)
-
-    two_blocks, two_partners = plane.gather(normed_two)
+
+    def norm_next(normed, block, t, deps=()):
+        return norm_block(block, gain_one, shift_one, t, n_sp, normed, deps)
+
+    partner, one, twos = plane.gather_first(held(x, (joint_blocks[0], small_all)))
+    normed = norm_next(None, x, 0)
+    normed = norm_next(normed, partner, half)
+    one = held(one, (normed, joint_blocks[1:3], gate_up_cols))
+    one_other, two_others, threes = plane.gather_second(one, twos)
+    normed = norm_next(normed, one, 1)
+    for n, two in enumerate(twos):
+        normed = norm_next(normed, two, 2 + 2 * n)
+    normed = norm_next(normed, one_other, half + 1)
+    for n, two in enumerate(two_others):
+        normed = norm_next(normed, two, half + 2 + 2 * n)
+    threes = [held(three, (normed, joint_blocks[3:])) if n == 0 else three for n, three in enumerate(threes)]
+    for n, three in enumerate(threes):
+        normed = norm_next(normed, three, 3 + 2 * n)
+    for n, three in enumerate(plane.gather_third(threes)):
+        normed = norm_next(normed, three, half + 3 + 2 * n)
+    tables = rotary_columns(length, group)
+    heads = joint_projection(order, normed, joint_mine, bias, tables, span, groups)
+
+    out_full = lax.all_gather(held(out_weight, threes), ("fsdp", "sp"), axis=0, tiled=True)
+    ring = [(i, (i + 1) % n_z) for i in range(n_z)]
+    gate_up_blocks = [held(swap_sp(held(gate_up_cols, threes)).reshape(n_sp * depth, 2 * ff), heads[0])]
+    gate_up_blocks.append(lax.ppermute(gate_up_blocks[0], "fsdp", ring))
+    cot = cotangent.reshape(span, D)
+    cot_partner, cot_one, cot_twos = plane.gather_first(held(cot, gate_up_blocks[0]))
+    results = [attend(*heads[:3])]
+    cot_one = held(cot_one, results[0][1])
+    gate_up_blocks[1] = held(gate_up_blocks[1], results[0][1])
+    gate_up_blocks.append(lax.ppermute(gate_up_blocks[1], "fsdp", ring))
+    cot_one_other, cot_two_others, cot_threes = plane.gather_second(cot_one, cot_twos)
+    for g in range(1, groups):
+        results.append(attend(*heads[3 * g : 3 * g + 3], (cot_partner, cot_one, cot_twos, gate_up_blocks[1])))
+    cot_threes = [held(c, results[-1][1]) for c in cot_threes]
+    gate_up_blocks[2] = held(gate_up_blocks[2], results[-1][1])
+    for _ in range(3, n_z):
+        gate_up_blocks.append(lax.ppermute(gate_up_blocks[-1], "fsdp", ring))
+    cot_three_others = plane.gather_third(cot_threes)
+    cot_blocks, cot_partners = [cot, cot_one], [cot_partner, cot_one_other]
+    for pieces in zip(cot_twos, cot_threes):
+        cot_blocks += pieces
+    for pieces in zip(cot_two_others, cot_three_others):
+        cot_partners += pieces
+    gate_up = jnp.zeros((D, 2 * ff), bf16)
+    for step, block in enumerate(gate_up_blocks):
+        at = lax.rem(my_z - step + n_z, n_z) * (n_sp * depth)
+        gate_up = lax.dynamic_update_slice(gate_up, block, (at, 0))
+    attended = [swap_sp(o).reshape(n_sp, span, group) for o, _ in results]
+    middle, normed_two, attended_all = middle_of(attended, out_full, x, gain_two, shift_two, gate_up_blocks[:3])
+
     feed = None
-    for t in range(half):
-        feed = feed_block(
-            (two_blocks[t], two_partners[t]), (cot_blocks[t], cot_partners[t]), gate_up, down, t, half, feed
-        )
+
+    def feed_next(feed, pair, t, deps=()):
+        return feed_block(pair, (cot_blocks[t], cot_partners[t]), gate_up, down, t, half, feed, deps)
+
+    partner, one, twos = plane.gather_first(normed_two)
+    feed = feed_next(None, (normed_two, partner), 0, (cot_blocks, cot_partners))
+    one = held(one, feed[0])
+    one_other, two_others, threes = plane.gather_second(one, twos)
+    feed = feed_next(feed, (one, one_other), 1)
+    for n, two in enumerate(twos):
+        feed = feed_next(feed, (two, two_others[n]), 2 + 2 * n)
+        three = held(threes[n], feed[0]) if n == len(twos) - 1 else threes[n]
+        feed = feed_next(feed, (three, plane.send(three, plane.core)), 3 + 2 * n)
     hidden, gate_up_grad, two_all, cot_all = feed
 
-    def two_part(start, stop):
-        rows = gate_up_grad[start * span : stop * span]
-        return dot(rows, gate_up, NT).reshape(stop - start, span, D)
-
-    two_grad = plane.reduce(two_part)
-
-    def out_part(start, stop):
-        rows = hidden[start * span : stop * span]
-        return dot(rows, down, NN).reshape(stop - start, span, D)
-
-    output = (middle + plane.reduce(out_part)).astype(bf16)
-
+    two_product = product_of([gate_up_grad], gate_up, NT, span)
+    out_product = product_of([hidden], down, NN, span)
+    two_got = plane.reduce_far(two_product)
+    two_theirs = plane.reduce_near(two_product)
+    gate_up_sum = dot(two_all, gate_up_grad, TN).astype(bf16)
     down_sum = dot(hidden, cot_all, TN).astype(bf16)
-    gate_up_sum = dot(two_all, gate_up_grad, TN).astype(bf16)
-    down_grad = lax.psum_scatter(down_sum, "fsdp", scatter_dimension=0, tiled=True)[:ff_rows].astype(f32)
-    gate_up_own = swap_sp(lax.psum_scatter(gate_up_sum, "fsdp", scatter_dimension=0, tiled=True))
-    gate_up_own = gate_up_own.reshape(n_sp, depth, 2, n_z, ff_pad)[..., :ff_rows].transpose(2, 1, 3, 0, 4)
-    gate_up_own = gate_up_own.reshape(2, depth, n_z * n_sp * ff_rows).astype(f32)
-
-    two_input_grad, gain_two_sum, shift_two_sum = norm_back(two_grad, xhat_two, inverse_two, gain_two)
-    middle_grad = cotangent.reshape(span, D).astype(f32) + two_input_grad
-    branch_grad = middle_grad.astype(bf16)
-    attended_grad = jnp.einsum("re,jce->jrc", branch_grad, out_groups, preferred_element_type=f32).astype(bf16)
-    do = swap_sp(attended_grad.reshape(n_sp * span, width))
-    out_sum = jnp.einsum("jrc,re->jce", attended, branch_grad, preferred_element_type=f32).reshape(D, D)
-    out_grad = lax.psum_scatter(out_sum.astype(bf16), ("fsdp", "sp"), scatter_dimension=0, tiled=True).astype(f32)
-
-    joint_grad_rows = attend_back(place, q, k, v, do, o, lse, tables, span)
-
-    def normed_part(start, stop):
-        rows = joint_grad_rows[start * span : stop * span]
-        return dot(rows, joint_mine, NT).reshape(stop - start, span, D)
-
-    normed_grad = plane.reduce(normed_part)
-    joint_sum = dot(normed, joint_grad_rows, TN).astype(bf16)
-    joint_own = swap_sp(lax.psum_scatter(joint_sum, "fsdp", scatter_dimension=0, tiled=True))
-    joint_grad = joint_own.reshape(n_sp, depth, 3, width).transpose(1, 2, 0, 3).reshape(depth, 3 * D).astype(f32)
-    bias_sum = jnp.sum(joint_grad_rows.astype(f32), axis=0).reshape(3, 1, width)
+    gate_up_part = lax.psum_scatter(gate_up_sum, "fsdp", scatter_dimension=0, tiled=True)
+    down_part = lax.psum_scatter(down_sum, "fsdp", scatter_dimension=0, tiled=True)
+    two_last = plane.reduce_next(two_product, two_got, two_theirs, (gate_up_sum, down_sum))
+    two_grad = plane.reduce_own(two_product, two_got, two_theirs, two_last)
+    middle_grad, two_sums, branch_grad, *parts = norm_back(
+        two_grad, middle, gain_two, cotangent.reshape(span, D), out_full, n_sp, groups
+    )
+    dos = [swap_sp(part).reshape(n_sp * span, group) for part in parts]
+    out_sum = dot(attended_all, branch_grad, TN).astype(bf16).reshape(n_z, n_sp, depth, D)
+
+    def out_weight_part(start, stop, addends, dtype, deps=()):
+        parts = [lax.dynamic_index_in_dim(out_sum, order[b], 1, False).reshape(n_z * depth, D) for b in range(start, stop)]
+        total = jnp.stack(parts).astype(f32)
+        for addend, at in addends:
+            total += addend[at : at + stop - start].astype(f32)
+        return total.astype(dtype)
+
+    rows = attend_back(place, *heads[:3], dos[0], *results[0], tables, span, out_sum)
+    joint_rows = [rows]
+    joint_sums = [dot(normed, rows, TN).astype(bf16)]
+    joint_parts = [lax.psum_scatter(joint_sums[0], "fsdp", scatter_dimension=0, tiled=True)]
+    out_got = plane.reduce_far(out_product, branch_grad)
+    out_theirs = plane.reduce_near(out_product, branch_grad)
+    weight_got = plane.reduce_far(out_weight_part)
+    weight_theirs = plane.reduce_near(out_weight_part)
+    gate_up_own = swap_sp(gate_up_part)
+    for g in range(1, groups):
+        deps = (joint_sums, out_got, out_theirs, weight_got, weight_theirs, gate_up_own, down_part)
+        rows = attend_back(place, *heads[3 * g : 3 * g + 3], dos[g], *results[g], tables, span, deps)
+        joint_rows.append(rows)
+        joint_sums.append(dot(normed, rows, TN).astype(bf16))
+        joint_parts.append(lax.psum_scatter(joint_sums[g], "fsdp", scatter_dimension=0, tiled=True))
+    out_last = plane.reduce_next(out_product, out_got, out_theirs)
+    weight_last = plane.reduce_next(out_weight_part, weight_got, weight_theirs)
+
+    normed_product = product_of(joint_rows, joint_mine, NT, span)
+    normed_got = plane.reduce_far(normed_product, (out_last, weight_last, gate_up_own))
+    normed_theirs = plane.reduce_near(normed_product)
+    output = (middle + plane.reduce_own(out_product, out_got, out_theirs, out_last, f32)).astype(bf16)
+    out_own = plane.reduce_own(out_weight_part, weight_got, weight_theirs, weight_last)
+    out_grad = lax.psum_scatter(held(out_own, joint_parts), "fsdp", scatter_dimension=0, tiled=True).astype(f32)
+    down_grad = down_part[:ff_rows].astype(f32)
+    gate_grad, up_grad = join_feed(gate_up_own.reshape(n_sp, depth, 2 * ff), n_z, ff_rows, ff_pad)
+    bias_sum = jnp.stack([jnp.sum(r.astype(f32), axis=0).reshape(3, group) for r in joint_rows], 1)
+    bias_sum = bias_sum.reshape(3, 1, width)
     bias_sum = lax.dynamic_update_slice(jnp.zeros((3, n_sp, width), f32), bias_sum, (0, me, 0))
-
-    xhat_one, inverse_one = norm_parts(inputs)
-    input_grad, gain_one_sum, shift_one_sum = norm_back(normed_grad, xhat_one, inverse_one, gain_one)
-    tokens_grad = (middle_grad + input_grad).reshape(tokens.shape)
-
-    sums = [gain_one_sum, shift_one_sum, gain_two_sum, shift_two_sum]
+    joint_own = [swap_sp(j).reshape(n_sp, depth, 3 * group) for j in joint_parts]
+    fill = (joint_sums, output, gate_grad, up_grad, bias_sum, joint_own[:-1])
+    normed_last = plane.reduce_next(normed_product, normed_got, normed_theirs, fill)
+    normed_grad = plane.reduce_own(normed_product, normed_got, normed_theirs, normed_last)
+    tokens_grad, one_sums = norm_back(normed_grad, x, gain_one, middle_grad)
+    tokens_grad = tokens_grad.reshape(tokens.shape)
+
+    joint_grad = join_joint(joint_own, n_sp)
+
+    sums = [one_sums[0], one_sums[1], two_sums[0], two_sums[1]]
     sums = jnp.concatenate([s.reshape(n_all, n_gain) for s in sums] + [bias_sum.reshape(n_all, -1)], axis=1)
     sums = jnp.sum(lax.all_to_all(sums, ("fsdp", "sp"), split_axis=0, concat_axis=0, tiled=True), axis=0)
     gain_one_grad, shift_one_grad, gain_two_grad, shift_two_grad = (
@@ -613,8 +936,8 @@
         out_grad,
         gain_two_grad,
         shift_two_grad,
-        gate_up_own[0],
-        gate_up_own[1],
+        gate_grad,
+        up_grad,
         down_grad,
     )
 

time: 1230 us -> 1010 us (0.82)
  waiting for transfers between devices: 407 us -> 192 us
  Pallas kernels: 314 us -> 519 us
  matrix products: 196 us -> 88.1 us
  other arithmetic: 97.8 us -> 27.1 us
  local copies, waits for them, and re-layouts: 111 us -> 59.4 us
  starting transfers between devices: 58 us -> 80.7 us
  blocking collectives: 17.8 us -> 0 us
  between operations: 15.2 us -> 30.5 us
    pallas_call x12 -> x48, Pallas kernels: 93.4 us -> 280 us  [launch(): pl.pallas_call(body, grid_spec=pltpu.PrefetchScalarGridSpec(num_scalar_pr...]
    ppermute x27 -> x29, waiting for transfers between devices: 180 us -> 17.5 us  [send(): return lax.ppermute(value, 'sp', perm)]
    dot_general x15 -> x5, matrix products: 170 us -> 88.1 us  [dot(): return lax.dot_general(a, b, dims, preferred_element_type=f32)]
    ppermute x0 -> x6, waiting for transfers between devices: none -> 81.8 us  [the longest x3 35 us: per_device(): lax.ppermute(joint_blocks[-1], 'fsdp', [(i, (i + 1) % n_z) for i in range...]
    ppermute x6 -> x8, waiting for transfers between devices: 133 us -> 55.3 us  [back(): return lax.ppermute(value, 'sp', [(b, a) for a, b in perm])]
    all_to_all x5 -> x9, waiting for transfers between devices: 92.7 us -> 30.1 us  [swap_sp(): return lax.all_to_all(value, 'sp', split_axis=0, concat_axis=0, tiled=True)]
    add x4 -> x0, other arithmetic: 40.2 us -> none  [the longest x3 34.9 us: reduce(): total = mine if total is None else mine + total]
    dot_general x3 -> x0, matrix products: 26.2 us -> none  [the longest x1 9.19 us: per_device(): jnp.einsum('re,jce->jrc', branch_grad, out_groups, preferred_element_type...]
  transfers between devices with their start and end apart: 48 -> 61, of which waited for: 16 -> 19; matrix products, arithmetic and copies ran while one was open for 28% -> 15% of each run, Pallas kernels for 24% -> 48%
where the time goes in v2:
time: 1010 us; the launch traced here: 997 us
  Pallas kernels  519 us (51%)
  waiting for transfers between devices  192 us (19%)
  matrix products  88.1 us (9%)
  starting transfers between devices  80.7 us (8%)
  local copies, waits for them, and re-layouts  59.4 us (6%)
  between operations  30.5 us (3%)
  other arithmetic  27.1 us (3%)
    pallas_call x48, Pallas kernels, launch(): pl.pallas_call(body, grid_spec=pltpu.PrefetchScalarGridSpec(num_scalar_pr...  280 us
    pallas_call x2, Pallas kernels, attend_back(): pl.pallas_call(functools.partial(attend_back_kernel, heads, bq, bk), grid...  126 us
    pallas_call x2, Pallas kernels, attend(): pl.pallas_call(functools.partial(attend_kernel, heads, bq, bk), grid=(len...  92.2 us
    dot_general x5, matrix products, dot(): return lax.dot_general(a, b, dims, preferred_element_type=f32)  88.1 us
    ppermute x8, waiting for transfers between devices, back(): return lax.ppermute(value, 'sp', [(b, a) for a, b in perm])  55.3 us
    all_to_all x9, starting transfers between devices, swap_sp(): return lax.all_to_all(value, 'sp', split_axis=0, concat_axis=0, tiled=True)  35.2 us
    ppermute x3, waiting for transfers between devices, per_device(): lax.ppermute(joint_blocks[-1], 'fsdp', [(i, (i + 1) % n_z) for i in range...  35 us
    all_to_all x9, waiting for transfers between devices, swap_sp(): return lax.all_to_all(value, 'sp', split_axis=0, concat_axis=0, tiled=True)  30.1 us
  transfers between devices with their start and end apart: 61, of which 19 were waited for; matrix products, arithmetic and copies ran while one was open for 15% of the time, Pallas kernels for 48%

profile of v2, /device:TPU:0, one launch (start us, length us, event | category | flops | bytes accessed | tf_op | source)
XLA Modules:
  0.0 996.9 jit_solution(15853860034246106570)
XLA Ops:
  47.8 20.9 %collective-permute-done.2.refs_2_ = bf16[512,768]{1,0:T(8,128)(2,1)} collective-permute-done((bf16[512,768]{1,0:T(8,128)(2,1)}, bf16[512,768]{1,0:T(8,128)(2,1)}, u32[]{:S(2)}, u32[]{:S(2)}) %collective-permute-start.2) | collective-permute-done | bytes 786464 | tf_op jit(solution)/shard_map/ppermute | solution.py:781
  147.0 21.4 %joint_projection.1 = (bf16[4096,128]{1,0:T(8,128)(2,1)}, bf16[4096,128]{1,0:T(8,128)(2,1)}, bf16[4096,128]{1,0:T(8,128)(2,1)}, bf16[4096,128]{1,0:T(8,128)(2,1)...) custom-call(s32[8]{0:T(128)} %get-tuple-element.105.table_ref, bf16[4096,2048]{1,0:T(8,128)(2,1)} %first_norm.15.x_ref, ...), custom_call_target="tpu_custom_call" | custom-call | flops 12884901888 | bytes 23068672 | tf_op jit(solution)/shard_map/joint_projection/pallas_call | solution.py:434
  173.5 46.3 %attend.2 = (bf16[4096,128]{1,0:T(8,128)(2,1)}, f32[8,4096]{1,0:T(8,128)}) custom-call(bf16[4096,128]{1,0:T(8,128)(2,1)} %get-tuple-element.50.q_ref.refs_1_, bf16[4096,128]{1,0:T(8,128)(2,1)} %get-tuple-element.51.k_ref, bf16[4096,128]{1,0:T(8,128)(2,1)} %get-tuple-element.52.v_ref), custom_call_target="tpu_custom_call" | custom-call | flops 17179869184 | bytes 4194304 | tf_op jit(solution)/shard_map/attend/pallas_call | solution.py:517
  235.9 45.8 %attend.3 = (bf16[4096,128]{1,0:T(8,128)(2,1)}, f32[8,4096]{1,0:T(8,128)}) custom-call(bf16[4096,128]{1,0:T(8,128)(2,1)} %get-tuple-element.54.q_ref, bf16[4096,128]{1,0:T(8,128)(2,1)} %get-tuple-element.55.k_ref, bf16[4096,128]{1,0:T(8,128)(2,1)} %get-tuple-element.56.v_ref, bf16[512,2048]{1,0:T(8,128)(2,1)} %collective-permute-done.10.rest_0_.refs_3_.refs_10_, ...), custom_call_target="tpu_custom_call" | custom-call | flops 17179869184 | bytes 4194304 | tf_op jit(solution)/shard_map/attend/pallas_call | solution.py:517
  287.5 19.1 %collective-permute-done.14.refs_0_ = bf16[512,1536]{1,0:T(8,128)(2,1)S(1)} collective-permute-done((bf16[512,1536]{1,0:T(8,128)(2,1)}, bf16[512,1536]{1,0:T(8,128)(2,1)S(1)}, u32[]{:S(2)}, u32[]{:S(2)}) %collective-permute-start.14) | collective-permute-done | bytes 1572896 | tf_op jit(solution)/shard_map/ppermute | solution.py:825
  318.3 11.3 %middle.1 = (f32[512,2048]{1,0:T(8,128)}, bf16[512,2048]{1,0:T(8,128)(2,1)}, bf16[512,2048]{1,0:T(8,128)(2,1)}) custom-call(bf16[8,512,128]{2,1,0:T(8,128)(2,1)} %all-to-all-done.2.refs_0_, bf16[8,512,128]{2,1,0:T(8,128)(2,1)} %copy-done.18, bf16[2048,2048]{1,0:T(8,128)(2,1)} %all-gather.3.cloned.1.call-done.refs_2_.refs_4_, bf16[512,2048]{1,0:T(8,128)(2,1)} %bitcast.63, ...), custom_call_target="tpu_custom_call" | custom-call | flops 4294967296 | bytes 20971520 | tf_op jit(solution)/shard_map/middle/pallas_call | solution.py:128
  338.7 18.3 %collective-permute-done.17 = bf16[512,1536]{1,0:T(8,128)(2,1)} collective-permute-done((bf16[512,1536]{1,0:T(8,128)(2,1)}, bf16[512,1536]{1,0:T(8,128)(2,1)}, u32[]{:S(2)}, u32[]{:S(2)}) %collective-permute-start.17) | collective-permute-done | bytes 1572896 | tf_op jit(solution)/shard_map/ppermute | solution.py:832
  362.1 18.1 %feed_forward.4 = (bf16[4096,768]{1,0:T(8,128)(2,1)}, bf16[4096,1536]{1,0:T(8,128)(2,1)}, bf16[4096,2048]{1,0:T(8,128)(2,1)}, bf16[4096,2048]{1,0:T(8,128)(2,1)}) custom-call(bf16[512,2048]{1,0:T(8,128)(2,1)} %get-tuple-element.61.refs_0_, bf16[512,2048]{1,0:T(8,128)(2,1)} %collective-permute-done.16.refs_1_, bf16[512,2048]{1,0:T(8,128)(2,1)} %bitcast.70, ...), custom_call_target="tpu_custom_call" | custom-call | flops 9663676416 | bytes 26214400 | tf_op jit(solution)/shard_map/feed_forward/pallas_call | solution.py:128
  386.0 18.0 %feed_forward.5 = (bf16[4096,768]{1,0:T(8,128)(2,1)}, bf16[4096,1536]{1,0:T(8,128)(2,1)}, bf16[4096,2048]{1,0:T(8,128)(2,1)}, bf16[4096,2048]{1,0:T(8,128)(2,1)}) custom-call(bf16[512,2048]{1,0:T(8,128)(2,1)} %held.25.refs_0_, ...), custom_call_target="tpu_custom_call", output_to_operand_aliasing={{0}: (6, {}), {1}: (7, {}), {2}: (8, {}), {3}: (9, {})} | custom-call | flops 9663676416 | bytes 26214400 | tf_op jit(solution)/shard_map/feed_forward/pallas_call | solution.py:128
  404.0 18.1 %feed_forward.6 = (bf16[4096,768]{1,0:T(8,128)(2,1)}, bf16[4096,1536]{1,0:T(8,128)(2,1)}, bf16[4096,2048]{1,0:T(8,128)(2,1)}, bf16[4096,2048]{1,0:T(8,128)(2,1)}) custom-call(bf16[512,2048]{1,0:T(8,128)(2,1)} %collective-permute-done.23.refs_0_, ...), custom_call_target="tpu_custom_call", output_to_operand_aliasing={{0}: (6, {}), {1}: (7, {}), {2}: (8, {}), {3}: (9, {})} | custom-call | flops 9663676416 | bytes 26214400 | tf_op jit(solution)/shard_map/feed_forward/pallas_call | solution.py:128
  429.1 18.2 %feed_forward.7 = (bf16[4096,768]{1,0:T(8,128)(2,1)}, bf16[4096,1536]{1,0:T(8,128)(2,1)}, bf16[4096,2048]{1,0:T(8,128)(2,1)}, bf16[4096,2048]{1,0:T(8,128)(2,1)}) custom-call(bf16[512,2048]{1,0:T(8,128)(2,1)} %held.26.refs_0_, bf16[512,2048]{1,0:T(8,128)(2,1)} %copy-done.24, ...), custom_call_target="tpu_custom_call", output_to_operand_aliasing={{0}: (6, {}), {1}: (7, {}), {2}: (8, {}), {3}: (9, {})} | custom-call | flops 9663676416 | bytes 26214400 | tf_op jit(solution)/shard_map/feed_forward/pallas_call | solution.py:128
  447.3 10.7 %block_product.16 = bf16[2,512,2048]{2,1,0:T(8,128)(2,1)} custom-call(bf16[4096,1536]{1,0:T(8,128)(2,1)} %get-tuple-element.75.refs_0_, bf16[2048,1536]{1,0:T(8,128)(2,1)} %constant_dynamic-update-slice_fusion.refs_4_.refs_1_), custom_call_target="tpu_custom_call" | custom-call | flops 6442450944 | bytes 17825792 | tf_op jit(solution)/shard_map/block_product/pallas_call | solution.py:128
  458.1 34.0 %convolution_convert_fusion.1.refs_4_ = bf16[2048,1536]{1,0:T(8,128)(2,1)} fusion(bf16[4096,2048]{1,0:T(8,128)(2,1)} %get-tuple-element.76, bf16[4096,1536]{1,0:T(8,128)(2,1)} %get-tuple-element.75.refs_0_), kind=kOutput, calls=%fused_computation.1 | convolution fusion | flops 25772949504 | bytes 35651584 | tf_op jit(solution)/shard_map/dot_general | solution.py:28
  492.2 11.1 %block_product.15 = bf16[2,512,2048]{2,1,0:T(8,128)(2,1)} custom-call(bf16[4096,1536]{1,0:T(8,128)(2,1)} %get-tuple-element.75.refs_0_, bf16[2048,1536]{1,0:T(8,128)(2,1)} %constant_dynamic-update-slice_fusion.refs_4_.refs_1_), custom_call_target="tpu_custom_call" | custom-call | flops 6442450944 | bytes 17825792 | tf_op jit(solution)/shard_map/block_product/pallas_call | solution.py:128
  503.7 11.4 %block_product.17 = bf16[2,512,2048]{2,1,0:T(8,128)(2,1)} custom-call(bf16[4096,1536]{1,0:T(8,128)(2,1)} %get-tuple-element.75.refs_0_, bf16[2048,1536]{1,0:T(8,128)(2,1)} %constant_dynamic-update-slice_fusion.refs_4_.refs_1_, bf16[2,512,2048]{2,1,0:T(8,128)(2,1)} %collective-permute-done.28.refs_2_), custom_call_target="tpu_custom_call" | custom-call | flops 6442450944 | bytes 17825792 | tf_op jit(solution)/shard_map/block_product/pallas_call | solution.py:128
  516.1 20.0 %convolution_convert_fusion.2.refs_5_ = bf16[768,2048]{1,0:T(8,128)(2,1)} fusion(bf16[4096,768]{1,0:T(8,128)(2,1)} %get-tuple-element.74.refs_0_, bf16[4096,2048]{1,0:T(8,128)(2,1)} %get-tuple-element.77), kind=kOutput, calls=%fused_computation.7 | convolution fusion | flops 12886474752 | bytes 26214400 | tf_op jit(solution)/shard_map/dot_general | solution.py:28
  536.1 27.7 %collective-permute-done.29.refs_3_ = bf16[2,512,2048]{2,1,0:T(8,128)(2,1)} collective-permute-done((bf16[2,512,2048]{2,1,0:T(8,128)(2,1)}, bf16[2,512,2048]{2,1,0:T(8,128)(2,1)}, u32[]{:S(2)}, u32[]{:S(2)}) %collective-permute-start.29) | collective-permute-done | bytes 4194336 | tf_op jit(solution)/shard_map/ppermute | solution.py:79
  608.9 20.7 %norm_back.2 = (f32[512,2048]{1,0:T(8,128)}, f32[8,2048]{1,0:T(8,128)}, bf16[512,2048]{1,0:T(8,128)(2,1)}, bf16[8,512,128]{2,1,0:T(8,128)(2,1)}, bf16[8,512,128]{2,1,0:T(8,128)(2,1)}) custom-call(bf16[512,2048]{1,0:T(8,128)(2,1)} %bitcast.74, f32[512,2048]{1,0:T(8,128)} %get-tuple-element.60.refs_1_, f32[1,2048]{1,0:T(1,128)} %reshape.169.refs_4_.refs_2_, ...), custom_call_target="tpu_custom_call" | custom-call | flops 4315938816 | bytes 25165824 | tf_op jit(solution)/shard_map/norm_back/pallas_call | solution.py:128
  683.3 62.8 %attend_back.2.refs_0_ = bf16[4096,384]{1,0:T(8,128)(2,1)} custom-call(s32[8]{0:T(128)} %fusion.7.place_ref, bf16[4096,128]{1,0:T(8,128)(2,1)} %get-tuple-element.50.q_ref.refs_1_, bf16[4096,128]{1,0:T(8,128)(2,1)} %get-tuple-element.51.k_ref, bf16[4096,128]{1,0:T(8,128)(2,1)} %get-tuple-element.52.v_ref, bf16[4096,128]{1,0:T(8,128)(2,1)} %bitcast.90, ...), custom_call_target="tpu_custom_call" | custom-call | flops 25769803776 | bytes 8388608 | tf_op jit(solution)/shard_map/attend_back/pallas_call | solution.py:621
  756.1 13.3 %convolution_convert_fusion.4.rest_0_.refs_6_ = bf16[2048,384]{1,0:T(8,128)(2,1)} fusion(bf16[4096,2048]{1,0:T(8,128)(2,1)} %first_norm.15.x_ref, bf16[4096,384]{1,0:T(8,128)(2,1)S(1)} %copy-done.1), kind=kOutput, calls=%fused_computation.9 | convolution fusion | flops 6443237376 | bytes 21495808 | tf_op jit(solution)/shard_map/dot_general | solution.py:28
  781.3 62.8 %attend_back.3.refs_1_ = bf16[4096,384]{1,0:T(8,128)(2,1)} custom-call(s32[8]{0:T(128)} %fusion.7.place_ref, bf16[4096,128]{1,0:T(8,128)(2,1)} %get-tuple-element.54.q_ref, bf16[4096,128]{1,0:T(8,128)(2,1)} %get-tuple-element.55.k_ref, bf16[4096,128]{1,0:T(8,128)(2,1)} %get-tuple-element.56.v_ref, bf16[4096,128]{1,0:T(8,128)(2,1)} %bitcast.14.do_ref, ...), custom_call_target="tpu_custom_call" | custom-call | flops 25769803776 | bytes 8388608 | tf_op jit(solution)/shard_map/attend_back/pallas_call | solution.py:621
  874.2 14.4 %convolution_convert_fusion.3.refs_7_ = bf16[2048,384]{1,0:T(8,128)(2,1)} fusion(bf16[4096,2048]{1,0:T(8,128)(2,1)} %first_norm.15.x_ref, bf16[4096,384]{1,0:T(8,128)(2,1)} %attend_back.3.refs_1_), kind=kOutput, calls=%fused_computation.8 | convolution fusion | flops 6443237376 | bytes 21495808 | tf_op jit(solution)/shard_map/dot_general | solution.py:28
  911.7 13.9 %all-to-all-done.8.refs_12_.refs_0_ = bf16[8,64,384]{2,1,0:T(8,128)(2,1)S(1)} async-done(((bf16[8,64,384]{2,1,0:T(8,128)(2,1)}), bf16[8,64,384]{2,1,0:T(8,128)(2,1)S(1)}, u32[]{:S(2)}, u32[]{:S(2)}) %all-to-all-start.8) | async-done | bytes 393248 | tf_op jit(solution)/shard_map/all_to_all | solution.py:739
  942.7 19.0 %collective-permute-done.42.refs_6_ = bf16[1,512,2048]{2,1,0:T(8,128)(2,1)} collective-permute-done((bf16[1,512,2048]{2,1,0:T(8,128)(2,1)}, bf16[1,512,2048]{2,1,0:T(8,128)(2,1)}, u32[]{:S(2)}, u32[]{:S(2)}) %collective-permute-start.42) | collective-permute-done | bytes 2097184 | tf_op jit(solution)/shard_map/ppermute | solution.py:79
  (297 shorter events, 389.2 us)
Async XLA Ops:
  32.6 284.7 %all-gather.3.cloned.1.call-start = ((), (), s32[]{:S(2)}) async-start(), calls=%async_computation.16 | async-start | bytes 8650752 | tf_op jit(solution)/shard_map/all_gather | solution.py:816
  135.8 226.3 %all-gather.5.cloned.1.call-start = ((), (), s32[]{:S(2)}) async-start(), calls=%async_computation.17 | async-start | bytes 3932160 | tf_op jit(solution)/shard_map/all_gather | solution.py:789
  168.4 66.2 %collective-permute-start.11 = (bf16[512,2048]{1,0:T(8,128)(2,1)}, bf16[512,2048]{1,0:T(8,128)(2,1)}, u32[]{:S(2)}, u32[]{:S(2)}) collective-permute-start(bf16[512,2048]{1,0:T(8,128)(2,1)} %held.19), channel_id=1, source_target_pairs={{0,2},{1,5},{2,0},{3,7},{4,6},{5,1},{6,4},{7,3},{8,10},{9,13},{10,... | collective-permute-start | bytes 6291464 | tf_op jit(solution)/shard_map/ppermute | solution.py:75
  170.3 65.6 %collective-permute-start.10 = (bf16[512,2048]{1,0:T(8,128)(2,1)}, bf16[512,2048]{1,0:T(8,128)(2,1)}, u32[]{:S(2)}, u32[]{:S(2)}) collective-permute-start(bf16[512,2048]{1,0:T(8,128)(2,1)} %held.19), channel_id=1, source_target_pairs={{0,1},{1,0},{2,3},{3,2},{4,5},{5,4},{6,7},{7,6},{8,9},{9,8},{10,11... | collective-permute-start | bytes 6291464 | tf_op jit(solution)/shard_map/ppermute | solution.py:75
  170.3 65.6 %collective-permute-start.12 = (bf16[512,2048]{1,0:T(8,128)(2,1)}, bf16[512,2048]{1,0:T(8,128)(2,1)}, u32[]{:S(2)}, u32[]{:S(2)}) collective-permute-start(bf16[512,2048]{1,0:T(8,128)(2,1)} %held.19), channel_id=1, source_target_pairs={{0,4},{1,3},{2,6},{3,1},{4,0},{5,7},{6,2},{7,5},{8,12},{9,11},{10,... | collective-permute-start | bytes 6291464 | tf_op jit(solution)/shard_map/ppermute | solution.py:75
  172.8 60.7 %collective-permute-start.13 = (bf16[512,1536]{1,0:T(8,128)(2,1)}, bf16[512,1536]{1,0:T(8,128)(2,1)S(1)}, u32[]{:S(2)}, u32[]{:S(2)}) collective-permute-start(bf16[512,1536]{1,0:T(8,128)(2,1)} %held.18.refs_1_.refs_6_), channel_id=1, source_target_pairs={{0,8},{8,16},{16,24},{24,0},{1,9},{9,17},{17,25},{25,1},{2,10},{10... | collective-permute-start | bytes 4718600 | tf_op jit(solution)/shard_map/ppermute | solution.py:819
  219.8 61.9 %all-to-all-start.2 = ((bf16[8,512,128]{2,1,0:T(8,128)(2,1)}), bf16[8,512,128]{2,1,0:T(8,128)(2,1)}, u32[]{:S(2)}, u32[]{:S(2)}) async-start(bf16[8,512,128]{2,1,0:T(8,128)(2,1)} %bitcast.89), calls=%async_computation.2 | async-start | bytes 2097152 | tf_op jit(solution)/shard_map/all_to_all | solution.py:739
  234.6 71.9 %collective-permute-start.14 = (bf16[512,1536]{1,0:T(8,128)(2,1)}, bf16[512,1536]{1,0:T(8,128)(2,1)S(1)}, u32[]{:S(2)}, u32[]{:S(2)}) collective-permute-start(bf16[512,1536]{1,0:T(8,128)(2,1)} %held.21.rest_3_.refs_7_), channel_id=1, source_target_pairs={{0,8},{8,16},{16,24},{24,0},{1,9},{9,17},{17,25},{25,1},{2,10},{10... | collective-permute-start | bytes 4718600 | tf_op jit(solution)/shard_map/ppermute | solution.py:825
  234.7 82.6 %collective-permute-start.18 = (bf16[512,2048]{1,0:T(8,128)(2,1)}, bf16[512,2048]{1,0:T(8,128)(2,1)}, u32[]{:S(2)}, u32[]{:S(2)}) collective-permute-start(bf16[512,2048]{1,0:T(8,128)(2,1)} %held.20.rest_1_.refs_7_.refs_2_), channel_id=1, source_target_pairs={{0,4},{1,3},{2,6},{3,1},{4,0},{5,7},{6,2},{7,5},{8,12},{9,11},{10,... | collective-permute-start | bytes 6291464 | tf_op jit(solution)/shard_map/ppermute | solution.py:75
  285.6 466.2 %reduce-scatter.6.cloned.1.call-start = ((), (), s32[]{:S(2)}) async-start(), calls=%async_computation.18 | async-start | bytes 7864320 | tf_op jit(solution)/shard_map/reduce_scatter | solution.py:868
  287.4 74.6 %collective-permute-start.20 = (bf16[512,2048]{1,0:T(8,128)(2,1)}, bf16[512,2048]{1,0:T(8,128)(2,1)}, u32[]{:S(2)}, u32[]{:S(2)}) collective-permute-start(bf16[512,2048]{1,0:T(8,128)(2,1)} %collective-permute-done.12.rest_2_.refs_8_.refs_2_), channel_id=1, source_target_pairs={{0,1},{1,0},{2,3},{3,2},{4,5},{5,4},{6,7},{7,6},{8,9},{9,8},{10,11... | collective-permute-start | bytes 6291464 | tf_op jit(solution)/shard_map/ppermute | solution.py:75
  492.1 289.1 %reduce-scatter.8.cloned.1.call-start = ((), (), s32[]{:S(2)}) async-start(), calls=%async_computation.19 | async-start | bytes 3932160 | tf_op jit(solution)/shard_map/reduce_scatter | solution.py:869
  653.7 115.7 %collective-permute-start.37 = (bf16[2,256,2048]{2,1,0:T(8,128)(2,1)}, bf16[2,256,2048]{2,1,0:T(8,128)(2,1)}, u32[]{:S(2)}, u32[]{:S(2)}) collective-permute-start(bf16[2,256,2048]{2,1,0:T(8,128)(2,1)} %pad_maximum_fusion.1), channel_id=1, source_target_pairs={{0,1},{1,0},{2,3},{3,2},{4,5},{5,4},{6,7},{7,6},{8,9},{9,8},{10,11... | collective-permute-start | bytes 6291464 | tf_op jit(solution)/shard_map/ppermute | solution.py:75
  664.6 110.1 %collective-permute-start.31 = (bf16[2,512,2048]{2,1,0:T(8,128)(2,1)}, bf16[2,512,2048]{2,1,0:T(8,128)(2,1)}, u32[]{:S(2)}, u32[]{:S(2)}) collective-permute-start(bf16[2,512,2048]{2,1,0:T(8,128)(2,1)} %block_product.20), channel_id=1, source_target_pairs={{0,1},{1,0},{2,3},{3,2},{4,5},{5,4},{6,7},{7,6},{8,9},{9,8},{10,11... | collective-permute-start | bytes 12582920 | tf_op jit(solution)/shard_map/ppermute | solution.py:75
  668.8 100.7 %collective-permute-start.36 = (bf16[2,256,2048]{2,1,0:T(8,128)(2,1)}, bf16[2,256,2048]{2,1,0:T(8,128)(2,1)}, u32[]{:S(2)}, u32[]{:S(2)}) collective-permute-start(bf16[2,256,2048]{2,1,0:T(8,128)(2,1)} %add_convert_fusion), channel_id=1, source_target_pairs={{4,0},{3,1},{6,2},{1,3},{0,4},{7,5},{2,6},{5,7},{12,8},{11,9},{14,... | collective-permute-start | bytes 6291464 | tf_op jit(solution)/shard_map/ppermute | solution.py:79
  678.4 96.3 %collective-permute-start.33 = (bf16[2,512,2048]{2,1,0:T(8,128)(2,1)}, bf16[2,512,2048]{2,1,0:T(8,128)(2,1)}, u32[]{:S(2)}, u32[]{:S(2)}) collective-permute-start(bf16[2,512,2048]{2,1,0:T(8,128)(2,1)} %block_product.22), channel_id=1, source_target_pairs={{4,0},{3,1},{6,2},{1,3},{0,4},{7,5},{2,6},{5,7},{12,8},{11,9},{14,... | collective-permute-start | bytes 12582920 | tf_op jit(solution)/shard_map/ppermute | solution.py:79
  678.8 73.0 %all-to-all-start.6 = ((bf16[8,512,128]{2,1,0:T(8,128)(2,1)}), bf16[8,512,128]{2,1,0:T(8,128)(2,1)}, u32[]{:S(2)}, u32[]{:S(2)}) async-start(bf16[8,512,128]{2,1,0:T(8,128)(2,1)} %get-tuple-element.81), calls=%async_computation.6 | async-start | bytes 2097152 | tf_op jit(solution)/shard_map/all_to_all | solution.py:739
  756.0 136.5 %reduce-scatter.10.cloned.1.call-start = ((), (), s32[]{:S(2)}) async-start(), calls=%async_computation.20 | async-start | bytes 1966080 | tf_op jit(solution)/shard_map/reduce_scatter | solution.py:888
  772.8 71.2 %collective-permute-start.39 = (bf16[1,256,2048]{2,1,0:T(8,128)(2,1)}, bf16[1,256,2048]{2,1,0:T(8,128)(2,1)S(1)}, u32[]{:S(2)}, u32[]{:S(2)}) collective-permute-start(bf16[1,256,2048]{2,1,0:T(8,128)(2,1)} %fusion.5), channel_id=1, source_target_pairs={{2,0},{5,1},{0,2},{7,3},{6,4},{1,5},{4,6},{3,7},{10,8},{13,9},{8,1... | collective-permute-start | bytes 3145736 | tf_op jit(solution)/shard_map/ppermute | solution.py:79
  781.1 62.9 %collective-permute-start.34 = (bf16[1,512,2048]{2,1,0:T(8,128)(2,1)}, bf16[1,512,2048]{2,1,0:T(8,128)(2,1)S(1)}, u32[]{:S(2)}, u32[]{:S(2)}) collective-permute-start(bf16[1,512,2048]{2,1,0:T(8,128)(2,1)} %block_product.23), channel_id=1, source_target_pairs={{2,0},{5,1},{0,2},{7,3},{6,4},{1,5},{4,6},{3,7},{10,8},{13,9},{8,1... | collective-permute-start | bytes 6291464 | tf_op jit(solution)/shard_map/ppermute | solution.py:79
  854.4 83.6 %reduce-scatter.12.cloned.1.call-start = ((), (), s32[]{:S(2)}) async-start(), calls=%async_computation.21 | async-start | bytes 1966080 | tf_op jit(solution)/shard_map/reduce_scatter | solution.py:899
  862.8 62.8 %collective-permute-start.38 = (bf16[2,512,2048]{2,1,0:T(8,128)(2,1)}, bf16[2,512,2048]{2,1,0:T(8,128)(2,1)}, u32[]{:S(2)}, u32[]{:S(2)}) collective-permute-start(bf16[2,512,2048]{2,1,0:T(8,128)(2,1)} %block_product.25), channel_id=1, source_target_pairs={{0,1},{1,0},{2,3},{3,2},{4,5},{5,4},{6,7},{7,6},{8,9},{9,8},{10,11... | collective-permute-start | bytes 12582920 | tf_op jit(solution)/shard_map/ppermute | solution.py:75
  872.2 53.4 %collective-permute-start.41 = (bf16[2,512,2048]{2,1,0:T(8,128)(2,1)}, bf16[2,512,2048]{2,1,0:T(8,128)(2,1)}, u32[]{:S(2)}, u32[]{:S(2)}) collective-permute-start(bf16[2,512,2048]{2,1,0:T(8,128)(2,1)} %block_product.27), channel_id=1, source_target_pairs={{4,0},{3,1},{6,2},{1,3},{0,4},{7,5},{2,6},{5,7},{12,8},{11,9},{14,... | collective-permute-start | bytes 12582920 | tf_op jit(solution)/shard_map/ppermute | solution.py:79
  896.0 88.8 %reduce-scatter.14.cloned.1.call-start = ((), (), s32[]{:S(2)}) async-start(), calls=%async_computation.22 | async-start | bytes 1310720 | tf_op jit(solution)/shard_map/reduce_scatter | solution.py:908
  (73 other events, 1393.3 us)
Sparse Core Ops, SparseCore 0:
  124.1 103.6 all-gather.2
  229.4 94.7 all-gather.4
  492.3 108.1 reduce-scatter.5
  649.9 57.8 reduce-scatter.7
  854.5 33.9 reduce-scatter.9
  890.7 34.2 reduce-scatter.11
  938.1 24.3 reduce-scatter.13

commit v3 on v2

--- a/solution.py
+++ b/solution.py
@@ -69,6 +69,7 @@
         blocks += [moved(b, self.core) for b in blocks]
         self.table = np.array(blocks, np.int32).T
         self.half = 2 * outer
+        self.far = list(reversed(range(2, self.half, 2)))
 
     @staticmethod
     def send(value, perm):
@@ -96,23 +97,37 @@
         return [self.send(three, self.core) for three in threes]
 
 
-    def reduce_far(self, product, deps=()):
-        sent = []
-        for start in reversed(range(2, self.half, 2)):
-            theirs = self.send(product(self.half + start, self.half + start + 2, (), bf16, deps), self.core)
-            mine = product(start, start + 2, ((theirs, 0),), bf16)
-            sent.append(self.back(mine, self.later[start // 2 - 1]))
-        return sent
-
-    def reduce_near(self, product, deps=()):
-        return self.send(product(self.half, self.half + 2, (), bf16, deps), self.core)
+    def reduce_sums(self, product, deps=(), apart=False):
+        far = [product(self.half + start, self.half + start + 2, (), bf16, deps) for start in self.far]
+        near = product(self.half, self.half + 2, (), bf16, far)
+        theirs = [self.send(value, self.core) for value in far]
+        more = (True,) if apart else ()
+        sums = [product(start, start + 2, ((value, 0),), bf16, near, *more) for start, value in zip(self.far, theirs)]
+        return sums, self.send(near, self.core)
+
+    def reduce_leg(self, sums):
+        return [self.back(value, self.later[start // 2 - 1]) for start, value in zip(self.far, sums)]
 
     def reduce_next(self, product, got, theirs, deps=()):
         one = product(1, 2, tuple((t, 1) for t in [theirs] + got), bf16, deps)
-        return self.back(one, self.first)
-
-    def reduce_own(self, product, got, theirs, last, dtype=bf16):
-        return product(0, 1, tuple((t, 0) for t in [theirs] + got + [last]), dtype)[0]
+        return one, self.back(one, self.first)
+
+    def reduce_own(self, product, got, theirs, last, dtype=bf16, deps=()):
+        return product(0, 1, tuple((t, 0) for t in [theirs] + got + [last]), dtype, deps)[0]
+
+
+    def legs(self, sums):
+        perms = [self.later[start // 2 - 1] for start in self.far]
+        further = [self.back(pair[1], perm) for pair, perm in zip(sums, perms)]
+        nearer = [self.back(held(pair[0], further), perm) for pair, perm in zip(sums, perms)]
+        return further, nearer
+
+    def legs_next(self, product, further, theirs, deps=()):
+        one = product(1, 2, ((theirs, 1), *((t, 0) for t in further)), bf16, deps)
+        return one, self.back(one, self.first)
+
+    def legs_own(self, product, nearer, theirs, last, deps=()):
+        return product(0, 1, ((theirs, 0), *((t, 0) for t in [*nearer, last])), bf16, deps)[0]
 
 
 def launch(
@@ -160,15 +175,18 @@
     return jax.ShapeDtypeStruct(shape, dtype)
 
 
-def product_kernel(terms, dims, *refs):
-    out_ref = refs[-1]
-    count, rows, width = out_ref.shape
+def product_kernel(terms, dims, pieces, *refs):
+    outs = refs[-pieces:]
+    each, rows, width = outs[0].shape
+    count = each * pieces
     total = dot(refs[0][...], refs[terms][...], dims)
     for t in range(1, terms):
         total += dot(refs[t][...], refs[terms + t][...], dims)
-    for ref in refs[2 * terms : -1]:
+    for ref in refs[2 * terms : -pieces]:
         total += ref[...].astype(f32).reshape(count * rows, width)
-    out_ref[...] = total.astype(out_ref.dtype).reshape(count, rows, width)
+    total = total.reshape(pieces, each, rows, width)
+    for n, out_ref in enumerate(outs):
+        out_ref[...] = total[n].astype(out_ref.dtype)
 
 
 def product_of(lefts, right, dims, span):
@@ -180,27 +198,29 @@
             return pl.BlockSpec((tile, left.shape[1]), lambda i: (i, at))
         return pl.BlockSpec((left.shape[1], tile), lambda i: (at, i))
 
-    def product(start, stop, addends, dtype, deps=()):
+    def product(start, stop, addends, dtype, deps=(), apart=False):
         count = stop - start
+        pieces = count if apart else 1
         assert start % count == 0 and all(at % count == 0 for _, at in addends)
 
         def columns(at):
             return pl.BlockSpec((count, span, tile), lambda i: (at // count, 0, i))
 
-        return launch(
-            functools.partial(product_kernel, len(lefts), dims),
+        values = launch(
+            functools.partial(product_kernel, len(lefts), dims, pieces),
             [*lefts, *[right] * len(lefts), *(value for value, _ in addends)],
             [pl.BlockSpec((count * span, a.shape[1]), lambda i: (start // count, 0)) for a in lefts]
             + [right_at(t, left) for t, left in enumerate(lefts)]
             + [columns(at) for _, at in addends],
-            [shape_of((count, span, D), dtype)],
-            [columns(0)],
+            [shape_of((count // pieces, span, D), dtype)] * pieces,
+            [pl.BlockSpec((count // pieces, span, tile), lambda i: (0, 0, i))] * pieces,
             grid=(D // tile,),
             deps=deps,
             mib=60,
             cost=(2 * count * span * D * depth, 2 * depth * (D + count * span) + 4 * count * span * D, 0),
             name="block_product",
-        )[0]
+        )
+        return values if apart else values[0]
 
     return product
 
@@ -312,7 +332,7 @@
     )
 
 
-def norm_back_kernel(steps, n_parts, *refs):
+def norm_back_kernel(depth, n_parts, *refs):
     grad_ref, x_ref, gain_ref, beside_ref = refs[:4]
     weights = refs[4 : 4 + n_parts]
     outs = refs[4 + n_parts :]
@@ -339,17 +359,14 @@
         branch = result.astype(bf16)
         outs[2][...] = branch
         parts = outs[3:]
-        group = parts[0].shape[2]
         full = dot(branch, weights[0][...], NT).astype(bf16)
-        for j in range(parts[0].shape[0]):
-            for g, part in enumerate(parts):
-                start = (j * len(parts) + g) * group
-                part[j] = full[:, start : start + group]
-
-
-def norm_back(grad, x, gain, beside, weight=None, n_sp=0, groups=0):
+        for place, g, j, columns in head_pieces(parts[0].shape[0], depth, len(parts)):
+            parts[g][j, :, columns] = full[:, place]
+
+
+def norm_back(grad, x, gain, beside, weight=None, depth=0, n_sp=0, groups=0):
     rows = x.shape[0]
-    tile = min(128, rows)
+    tile = min(256, rows)
     row = pl.BlockSpec((1, D), lambda i: (0, 0))
     block = pl.BlockSpec((tile, D), lambda i: (i, 0))
     outs = [shape_of((rows, D), f32), shape_of((8, D), f32)]
@@ -361,7 +378,7 @@
         outs += [shape_of((rows, D), bf16)] + [shape_of((n_sp, rows, group), bf16)] * groups
         out_specs += [block] + [pl.BlockSpec((n_sp, tile, group), lambda i: (0, i, 0))] * groups
     return launch(
-        functools.partial(norm_back_kernel, rows // tile, len(extra)),
+        functools.partial(norm_back_kernel, depth, len(extra)),
         [grad, x, gain, beside, *extra],
         [block, block, row, block, *specs],
         outs,
@@ -372,33 +389,42 @@
     )
 
 
-def middle_kernel(groups, n_sp, *refs):
+def head_pieces(n_sp, depth, groups):
+    group = D // n_sp // groups
+    n_z = D // n_sp // depth
+    for z in range(n_z):
+        for s in range(n_sp):
+            j, rest = divmod((z * n_sp + s) * depth, groups * group)
+            g, column = divmod(rest, group)
+            yield slice((s * n_z + z) * depth, (s * n_z + z + 1) * depth), g, j, slice(column, column + depth)
+
+
+def middle_kernel(groups, n_sp, depth, *refs):
     parts, (out_w, x_ref, gain_ref, shift_ref) = refs[:groups], refs[groups : groups + 4]
-    middle_ref, normed_ref, attended_ref = refs[groups + 4 :]
-    group = parts[0].shape[2]
-    for j in range(n_sp):
-        for g in range(groups):
-            start = (j * groups + g) * group
-            attended_ref[:, start : start + group] = parts[g][j]
+    middle_ref, normed_ref, again_ref, attended_ref = refs[groups + 4 :]
+    for to, g, j, columns in head_pieces(n_sp, depth, groups):
+        attended_ref[:, to] = parts[g][j, :, columns]
     values = x_ref[...].astype(f32) + dot(attended_ref[...], out_w[...], NN)
     middle_ref[...] = values
     center = values - jnp.mean(values, axis=-1, keepdims=True)
     spread = jnp.mean(center * center, axis=-1, keepdims=True)
-    normed_ref[...] = (center * lax.rsqrt(spread + epsilon) * gain_ref[...] + shift_ref[...]).astype(bf16)
-
-
-def middle_of(parts, out_w, x, gain, shift, deps=()):
+    normed = (center * lax.rsqrt(spread + epsilon) * gain_ref[...] + shift_ref[...]).astype(bf16)
+    normed_ref[...] = normed
+    again_ref[...] = normed
+
+
+def middle_of(parts, out_w, depth, x, gain, shift, deps=()):
     n_sp, rows, group = parts[0].shape
-    tile = min(128, rows)
+    tile = min(256, rows)
     row = pl.BlockSpec((1, D), lambda i: (0, 0))
     block = pl.BlockSpec((tile, D), lambda i: (i, 0))
     return launch(
-        functools.partial(middle_kernel, len(parts), n_sp),
+        functools.partial(middle_kernel, len(parts), n_sp, depth),
         [*parts, out_w, x, gain, shift],
         [pl.BlockSpec((n_sp, tile, group), lambda i: (0, i, 0))] * len(parts)
         + [pl.BlockSpec((D, D), lambda i: (0, 0)), block, row, row],
-        [shape_of((rows, D), f32), shape_of((rows, D), bf16), shape_of((rows, D), bf16)],
-        [block] * 3,
+        [shape_of((rows, D), f32)] + [shape_of((rows, D), bf16)] * 3,
+        [block] * 4,
         grid=(rows // tile,),
         deps=deps,
         cost=(2 * rows * D * D, 2 * D * D + rows * D * 12, rows),
@@ -455,8 +481,7 @@
     )(table, normed, weight, bias, *tables)
 
 
-def attend_kernel(heads, bq, bk, q_ref, k_ref, v_ref, *rest):
-    o_ref, lse_ref, qm, vt, acc, m_s, l_s = rest[-7:]
+def attend_kernel(heads, bq, bk, q_ref, k_ref, v_ref, o_ref, lse_ref, qm, vt, acc, m_s, l_s):
     i = pl.program_id(0)
     length, width = k_ref.shape
     lane = lax.broadcasted_iota(jnp.int32, (1, width), 1) // HEAD
@@ -509,39 +534,34 @@
 
 
 def attend(q, k, v, deps=()):
-    deps = jax.tree.leaves(deps)
     length, width = q.shape
     heads = width // HEAD
-    bq = bk = min(512, length)
+    bq, bk = min(1024, length), min(512, length)
     full = pl.BlockSpec((length, width), lambda i: (0, 0))
-    return pl.pallas_call(
+    return launch(
         functools.partial(attend_kernel, heads, bq, bk),
+        [q, k, v],
+        [pl.BlockSpec((bq, width), lambda i: (i, 0)), full, full],
+        [shape_of((length, width), bf16), shape_of((8, length), f32)],
+        [pl.BlockSpec((bq, width), lambda i: (i, 0)), pl.BlockSpec((8, bq), lambda i: (0, i))],
         grid=(length // bq,),
-        in_specs=[pl.BlockSpec((bq, width), lambda i: (i, 0)), full, full]
-        + [pl.BlockSpec(memory_space=pl.ANY)] * len(deps),
-        out_specs=[pl.BlockSpec((bq, width), lambda i: (i, 0)), pl.BlockSpec((8, bq), lambda i: (0, i))],
-        out_shape=[jax.ShapeDtypeStruct((length, width), bf16), jax.ShapeDtypeStruct((8, length), f32)],
-        scratch_shapes=[
+        scratch=[
             pltpu.VMEM((heads, bq, width), bf16),
             pltpu.VMEM((width, length), bf16),
             pltpu.VMEM((width, bq), f32),
             pltpu.VMEM((8, bq), f32),
             pltpu.VMEM((8, bq), f32),
         ],
-        compiler_params=params(),
-        cost_estimate=pl.CostEstimate(
-            flops=8 * length * length * width,
-            bytes_accessed=length * width * 8,
-            transcendentals=length * length * heads // 2,
-        ),
+        deps=deps,
+        cost=(8 * length * length * width, length * width * 8, length * length * heads // 2),
         name="attend",
-    )(q, k, v, *deps)
+    )
 
 
 def attend_back_kernel(
-    heads, bq, bk, place_ref, q_ref, k_ref, v_ref, do_ref, o_ref, lse_ref, cos_ref, up_ref, down_ref, *rest
+    heads, bq, bk, place_ref, q_ref, k_ref, v_ref, do_ref, o_ref, lse_ref, cos_ref, up_ref, down_ref, out_ref,
+    dq_acc, dk_acc, dv_acc, delta,
 ):
-    out_ref, dq_acc, dk_acc, dv_acc, delta = rest[-5:]
     j = pl.program_id(0)
     length, width = q_ref.shape
     lane = lax.broadcasted_iota(jnp.int32, (1, width), 1) // HEAD
@@ -611,37 +631,30 @@
 
 
 def attend_back(place, q, k, v, do, o, lse, tables, span, deps=()):
-    deps = jax.tree.leaves(deps)
     length, width = q.shape
     heads = width // HEAD
     bq = min(512, length)
     bk = span
     full = pl.BlockSpec((length, width), lambda i, t: (0, 0))
     block = pl.BlockSpec((bk, width), lambda i, t: (i, 0))
-    return pl.pallas_call(
+    return launch(
         functools.partial(attend_back_kernel, heads, bq, bk),
-        grid_spec=pltpu.PrefetchScalarGridSpec(
-            num_scalar_prefetch=1,
-            grid=(length // bk,),
-            in_specs=[full] * 5 + [pl.BlockSpec((8, length), lambda i, t: (0, 0))] + [block] * 3
-            + [pl.BlockSpec(memory_space=pl.ANY)] * len(deps),
-            out_specs=pl.BlockSpec((bk, 3 * width), lambda i, t: (t[i], 0)),
-            scratch_shapes=[
-                pltpu.VMEM((width, length), f32),
-                pltpu.VMEM((bk, width), f32),
-                pltpu.VMEM((bk, width), f32),
-                pltpu.VMEM((8, length), f32),
-            ],
-        ),
-        out_shape=jax.ShapeDtypeStruct((length, 3 * width), bf16),
-        compiler_params=params(60),
-        cost_estimate=pl.CostEstimate(
-            flops=12 * length * length * width,
-            bytes_accessed=length * width * 16,
-            transcendentals=length * length * heads // 2,
-        ),
+        [place, q, k, v, do, o, lse, *tables],
+        [full] * 5 + [pl.BlockSpec((8, length), lambda i, t: (0, 0))] + [block] * 3,
+        [shape_of((length, 3 * width), bf16)],
+        [pl.BlockSpec((bk, 3 * width), lambda i, t: (t[i], 0))],
+        grid=(length // bk,),
+        prefetch=1,
+        scratch=[
+            pltpu.VMEM((width, length), f32),
+            pltpu.VMEM((bk, width), f32),
+            pltpu.VMEM((bk, width), f32),
+            pltpu.VMEM((8, length), f32),
+        ],
+        deps=deps,
+        cost=(12 * length * length * width, length * width * 16, length * length * heads // 2),
         name="attend_back",
-    )(place, q, k, v, do, o, lse, *tables, *deps)
+    )[0]
 
 
 def feed_kernel(ff, x0, x1, c0, c1, wgu_ref, wd_ref, *rest):
@@ -739,6 +752,14 @@
     return lax.all_to_all(value, "sp", split_axis=0, concat_axis=0, tiled=True)
 
 
+def in_line(blocks, mine):
+    count, rows = len(blocks), blocks[0].shape[0]
+    total = jnp.zeros((count * rows, blocks[0].shape[1]), blocks[0].dtype)
+    for step, block in enumerate(blocks):
+        total = lax.dynamic_update_slice(total, block, (lax.rem(mine - step + count, count) * rows, 0))
+    return total
+
+
 def per_device(
     tokens, cotangent, first_gain, first_shift, joint_weight, joint_bias, out_weight, second_gain, second_shift,
     gate_weight, up_weight, down_weight,
@@ -776,25 +797,26 @@
     bias = lax.dynamic_index_in_dim(bias_all, me, axis=1, keepdims=False)
     bias = bias.reshape(3, groups, group).transpose(1, 0, 2).reshape(1, 3 * width)
 
-    joint_blocks = [swap_sp(cut_joint(joint_weight, n_sp, groups)).reshape(n_sp * depth, 3 * width)]
+    ring = [(i, (i + 1) % n_z) for i in range(n_z)]
+    joint_block = swap_sp(cut_joint(joint_weight, n_sp, groups)).reshape(n_sp * depth, 3 * width)
+    out_blocks = [out_weight]
     for _ in range(n_z - 1):
-        joint_blocks.append(lax.ppermute(joint_blocks[-1], "fsdp", [(i, (i + 1) % n_z) for i in range(n_z)]))
-    joint_mine = jnp.zeros((D, 3 * width), bf16)
-    for step, block in enumerate(joint_blocks):
-        at = lax.rem(my_z - step + n_z, n_z) * (n_sp * depth)
-        joint_mine = lax.dynamic_update_slice(joint_mine, block, (at, 0))
+        out_blocks.append(lax.ppermute(out_blocks[-1], "fsdp", ring))
+    out_rows = in_line(out_blocks, my_z)
+    joint_blocks = [held(joint_block, out_blocks[1:])]
+    for _ in range(n_z - 1):
+        joint_blocks.append(lax.ppermute(joint_blocks[-1], "fsdp", ring))
+    joint_mine = in_line(joint_blocks, my_z)
 
     gate_up_cols = cut_feed(gate_weight, up_weight, n_sp, n_z, ff_pad, ())
     down_rows = jnp.pad(down_weight, ((0, ff_pad - ff_rows), (0, 0)))
-    down = lax.all_gather(down_rows, "fsdp", axis=0, tiled=True)
-
     x = tokens.reshape(span, D)
     normed = None
 
     def norm_next(normed, block, t, deps=()):
         return norm_block(block, gain_one, shift_one, t, n_sp, normed, deps)
 
-    partner, one, twos = plane.gather_first(held(x, (joint_blocks[0], small_all)))
+    partner, one, twos = plane.gather_first(x)
     normed = norm_next(None, x, 0)
     normed = norm_next(normed, partner, half)
     one = held(one, (normed, joint_blocks[1:3], gate_up_cols))
@@ -805,7 +827,7 @@
     normed = norm_next(normed, one_other, half + 1)
     for n, two in enumerate(two_others):
         normed = norm_next(normed, two, half + 2 + 2 * n)
-    threes = [held(three, (normed, joint_blocks[3:])) if n == 0 else three for n, three in enumerate(threes)]
+    threes = [held(three, (normed, joint_mine, bias)) if n == 0 else three for n, three in enumerate(threes)]
     for n, three in enumerate(threes):
         normed = norm_next(normed, three, 3 + 2 * n)
     for n, three in enumerate(plane.gather_third(threes)):
@@ -813,12 +835,13 @@
     tables = rotary_columns(length, group)
     heads = joint_projection(order, normed, joint_mine, bias, tables, span, groups)
 
-    out_full = lax.all_gather(held(out_weight, threes), ("fsdp", "sp"), axis=0, tiled=True)
-    ring = [(i, (i + 1) % n_z) for i in range(n_z)]
+    out_full = lax.all_gather(held(out_rows, threes), "sp", axis=0, tiled=True)
+    down = lax.all_gather(held(down_rows, threes), "fsdp", axis=0, tiled=True)
     gate_up_blocks = [held(swap_sp(held(gate_up_cols, threes)).reshape(n_sp * depth, 2 * ff), heads[0])]
     gate_up_blocks.append(lax.ppermute(gate_up_blocks[0], "fsdp", ring))
     cot = cotangent.reshape(span, D)
-    cot_partner, cot_one, cot_twos = plane.gather_first(held(cot, gate_up_blocks[0]))
+    cot_held = held(cot, gate_up_blocks[0])
+    cot_partner, cot_one, cot_twos = plane.gather_first(cot_held)
     results = [attend(*heads[:3])]
     cot_one = held(cot_one, results[0][1])
     gate_up_blocks[1] = held(gate_up_blocks[1], results[0][1])
@@ -827,7 +850,6 @@
     for g in range(1, groups):
         results.append(attend(*heads[3 * g : 3 * g + 3], (cot_partner, cot_one, cot_twos, gate_up_blocks[1])))
     cot_threes = [held(c, results[-1][1]) for c in cot_threes]
-    gate_up_blocks[2] = held(gate_up_blocks[2], results[-1][1])
     for _ in range(3, n_z):
         gate_up_blocks.append(lax.ppermute(gate_up_blocks[-1], "fsdp", ring))
     cot_three_others = plane.gather_third(cot_threes)
@@ -836,73 +858,83 @@
         cot_blocks += pieces
     for pieces in zip(cot_two_others, cot_three_others):
         cot_partners += pieces
-    gate_up = jnp.zeros((D, 2 * ff), bf16)
-    for step, block in enumerate(gate_up_blocks):
-        at = lax.rem(my_z - step + n_z, n_z) * (n_sp * depth)
-        gate_up = lax.dynamic_update_slice(gate_up, block, (at, 0))
+    gate_up = in_line(gate_up_blocks, my_z)
     attended = [swap_sp(o).reshape(n_sp, span, group) for o, _ in results]
-    middle, normed_two, attended_all = middle_of(attended, out_full, x, gain_two, shift_two, gate_up_blocks[:3])
+    middle, normed_two, normed_again, attended_all = middle_of(
+        attended, out_full, depth, x, gain_two, shift_two, (gate_up_blocks[:3], down)
+    )
 
     feed = None
 
     def feed_next(feed, pair, t, deps=()):
         return feed_block(pair, (cot_blocks[t], cot_partners[t]), gate_up, down, t, half, feed, deps)
 
-    partner, one, twos = plane.gather_first(normed_two)
+    partner = plane.send(normed_two, plane.core)
+    one = plane.send(normed_two, plane.first)
     feed = feed_next(None, (normed_two, partner), 0, (cot_blocks, cot_partners))
-    one = held(one, feed[0])
-    one_other, two_others, threes = plane.gather_second(one, twos)
-    feed = feed_next(feed, (one, one_other), 1)
-    for n, two in enumerate(twos):
-        feed = feed_next(feed, (two, two_others[n]), 2 + 2 * n)
-        three = held(threes[n], feed[0]) if n == len(twos) - 1 else threes[n]
+    one_other = plane.send(one, plane.core)
+    again = held(normed_again, one)
+    for n, perm in enumerate(plane.later):
+        two = plane.send(again, perm)
+        if n == 0:
+            feed = feed_next(feed, (one, one_other), 1)
+        one = held(one, (two, one_other, feed[0]))
+        three = plane.send(one, perm)
+        feed = feed_next(feed, (two, plane.send(two, plane.core)), 2 + 2 * n)
+        three = held(three, feed[0])
         feed = feed_next(feed, (three, plane.send(three, plane.core)), 3 + 2 * n)
     hidden, gate_up_grad, two_all, cot_all = feed
 
     two_product = product_of([gate_up_grad], gate_up, NT, span)
     out_product = product_of([hidden], down, NN, span)
-    two_got = plane.reduce_far(two_product)
-    two_theirs = plane.reduce_near(two_product)
-    gate_up_sum = dot(two_all, gate_up_grad, TN).astype(bf16)
-    down_sum = dot(hidden, cot_all, TN).astype(bf16)
-    gate_up_part = lax.psum_scatter(gate_up_sum, "fsdp", scatter_dimension=0, tiled=True)
-    down_part = lax.psum_scatter(down_sum, "fsdp", scatter_dimension=0, tiled=True)
-    two_last = plane.reduce_next(two_product, two_got, two_theirs, (gate_up_sum, down_sum))
-    two_grad = plane.reduce_own(two_product, two_got, two_theirs, two_last)
+    two_far, two_theirs = plane.reduce_sums(two_product, (), True)
+    further, nearer = plane.legs(two_far)
+    down_sum = dot(hidden, held(cot_all, two_far), TN).astype(bf16)
+    two_one, two_last = plane.legs_next(two_product, further, two_theirs, down_sum)
+    gate_up_sum = dot(held(two_all, two_one), gate_up_grad, TN).astype(bf16)
+    down_part = lax.psum_scatter(held(down_sum, two_one), "fsdp", scatter_dimension=0, tiled=True)
+    two_grad = plane.legs_own(two_product, nearer, two_theirs, two_last, gate_up_sum)
+    gate_up_part = lax.psum_scatter(held(gate_up_sum, two_grad), "fsdp", scatter_dimension=0, tiled=True)
     middle_grad, two_sums, branch_grad, *parts = norm_back(
-        two_grad, middle, gain_two, cotangent.reshape(span, D), out_full, n_sp, groups
+        two_grad, middle, gain_two, cot, out_full, depth, n_sp, groups
     )
     dos = [swap_sp(part).reshape(n_sp * span, group) for part in parts]
-    out_sum = dot(attended_all, branch_grad, TN).astype(bf16).reshape(n_z, n_sp, depth, D)
+    out_sum = dot(attended_all, branch_grad, TN).astype(bf16).reshape(n_sp, n_z * depth, D)
 
     def out_weight_part(start, stop, addends, dtype, deps=()):
-        parts = [lax.dynamic_index_in_dim(out_sum, order[b], 1, False).reshape(n_z * depth, D) for b in range(start, stop)]
+        parts = [lax.dynamic_index_in_dim(out_sum, order[b], 0, False) for b in range(start, stop)]
         total = jnp.stack(parts).astype(f32)
         for addend, at in addends:
             total += addend[at : at + stop - start].astype(f32)
         return total.astype(dtype)
 
-    rows = attend_back(place, *heads[:3], dos[0], *results[0], tables, span, out_sum)
+    out_sums, out_theirs = plane.reduce_sums(out_product, branch_grad)
+    out_got = plane.reduce_leg(out_sums)
+    rows = attend_back(place, *heads[:3], dos[0], *results[0], tables, span, out_sums)
     joint_rows = [rows]
     joint_sums = [dot(normed, rows, TN).astype(bf16)]
     joint_parts = [lax.psum_scatter(joint_sums[0], "fsdp", scatter_dimension=0, tiled=True)]
-    out_got = plane.reduce_far(out_product, branch_grad)
-    out_theirs = plane.reduce_near(out_product, branch_grad)
-    weight_got = plane.reduce_far(out_weight_part)
-    weight_theirs = plane.reduce_near(out_weight_part)
+    out_one, out_last = plane.reduce_next(out_product, out_got, out_theirs)
+    weight_sums, weight_theirs = plane.reduce_sums(out_weight_part)
+    weight_got = plane.reduce_leg(weight_sums)
     gate_up_own = swap_sp(gate_up_part)
     for g in range(1, groups):
-        deps = (joint_sums, out_got, out_theirs, weight_got, weight_theirs, gate_up_own, down_part)
+        deps = (joint_sums, out_one, weight_sums, weight_theirs)
         rows = attend_back(place, *heads[3 * g : 3 * g + 3], dos[g], *results[g], tables, span, deps)
         joint_rows.append(rows)
-        joint_sums.append(dot(normed, rows, TN).astype(bf16))
+    _, weight_last = plane.reduce_next(out_weight_part, weight_got, weight_theirs)
+
+    normed_product = product_of(joint_rows, joint_mine, NT, span)
+    normed_far, normed_theirs = plane.reduce_sums(normed_product, (out_last, weight_got, joint_parts, down_part, gate_up_own), True)
+    further, nearer = plane.legs(normed_far)
+    last_normed = held(normed, (normed_far, joint_sums))
+    for g in range(1, groups):
+        joint_sums.append(dot(last_normed, joint_rows[g], TN).astype(bf16))
         joint_parts.append(lax.psum_scatter(joint_sums[g], "fsdp", scatter_dimension=0, tiled=True))
-    out_last = plane.reduce_next(out_product, out_got, out_theirs)
-    weight_last = plane.reduce_next(out_weight_part, weight_got, weight_theirs)
-
-    normed_product = product_of(joint_rows, joint_mine, NT, span)
-    normed_got = plane.reduce_far(normed_product, (out_last, weight_last, gate_up_own))
-    normed_theirs = plane.reduce_near(normed_product)
+    joint_own = [swap_sp(j).reshape(n_sp, depth, 3 * group) for j in joint_parts]
+    normed_one, normed_last = plane.legs_next(
+        normed_product, further, normed_theirs, (joint_sums, joint_own[:-1])
+    )
     output = (middle + plane.reduce_own(out_product, out_got, out_theirs, out_last, f32)).astype(bf16)
     out_own = plane.reduce_own(out_weight_part, weight_got, weight_theirs, weight_last)
     out_grad = lax.psum_scatter(held(out_own, joint_parts), "fsdp", scatter_dimension=0, tiled=True).astype(f32)
@@ -911,10 +943,8 @@
     bias_sum = jnp.stack([jnp.sum(r.astype(f32), axis=0).reshape(3, group) for r in joint_rows], 1)
     bias_sum = bias_sum.reshape(3, 1, width)
     bias_sum = lax.dynamic_update_slice(jnp.zeros((3, n_sp, width), f32), bias_sum, (0, me, 0))
-    joint_own = [swap_sp(j).reshape(n_sp, depth, 3 * group) for j in joint_parts]
-    fill = (joint_sums, output, gate_grad, up_grad, bias_sum, joint_own[:-1])
-    normed_last = plane.reduce_next(normed_product, normed_got, normed_theirs, fill)
-    normed_grad = plane.reduce_own(normed_product, normed_got, normed_theirs, normed_last)
+    fill = (output, out_own, gate_grad, up_grad, bias_sum)
+    normed_grad = plane.legs_own(normed_product, nearer, normed_theirs, normed_last, fill)
     tokens_grad, one_sums = norm_back(normed_grad, x, gain_one, middle_grad)
     tokens_grad = tokens_grad.reshape(tokens.shape)
 

time: 1010 us -> 970 us (0.960)
  waiting for transfers between devices: 192 us -> 171 us
    pallas_call x4 -> x0, Pallas kernels: 218 us -> none  [the longest x2 126 us: attend_back(): pl.pallas_call(functools.partial(attend_back_kernel, heads, bq, bk), grid...]
    pallas_call x48 -> x60, Pallas kernels: 280 us -> 488 us  [launch(): pl.pallas_call(body, grid_spec=pltpu.PrefetchScalarGridSpec(num_scalar_pr...]
    ppermute x29, waiting for transfers between devices: 17.5 us -> 45.3 us  [send(): return lax.ppermute(value, 'sp', perm)]
    ppermute x8 -> x10, waiting for transfers between devices: 55.3 us -> 34.5 us  [back(): return lax.ppermute(value, 'sp', [(b, a) for a, b in perm])]
    ppermute x1, waiting for transfers between devices: 19.1 us -> 0.01 us  [per_device(): gate_up_blocks.append(lax.ppermute(gate_up_blocks[1], 'fsdp', ring))]
    ppermute x1, waiting for transfers between devices: 18.3 us -> 6.44 us  [per_device(): gate_up_blocks.append(lax.ppermute(gate_up_blocks[-1], 'fsdp', ring))]
    ppermute x3 -> x6, waiting for transfers between devices: 35 us -> 44.1 us  [the longest x3 27.9 us: per_device(): joint_blocks.append(lax.ppermute(joint_blocks[-1], 'fsdp', ring))]
    unnamed x78 -> x91, local copies, waits for them, and re-layouts: 24.2 us -> 25.9 us
  transfers between devices with their start and end apart: 61 -> 66, of which waited for: 19 -> 22; matrix products, arithmetic and copies ran while one was open for 15% -> 15% of each run, Pallas kernels for 48% -> 47%
where the time goes in v3:
time: 970 us; the launch traced here: 960 us
  Pallas kernels  509 us (52%)
  waiting for transfers between devices  171 us (18%)
  matrix products  89.9 us (9%)
  starting transfers between devices  78.4 us (8%)
  local copies, waits for them, and re-layouts  56.6 us (6%)
  between operations  30.2 us (3%)
  other arithmetic  23.8 us (2%)
    pallas_call x60, Pallas kernels, launch(): pl.pallas_call(body, grid_spec=pltpu.PrefetchScalarGridSpec(num_scalar_pr...  488 us
    dot_general x5, matrix products, dot(): return lax.dot_general(a, b, dims, preferred_element_type=f32)  89.9 us
    ppermute x29, waiting for transfers between devices, send(): return lax.ppermute(value, 'sp', perm)  45.3 us
    ppermute x10, waiting for transfers between devices, back(): return lax.ppermute(value, 'sp', [(b, a) for a, b in perm])  34.5 us
    all_to_all x9, starting transfers between devices, swap_sp(): return lax.all_to_all(value, 'sp', split_axis=0, concat_axis=0, tiled=True)  33.8 us
    ppermute x3, waiting for transfers between devices, per_device(): joint_blocks.append(lax.ppermute(joint_blocks[-1], 'fsdp', ring))  27.9 us
    all_to_all x9, waiting for transfers between devices, swap_sp(): return lax.all_to_all(value, 'sp', split_axis=0, concat_axis=0, tiled=True)  26.2 us
    unnamed x91, local copies, waits for them, and re-layouts  25.9 us
  transfers between devices with their start and end apart: 66, of which 22 were waited for; matrix products, arithmetic and copies ran while one was open for 15% of the time, Pallas kernels for 47%

profile of v3, /device:TPU:0, one launch (start us, length us, event | category | flops | bytes accessed | tf_op | source)
XLA Modules:
  0.0 959.6 jit_solution(983024216228268256)
XLA Ops:
  37.0 19.0 %collective-permute-done.5.refs_2_ = bf16[512,768]{1,0:T(8,128)(2,1)} collective-permute-done((bf16[512,768]{1,0:T(8,128)(2,1)}, bf16[512,768]{1,0:T(8,128)(2,1)}, u32[]{:S(2)}, u32[]{:S(2)}) %collective-permute-start.5) | collective-permute-done | bytes 786464 | tf_op jit(solution)/shard_map/ppermute | solution.py:808
  137.8 21.3 %joint_projection.1 = (bf16[4096,128]{1,0:T(8,128)(2,1)}, bf16[4096,128]{1,0:T(8,128)(2,1)}, bf16[4096,128]{1,0:T(8,128)(2,1)}, bf16[4096,128]{1,0:T(8,128)(2,1)...) custom-call(s32[8]{0:T(128)} %get-tuple-element.113.table_ref, bf16[4096,2048]{1,0:T(8,128)(2,1)} %first_norm.15.x_ref.refs_0_, ...), custom_call_target="tpu_custom_call" | custom-call | flops 12884901888 | bytes 23068672 | tf_op jit(solution)/shard_map/joint_projection/pallas_call | solution.py:460
  163.8 42.2 %attend.2 = (bf16[4096,128]{1,0:T(8,128)(2,1)}, f32[8,4096]{1,0:T(8,128)}) custom-call(bf16[4096,128]{1,0:T(8,128)(2,1)} %get-tuple-element.55.refs_0_.refs_1_, bf16[4096,128]{1,0:T(8,128)(2,1)} %get-tuple-element.56.refs_1_.refs_2_, bf16[4096,128]{1,0:T(8,128)(2,1)} %get-tuple-element.57.refs_2_.refs_3_), custom_call_target="tpu_custom_call" | custom-call | flops 17179869184 | bytes 4194304 | tf_op jit(solution)/shard_map/attend/pallas_call | solution.py:143
  218.8 42.2 %attend.3 = (bf16[4096,128]{1,0:T(8,128)(2,1)}, f32[8,4096]{1,0:T(8,128)}) custom-call(bf16[4096,128]{1,0:T(8,128)(2,1)} %get-tuple-element.59.refs_0_.refs_1_, bf16[4096,128]{1,0:T(8,128)(2,1)} %get-tuple-element.60.refs_1_.refs_2_, bf16[4096,128]{1,0:T(8,128)(2,1)} %get-tuple-element.61.refs_2_.refs_3_, ...), custom_call_target="tpu_custom_call" | custom-call | flops 17179869184 | bytes 4194304 | tf_op jit(solution)/shard_map/attend/pallas_call | solution.py:143
  269.1 12.3 %all-to-all-done.4.refs_1_ = bf16[8,512,128]{2,1,0:T(8,128)(2,1)S(1)} async-done(((bf16[8,512,128]{2,1,0:T(8,128)(2,1)}), bf16[8,512,128]{2,1,0:T(8,128)(2,1)S(1)}, u32[]{:S(2)}, u32[]{:S(2)}) %all-to-all-start.4) | async-done | bytes 1048608 | tf_op jit(solution)/shard_map/all_to_all | solution.py:752
  282.9 12.4 %middle.1 = (f32[512,2048]{1,0:T(8,128)}, bf16[512,2048]{1,0:T(8,128)(2,1)}, bf16[512,2048]{1,0:T(8,128)(2,1)}, bf16[512,2048]{1,0:T(8,128)(2,1)}) custom-call(bf16[8,512,128]{2,1,0:T(8,128)(2,1)} %all-to-all-done.2.refs_0_, bf16[8,512,128]{2,1,0:T(8,128)(2,1)} %copy-done.20, bf16[2048,2048]{1,0:T(8,128)(2,1)} %all-gather.3.cloned.1.call-done.refs_2_.refs_4_, ...), custom_call_target="tpu_custom_call" | custom-call | flops 4294967296 | bytes 20971520 | tf_op jit(solution)/shard_map/middle/pallas_call | solution.py:143
  295.9 14.3 %collective-permute-done.24.refs_0_ = bf16[512,2048]{1,0:T(8,128)(2,1)} collective-permute-done((bf16[512,2048]{1,0:T(8,128)(2,1)}, bf16[512,2048]{1,0:T(8,128)(2,1)}, u32[]{:S(2)}, u32[]{:S(2)}) %collective-permute-start.24) | collective-permute-done | bytes 2097184 | tf_op jit(solution)/shard_map/ppermute | solution.py:76
  310.2 14.7 %collective-permute-done.18.refs_1_.refs_0_ = bf16[512,2048]{1,0:T(8,128)(2,1)S(1)} collective-permute-done((bf16[512,2048]{1,0:T(8,128)(2,1)}, bf16[512,2048]{1,0:T(8,128)(2,1)S(1)}, u32[]{:S(2)}, u32[]{:S(2)}) %collective-permute-start.18) | collective-permute-done | bytes 2097184 | tf_op jit(solution)/shard_map/ppermute | solution.py:76
  343.1 18.5 %feed_forward.4 = (bf16[4096,768]{1,0:T(8,128)(2,1)}, bf16[4096,1536]{1,0:T(8,128)(2,1)}, bf16[4096,2048]{1,0:T(8,128)(2,1)}, bf16[4096,2048]{1,0:T(8,128)(2,1)}) custom-call(bf16[512,2048]{1,0:T(8,128)(2,1)} %get-tuple-element.65.refs_0_, bf16[512,2048]{1,0:T(8,128)(2,1)} %collective-permute-done.23.refs_1_, bf16[512,2048]{1,0:T(8,128)(2,1)} %bitcast.68, ...), custom_call_target="tpu_custom_call" | custom-call | flops 9663676416 | bytes 26214400 | tf_op jit(solution)/shard_map/feed_forward/pallas_call | solution.py:143
  362.2 18.2 %feed_forward.5 = (bf16[4096,768]{1,0:T(8,128)(2,1)}, bf16[4096,1536]{1,0:T(8,128)(2,1)}, bf16[4096,2048]{1,0:T(8,128)(2,1)}, bf16[4096,2048]{1,0:T(8,128)(2,1)}) custom-call(bf16[512,2048]{1,0:T(8,128)(2,1)} %copy-done.7, ...), custom_call_target="tpu_custom_call", output_to_operand_aliasing={{0}: (6, {}), {1}: (7, {}), {2}: (8, {}), {3}: (9, {})} | custom-call | flops 9663676416 | bytes 26214400 | tf_op jit(solution)/shard_map/feed_forward/pallas_call | solution.py:143
  381.7 18.0 %feed_forward.6 = (bf16[4096,768]{1,0:T(8,128)(2,1)}, bf16[4096,1536]{1,0:T(8,128)(2,1)}, bf16[4096,2048]{1,0:T(8,128)(2,1)}, bf16[4096,2048]{1,0:T(8,128)(2,1)}) custom-call(bf16[512,2048]{1,0:T(8,128)(2,1)} %copy-done.14, ...), custom_call_target="tpu_custom_call", output_to_operand_aliasing={{0}: (6, {}), {1}: (7, {}), {2}: (8, {}), {3}: (9, {})} | custom-call | flops 9663676416 | bytes 26214400 | tf_op jit(solution)/shard_map/feed_forward/pallas_call | solution.py:143
  412.5 18.1 %feed_forward.7 = (bf16[4096,768]{1,0:T(8,128)(2,1)}, bf16[4096,1536]{1,0:T(8,128)(2,1)}, bf16[4096,2048]{1,0:T(8,128)(2,1)}, bf16[4096,2048]{1,0:T(8,128)(2,1)}) custom-call(bf16[512,2048]{1,0:T(8,128)(2,1)} %held.35.refs_0_, bf16[512,2048]{1,0:T(8,128)(2,1)} %copy-done.27, ...), custom_call_target="tpu_custom_call", output_to_operand_aliasing={{0}: (6, {}), {1}: (7, {}), {2}: (8, {}), {3}: (9, {})} | custom-call | flops 9663676416 | bytes 26214400 | tf_op jit(solution)/shard_map/feed_forward/pallas_call | solution.py:143
  441.5 10.9 %block_product.16.refs_3_ = bf16[2,512,2048]{2,1,0:T(8,128)(2,1)} custom-call(bf16[4096,1536]{1,0:T(8,128)(2,1)} %get-tuple-element.81.refs_0_, bf16[2048,1536]{1,0:T(8,128)(2,1)} %constant_dynamic-update-slice_fusion.refs_4_.refs_1_, bf16[2,512,2048]{2,1,0:T(8,128)(2,1)} %block_product.15.refs_2_), custom_call_target="tpu_custom_call" | custom-call | flops 6442450944 | bytes 17825792 | tf_op jit(solution)/shard_map/block_product/pallas_call | solution.py:143
  452.8 11.0 %block_product.17 = (bf16[1,512,2048]{2,1,0:T(8,128)(2,1)}, bf16[1,512,2048]{2,1,0:T(8,128)(2,1)}) custom-call(bf16[4096,1536]{1,0:T(8,128)(2,1)} %get-tuple-element.81.refs_0_, bf16[2048,1536]{1,0:T(8,128)(2,1)} %constant_dynamic-update-slice_fusion.refs_4_.refs_1_, bf16[2,512,2048]{2,1,0:T(8,128)(2,1)} %collective-permute-done.31.refs_2_, ...), custom_call_target="tpu_custom_call" | custom-call | flops 6442450944 | bytes 17825792 | tf_op jit(solution)/shard_map/block_product/pallas_call | solution.py:143
  465.1 19.9 %convolution_convert_fusion.2.refs_4_.refs_0_ = bf16[768,2048]{1,0:T(8,128)(2,1)} fusion(bf16[4096,768]{1,0:T(8,128)(2,1)} %get-tuple-element.80.refs_0_, bf16[4096,2048]{1,0:T(8,128)(2,1)} %held.37), kind=kOutput, calls=%fused_computation.7 | convolution fusion | flops 12886474752 | bytes 26214400 | tf_op jit(solution)/shard_map/dot_general | solution.py:28
  502.3 34.0 %convolution_convert_fusion.1.refs_5_.refs_0_ = bf16[2048,1536]{1,0:T(8,128)(2,1)} fusion(bf16[4096,2048]{1,0:T(8,128)(2,1)} %held.38, bf16[4096,1536]{1,0:T(8,128)(2,1)} %get-tuple-element.81.refs_0_), kind=kOutput, calls=%fused_computation.1 | convolution fusion | flops 25772949504 | bytes 35651584 | tf_op jit(solution)/shard_map/dot_general | solution.py:28
  536.3 11.5 %collective-permute-done.34.refs_4_ = bf16[1,512,2048]{2,1,0:T(8,128)(2,1)S(1)} collective-permute-done((bf16[1,512,2048]{2,1,0:T(8,128)(2,1)}, bf16[1,512,2048]{2,1,0:T(8,128)(2,1)S(1)}, u32[]{:S(2)}, u32[]{:S(2)}) %collective-permute-start.34) | collective-permute-done | bytes 2097184 | tf_op jit(solution)/shard_map/ppermute | solution.py:80
  558.2 16.8 %norm_back.2 = (f32[512,2048]{1,0:T(8,128)}, f32[8,2048]{1,0:T(8,128)}, bf16[512,2048]{1,0:T(8,128)(2,1)}, bf16[8,512,128]{2,1,0:T(8,128)(2,1)}, bf16[8,512,128]{2,1,0:T(8,128)(2,1)}) custom-call(bf16[512,2048]{1,0:T(8,128)(2,1)} %bitcast.60, f32[512,2048]{1,0:T(8,128)} %get-tuple-element.64.refs_1_, f32[1,2048]{1,0:T(1,128)} %reshape.134.refs_4_.refs_2_, ...), custom_call_target="tpu_custom_call" | custom-call | flops 4315938816 | bytes 25165824 | tf_op jit(solution)/shard_map/norm_back/pallas_call | solution.py:143
  637.9 63.2 %attend_back.2.refs_0_ = bf16[4096,384]{1,0:T(8,128)(2,1)} custom-call(s32[8]{0:T(128)} %fusion.2.refs_0_, bf16[4096,128]{1,0:T(8,128)(2,1)} %get-tuple-element.55.refs_0_.refs_1_, bf16[4096,128]{1,0:T(8,128)(2,1)} %get-tuple-element.56.refs_1_.refs_2_, bf16[4096,128]{1,0:T(8,128)(2,1)} %get-tuple-element.57.refs_2_.refs_3_, bf16[4096,128]{1,0:T(8,128)(2,1)} %bitcast.76, ...), custom_call_target="tpu_custom_call" | custom-call | flops 25769803776 | bytes 8388608 | tf_op jit(solution)/shard_map/attend_back/pallas_call | solution.py:143
  701.1 14.3 %convolution_convert_fusion.4.refs_10_.refs_3_.refs_6_ = bf16[2048,384]{1,0:T(8,128)(2,1)} fusion(bf16[4096,2048]{1,0:T(8,128)(2,1)} %first_norm.15.x_ref.refs_0_, bf16[4096,384]{1,0:T(8,128)(2,1)} %attend_back.2.refs_0_), kind=kOutput, calls=%fused_computation.9 | convolution fusion | flops 6443237376 | bytes 21495808 | tf_op jit(solution)/shard_map/dot_general | solution.py:28
  732.7 63.0 %attend_back.3.refs_1_ = bf16[4096,384]{1,0:T(8,128)(2,1)} custom-call(s32[8]{0:T(128)} %fusion.2.refs_0_, bf16[4096,128]{1,0:T(8,128)(2,1)} %get-tuple-element.59.refs_0_.refs_1_, bf16[4096,128]{1,0:T(8,128)(2,1)} %get-tuple-element.60.refs_1_.refs_2_, bf16[4096,128]{1,0:T(8,128)(2,1)} %get-tuple-element.61.refs_2_.refs_3_, bf16[4096,128]{1,0:T(8,128)(2,1)} %bitcast.75, ...), custom_call_target="tpu_custom_call" | custom-call | flops 25769803776 | bytes 8388608 | tf_op jit(solution)/shard_map/attend_back/pallas_call | solution.py:143
  825.9 13.3 %convolution_convert_fusion.3.refs_7_ = bf16[2048,384]{1,0:T(8,128)(2,1)} fusion(bf16[4096,2048]{1,0:T(8,128)(2,1)} %held.42, bf16[4096,384]{1,0:T(8,128)(2,1)S(1)} %copy-done.2), kind=kOutput, calls=%fused_computation.8 | convolution fusion | flops 6443237376 | bytes 21495808 | tf_op jit(solution)/shard_map/dot_general | solution.py:28
  851.5 12.8 %all-to-all-done.8.refs_8_.refs_0_ = bf16[8,64,384]{2,1,0:T(8,128)(2,1)S(1)} async-done(((bf16[8,64,384]{2,1,0:T(8,128)(2,1)}), bf16[8,64,384]{2,1,0:T(8,128)(2,1)S(1)}, u32[]{:S(2)}, u32[]{:S(2)}) %all-to-all-start.8) | async-done | bytes 393248 | tf_op jit(solution)/shard_map/all_to_all | solution.py:752
  903.0 17.6 %collective-permute-done.46.refs_6_ = bf16[1,512,2048]{2,1,0:T(8,128)(2,1)} collective-permute-done((bf16[1,512,2048]{2,1,0:T(8,128)(2,1)}, bf16[1,512,2048]{2,1,0:T(8,128)(2,1)}, u32[]{:S(2)}, u32[]{:S(2)}) %collective-permute-start.46) | collective-permute-done | bytes 2097184 | tf_op jit(solution)/shard_map/ppermute | solution.py:80
  (333 shorter events, 389.7 us)
Async XLA Ops:
  16.2 64.8 %collective-permute-start.1 = (bf16[512,2048]{1,0:T(8,128)(2,1)S(1)}, bf16[512,2048]{1,0:T(8,128)(2,1)}, u32[]{:S(2)}, u32[]{:S(2)}) collective-permute-start(bf16[512,2048]{1,0:T(8,128)(2,1)S(1)} %bitcast.56), channel_id=1, source_target_pairs={{0,1},{1,0},{2,3},{3,2},{4,5},{5,4},{6,7},{7,6},{8,9},{9,8},{10,11... | collective-permute-start | bytes 6291464 | tf_op jit(solution)/shard_map/ppermute | solution.py:76
  18.9 65.9 %collective-permute-start = (bf16[512,2048]{1,0:T(8,128)(2,1)S(1)}, bf16[512,2048]{1,0:T(8,128)(2,1)}, u32[]{:S(2)}, u32[]{:S(2)}) collective-permute-start(bf16[512,2048]{1,0:T(8,128)(2,1)S(1)} %bitcast.57), channel_id=1, source_target_pairs={{0,2},{1,5},{2,0},{3,7},{4,6},{5,1},{6,4},{7,3},{8,10},{9,13},{10,... | collective-permute-start | bytes 6291464 | tf_op jit(solution)/shard_map/ppermute | solution.py:76
  20.4 65.3 %collective-permute-start.8 = (bf16[512,2048]{1,0:T(8,128)(2,1)S(1)}, bf16[512,2048]{1,0:T(8,128)(2,1)}, u32[]{:S(2)}, u32[]{:S(2)}) collective-permute-start(bf16[512,2048]{1,0:T(8,128)(2,1)S(1)} %bitcast.58), channel_id=1, source_target_pairs={{0,4},{1,3},{2,6},{3,1},{4,0},{5,7},{6,2},{7,5},{8,12},{9,11},{10,... | collective-permute-start | bytes 6291464 | tf_op jit(solution)/shard_map/ppermute | solution.py:76
  63.3 205.8 %all-gather.5.cloned.1.call-start = ((), (), s32[]{:S(2)}) async-start(), calls=%async_computation.17 | async-start | bytes 3932160 | tf_op jit(solution)/shard_map/all_gather | solution.py:839
  118.1 163.3 %all-gather.3.cloned.1.call-start = ((), (), s32[]{:S(2)}) async-start(), calls=%async_computation.16 | async-start | bytes 9437184 | tf_op jit(solution)/shard_map/all_gather | solution.py:838
  160.3 56.0 %collective-permute-start.14 = (bf16[512,2048]{1,0:T(8,128)(2,1)}, bf16[512,2048]{1,0:T(8,128)(2,1)}, u32[]{:S(2)}, u32[]{:S(2)}) collective-permute-start(bf16[512,2048]{1,0:T(8,128)(2,1)} %held.27), channel_id=1, source_target_pairs={{0,2},{1,5},{2,0},{3,7},{4,6},{5,1},{6,4},{7,3},{8,10},{9,13},{10,... | collective-permute-start | bytes 6291464 | tf_op jit(solution)/shard_map/ppermute | solution.py:76
  162.3 54.1 %collective-permute-start.13 = (bf16[512,2048]{1,0:T(8,128)(2,1)}, bf16[512,2048]{1,0:T(8,128)(2,1)}, u32[]{:S(2)}, u32[]{:S(2)}) collective-permute-start(bf16[512,2048]{1,0:T(8,128)(2,1)} %held.27), channel_id=1, source_target_pairs={{0,1},{1,0},{2,3},{3,2},{4,5},{5,4},{6,7},{7,6},{8,9},{9,8},{10,11... | collective-permute-start | bytes 6291464 | tf_op jit(solution)/shard_map/ppermute | solution.py:76
  162.3 56.5 %collective-permute-start.15 = (bf16[512,2048]{1,0:T(8,128)(2,1)}, bf16[512,2048]{1,0:T(8,128)(2,1)}, u32[]{:S(2)}, u32[]{:S(2)}) collective-permute-start(bf16[512,2048]{1,0:T(8,128)(2,1)} %held.27), channel_id=1, source_target_pairs={{0,4},{1,3},{2,6},{3,1},{4,0},{5,7},{6,2},{7,5},{8,12},{9,11},{10,... | collective-permute-start | bytes 6291464 | tf_op jit(solution)/shard_map/ppermute | solution.py:76
  206.0 55.0 %all-to-all-start.2 = ((bf16[8,512,128]{2,1,0:T(8,128)(2,1)}), bf16[8,512,128]{2,1,0:T(8,128)(2,1)}, u32[]{:S(2)}, u32[]{:S(2)}) async-start(bf16[8,512,128]{2,1,0:T(8,128)(2,1)} %bitcast.74), calls=%async_computation.2 | async-start | bytes 2097152 | tf_op jit(solution)/shard_map/all_to_all | solution.py:752
  214.0 67.5 %collective-permute-start.17 = (bf16[512,1536]{1,0:T(8,128)(2,1)}, bf16[512,1536]{1,0:T(8,128)(2,1)S(1)}, u32[]{:S(2)}, u32[]{:S(2)}) collective-permute-start(bf16[512,1536]{1,0:T(8,128)(2,1)} %held.29.refs_6_.refs_7_), channel_id=1, source_target_pairs={{0,8},{8,16},{16,24},{24,0},{1,9},{9,17},{17,25},{25,1},{2,10},{10... | collective-permute-start | bytes 4718600 | tf_op jit(solution)/shard_map/ppermute | solution.py:848
  265.5 463.6 %reduce-scatter.10.cloned.1.call-start = ((), (), s32[]{:S(2)}) async-start(), calls=%async_computation.20 | async-start | bytes 7864320 | tf_op jit(solution)/shard_map/reduce_scatter | solution.py:897
  558.1 237.6 %reduce-scatter.8.cloned.1.call-start = ((), (), s32[]{:S(2)}) async-start(), calls=%async_computation.19 | async-start | bytes 3932160 | tf_op jit(solution)/shard_map/reduce_scatter | solution.py:895
  614.0 118.7 %collective-permute-start.40 = (bf16[2,256,2048]{2,1,0:T(8,128)(2,1)}, bf16[2,256,2048]{2,1,0:T(8,128)(2,1)}, u32[]{:S(2)}, u32[]{:S(2)}) collective-permute-start(bf16[2,256,2048]{2,1,0:T(8,128)(2,1)} %pad_maximum_fusion.1), channel_id=1, source_target_pairs={{0,1},{1,0},{2,3},{3,2},{4,5},{5,4},{6,7},{7,6},{8,9},{9,8},{10,11... | collective-permute-start | bytes 6291464 | tf_op jit(solution)/shard_map/ppermute | solution.py:76
  616.0 99.4 %collective-permute-start.39 = (bf16[2,256,2048]{2,1,0:T(8,128)(2,1)}, bf16[2,256,2048]{2,1,0:T(8,128)(2,1)}, u32[]{:S(2)}, u32[]{:S(2)}) collective-permute-start(bf16[2,256,2048]{2,1,0:T(8,128)(2,1)} %pad_maximum_fusion), channel_id=1, source_target_pairs={{0,1},{1,0},{2,3},{3,2},{4,5},{5,4},{6,7},{7,6},{8,9},{9,8},{10,11... | collective-permute-start | bytes 6291464 | tf_op jit(solution)/shard_map/ppermute | solution.py:76
  623.2 97.9 %collective-permute-start.35 = (bf16[2,512,2048]{2,1,0:T(8,128)(2,1)}, bf16[2,512,2048]{2,1,0:T(8,128)(2,1)}, u32[]{:S(2)}, u32[]{:S(2)}) collective-permute-start(bf16[2,512,2048]{2,1,0:T(8,128)(2,1)} %block_product.21.refs_3_), channel_id=1, source_target_pairs={{0,1},{1,0},{2,3},{3,2},{4,5},{5,4},{6,7},{7,6},{8,9},{9,8},{10,11... | collective-permute-start | bytes 12582920 | tf_op jit(solution)/shard_map/ppermute | solution.py:76
  631.7 89.4 %collective-permute-start.37 = (bf16[2,512,2048]{2,1,0:T(8,128)(2,1)}, bf16[2,512,2048]{2,1,0:T(8,128)(2,1)}, u32[]{:S(2)}, u32[]{:S(2)}) collective-permute-start(bf16[2,512,2048]{2,1,0:T(8,128)(2,1)} %block_product.22.refs_10_), channel_id=1, source_target_pairs={{4,0},{3,1},{6,2},{1,3},{0,4},{7,5},{2,6},{5,7},{12,8},{11,9},{14,... | collective-permute-start | bytes 12582920 | tf_op jit(solution)/shard_map/ppermute | solution.py:80
  634.3 94.8 %all-to-all-start.6 = ((bf16[8,512,128]{2,1,0:T(8,128)(2,1)}), bf16[8,512,128]{2,1,0:T(8,128)(2,1)S(1)}, u32[]{:S(2)}, u32[]{:S(2)}) async-start(bf16[8,512,128]{2,1,0:T(8,128)(2,1)} %get-tuple-element.88), calls=%async_computation.6 | async-start | bytes 2097152 | tf_op jit(solution)/shard_map/all_to_all | solution.py:752
  637.9 157.9 %reduce-scatter.6.cloned.1.call-start = ((), (), s32[]{:S(2)}) async-start(), calls=%async_computation.18 | async-start | bytes 1966080 | tf_op jit(solution)/shard_map/reduce_scatter | solution.py:916
  719.1 76.6 %collective-permute-start.41 = (bf16[2,256,2048]{2,1,0:T(8,128)(2,1)}, bf16[2,256,2048]{2,1,0:T(8,128)(2,1)}, u32[]{:S(2)}, u32[]{:S(2)}) collective-permute-start(bf16[2,256,2048]{2,1,0:T(8,128)(2,1)} %add_convert_fusion.refs_12_), channel_id=1, source_target_pairs={{4,0},{3,1},{6,2},{1,3},{0,4},{7,5},{2,6},{5,7},{12,8},{11,9},{14,... | collective-permute-start | bytes 6291464 | tf_op jit(solution)/shard_map/ppermute | solution.py:80
  727.6 68.2 %collective-permute-start.38 = (bf16[1,512,2048]{2,1,0:T(8,128)(2,1)}, bf16[1,512,2048]{2,1,0:T(8,128)(2,1)}, u32[]{:S(2)}, u32[]{:S(2)}) collective-permute-start(bf16[1,512,2048]{2,1,0:T(8,128)(2,1)} %block_product.23.refs_11_), channel_id=1, source_target_pairs={{2,0},{5,1},{0,2},{7,3},{6,4},{1,5},{4,6},{3,7},{10,8},{13,9},{8,1... | collective-permute-start | bytes 6291464 | tf_op jit(solution)/shard_map/ppermute | solution.py:80
  729.1 66.7 %all-to-all-start.7 = ((bf16[8,64,1536]{2,1,0:T(8,128)(2,1)}), bf16[8,64,1536]{2,1,0:T(8,128)(2,1)S(1)}, u32[]{:S(2)}, u32[]{:S(2)}) async-start(bf16[8,64,1536]{2,1,0:T(8,128)(2,1)} %bitcast.72), calls=%async_computation.10 | async-start | bytes 3145728 | tf_op jit(solution)/shard_map/all_to_all | solution.py:752
  732.7 148.3 %reduce-scatter.12.cloned.1.call-start = ((), (), s32[]{:S(2)}) async-start(), calls=%async_computation.21 | async-start | bytes 1966080 | tf_op jit(solution)/shard_map/reduce_scatter | solution.py:933
  813.4 50.9 %collective-permute-start.42 = (bf16[2,512,2048]{2,1,0:T(8,128)(2,1)}, bf16[2,512,2048]{2,1,0:T(8,128)(2,1)}, u32[]{:S(2)}, u32[]{:S(2)}) collective-permute-start(bf16[2,512,2048]{2,1,0:T(8,128)(2,1)} %block_product.26.refs_5_), channel_id=1, source_target_pairs={{0,1},{1,0},{2,3},{3,2},{4,5},{5,4},{6,7},{7,6},{8,9},{9,8},{10,11... | collective-permute-start | bytes 12582920 | tf_op jit(solution)/shard_map/ppermute | solution.py:76
  849.5 101.2 %reduce-scatter.14.cloned.1.call-start = ((), (), s32[]{:S(2)}) async-start(), calls=%async_computation.22 | async-start | bytes 1310720 | tf_op jit(solution)/shard_map/reduce_scatter | solution.py:940
  (85 other events, 1669.7 us)
Sparse Core Ops, SparseCore 0:
  118.2 70.9 all-gather.4
  191.7 68.7 all-gather.2
  558.2 108.7 reduce-scatter.9
  669.2 60.7 reduce-scatter.7
  732.7 35.3 reduce-scatter.5
  839.3 32.5 reduce-scatter.11
  881.1 24.1 reduce-scatter.13

commit v4 on v3

--- a/solution.py
+++ b/solution.py
@@ -819,7 +819,8 @@
     partner, one, twos = plane.gather_first(x)
     normed = norm_next(None, x, 0)
     normed = norm_next(normed, partner, half)
-    one = held(one, (normed, joint_blocks[1:3], gate_up_cols))
+    cot = held(cotangent.reshape(span, D), small_all)
+    one = held(one, (normed, joint_blocks[1:3], gate_up_cols, cot))
     one_other, two_others, threes = plane.gather_second(one, twos)
     normed = norm_next(normed, one, 1)
     for n, two in enumerate(twos):
@@ -839,9 +840,8 @@
     down = lax.all_gather(held(down_rows, threes), "fsdp", axis=0, tiled=True)
     gate_up_blocks = [held(swap_sp(held(gate_up_cols, threes)).reshape(n_sp * depth, 2 * ff), heads[0])]
     gate_up_blocks.append(lax.ppermute(gate_up_blocks[0], "fsdp", ring))
-    cot = cotangent.reshape(span, D)
-    cot_held = held(cot, gate_up_blocks[0])
-    cot_partner, cot_one, cot_twos = plane.gather_first(cot_held)
+    cot = held(cot, gate_up_blocks[0])
+    cot_partner, cot_one, cot_twos = plane.gather_first(cot)
     results = [attend(*heads[:3])]
     cot_one = held(cot_one, results[0][1])
     gate_up_blocks[1] = held(gate_up_blocks[1], results[0][1])
@@ -849,7 +849,7 @@
     cot_one_other, cot_two_others, cot_threes = plane.gather_second(cot_one, cot_twos)
     for g in range(1, groups):
         results.append(attend(*heads[3 * g : 3 * g + 3], (cot_partner, cot_one, cot_twos, gate_up_blocks[1])))
-    cot_threes = [held(c, results[-1][1]) for c in cot_threes]
+    gate_up_blocks[2] = held(gate_up_blocks[2], results[-1][1])
     for _ in range(3, n_z):
         gate_up_blocks.append(lax.ppermute(gate_up_blocks[-1], "fsdp", ring))
     cot_three_others = plane.gather_third(cot_threes)
@@ -859,9 +859,10 @@
     for pieces in zip(cot_two_others, cot_three_others):
         cot_partners += pieces
     gate_up = in_line(gate_up_blocks, my_z)
+    results[-1] = (held(results[-1][0], cot_threes), results[-1][1])
     attended = [swap_sp(o).reshape(n_sp, span, group) for o, _ in results]
     middle, normed_two, normed_again, attended_all = middle_of(
-        attended, out_full, depth, x, gain_two, shift_two, (gate_up_blocks[:3], down)
+        attended, out_full, depth, x, gain_two, shift_two, (gate_up, down)
     )
 
     feed = None
@@ -871,14 +872,16 @@
 
     partner = plane.send(normed_two, plane.core)
     one = plane.send(normed_two, plane.first)
-    feed = feed_next(None, (normed_two, partner), 0, (cot_blocks, cot_partners))
+    feed = feed_next(None, (normed_two, partner), 0)
+    one = held(one, feed[0])
     one_other = plane.send(one, plane.core)
     again = held(normed_again, one)
     for n, perm in enumerate(plane.later):
         two = plane.send(again, perm)
         if n == 0:
-            feed = feed_next(feed, (one, one_other), 1)
-        one = held(one, (two, one_other, feed[0]))
+            feed = feed_next(feed, (one, one_other), 1, again)
+        two = held(two, feed[0])
+        one = held(one, (two, one_other))
         three = plane.send(one, perm)
         feed = feed_next(feed, (two, plane.send(two, plane.core)), 2 + 2 * n)
         three = held(three, feed[0])
@@ -933,7 +936,7 @@
         joint_parts.append(lax.psum_scatter(joint_sums[g], "fsdp", scatter_dimension=0, tiled=True))
     joint_own = [swap_sp(j).reshape(n_sp, depth, 3 * group) for j in joint_parts]
     normed_one, normed_last = plane.legs_next(
-        normed_product, further, normed_theirs, (joint_sums, joint_own[:-1])
+        normed_product, further, normed_theirs, joint_sums
     )
     output = (middle + plane.reduce_own(out_product, out_got, out_theirs, out_last, f32)).astype(bf16)
     out_own = plane.reduce_own(out_weight_part, weight_got, weight_theirs, weight_last)

time: 970 us -> 962 us (level)
  waiting for transfers between devices: 171 us -> 156 us
    ppermute x10, waiting for transfers between devices: 34.5 us -> 18.7 us  [back(): return lax.ppermute(value, 'sp', [(b, a) for a, b in perm])]
    unnamed x91 -> x95, local copies, waits for them, and re-layouts: 25.9 us -> 26.6 us
    pallas_call x60 -> x64, Pallas kernels: 488 us -> 488 us  [launch(): pl.pallas_call(body, grid_spec=pltpu.PrefetchScalarGridSpec(num_scalar_pr...]
  transfers between devices with their start and end apart: 66 -> 66, of which waited for: 22 -> 22; matrix products, arithmetic and copies ran while one was open for 15% -> 16% of each run, Pallas kernels for 47% -> 46%
where the time goes in v4:
time: 962 us; the launch traced here: 953 us
  Pallas kernels  509 us (53%)
  waiting for transfers between devices  156 us (16%)
  matrix products  89.9 us (9%)
  starting transfers between devices  80.4 us (8%)
  local copies, waits for them, and re-layouts  61.5 us (6%)
  between operations  30.3 us (3%)
  other arithmetic  25 us (3%)
    pallas_call x64, Pallas kernels, launch(): pl.pallas_call(body, grid_spec=pltpu.PrefetchScalarGridSpec(num_scalar_pr...  488 us
    dot_general x5, matrix products, dot(): return lax.dot_general(a, b, dims, preferred_element_type=f32)  89.9 us
    ppermute x29, waiting for transfers between devices, send(): return lax.ppermute(value, 'sp', perm)  37 us
    all_to_all x9, starting transfers between devices, swap_sp(): return lax.all_to_all(value, 'sp', split_axis=0, concat_axis=0, tiled=True)  34.1 us
    ppermute x3, waiting for transfers between devices, per_device(): joint_blocks.append(lax.ppermute(joint_blocks[-1], 'fsdp', ring))  27.9 us
    all_to_all x9, waiting for transfers between devices, swap_sp(): return lax.all_to_all(value, 'sp', split_axis=0, concat_axis=0, tiled=True)  26.6 us
    unnamed x95, local copies, waits for them, and re-layouts  26.6 us
    pallas_call x1, Pallas kernels, joint_projection(): pl.pallas_call(functools.partial(joint_kernel, width), grid_spec=pltpu.Pr...  21.4 us
  transfers between devices with their start and end apart: 66, of which 22 were waited for; matrix products, arithmetic and copies ran while one was open for 16% of the time, Pallas kernels for 46%

profile of v4, /device:TPU:0, one launch (start us, length us, event | category | flops | bytes accessed | tf_op | source)
XLA Modules:
  0.0 952.7 jit_solution(965484800225864327)
XLA Ops:
  40.2 19.0 %collective-permute-done.5.refs_2_ = bf16[512,768]{1,0:T(8,128)(2,1)} collective-permute-done((bf16[512,768]{1,0:T(8,128)(2,1)}, bf16[512,768]{1,0:T(8,128)(2,1)}, u32[]{:S(2)}, u32[]{:S(2)}) %collective-permute-start.5) | collective-permute-done | bytes 786464 | tf_op jit(solution)/shard_map/ppermute | solution.py:808
  138.3 21.4 %joint_projection.1 = (bf16[4096,128]{1,0:T(8,128)(2,1)}, bf16[4096,128]{1,0:T(8,128)(2,1)}, bf16[4096,128]{1,0:T(8,128)(2,1)}, bf16[4096,128]{1,0:T(8,128)(2,1)...) custom-call(s32[8]{0:T(128)} %get-tuple-element.113.table_ref, bf16[4096,2048]{1,0:T(8,128)(2,1)} %first_norm.15.x_ref.refs_0_, ...), custom_call_target="tpu_custom_call" | custom-call | flops 12884901888 | bytes 23068672 | tf_op jit(solution)/shard_map/joint_projection/pallas_call | solution.py:460
  164.3 42.2 %attend.2 = (bf16[4096,128]{1,0:T(8,128)(2,1)}, f32[8,4096]{1,0:T(8,128)}) custom-call(bf16[4096,128]{1,0:T(8,128)(2,1)} %get-tuple-element.55.refs_0_.refs_1_, bf16[4096,128]{1,0:T(8,128)(2,1)} %get-tuple-element.56.refs_1_.refs_2_, bf16[4096,128]{1,0:T(8,128)(2,1)} %get-tuple-element.57.refs_2_.refs_3_), custom_call_target="tpu_custom_call" | custom-call | flops 17179869184 | bytes 4194304 | tf_op jit(solution)/shard_map/attend/pallas_call | solution.py:143
  219.2 42.2 %attend.3 = (bf16[4096,128]{1,0:T(8,128)(2,1)}, f32[8,4096]{1,0:T(8,128)}) custom-call(bf16[4096,128]{1,0:T(8,128)(2,1)} %get-tuple-element.59.refs_0_.refs_1_, bf16[4096,128]{1,0:T(8,128)(2,1)} %get-tuple-element.60.refs_1_.refs_2_, bf16[4096,128]{1,0:T(8,128)(2,1)} %get-tuple-element.61.refs_2_.refs_3_, bf16[512,2048]{1,0:T(8,128)(2,1)} %collective-permute-done.13.refs_3_, ...), custom_call_target="tpu_custom_call" | custom-call | flops 17179869184 | bytes 4194304 | tf_op jit(solution)/shard_map/attend/pallas_call | solution.py:143
  264.0 12.6 %collective-permute-done.17.refs_1_.refs_2_ = bf16[512,2048]{1,0:T(8,128)(2,1)} collective-permute-done((bf16[512,2048]{1,0:T(8,128)(2,1)}, bf16[512,2048]{1,0:T(8,128)(2,1)}, u32[]{:S(2)}, u32[]{:S(2)}) %collective-permute-start.17) | collective-permute-done | bytes 2097184 | tf_op jit(solution)/shard_map/ppermute | solution.py:76
  288.7 11.9 %collective-permute-done.19 = bf16[512,1536]{1,0:T(8,128)(2,1)} collective-permute-done((bf16[512,1536]{1,0:T(8,128)(2,1)}, bf16[512,1536]{1,0:T(8,128)(2,1)}, u32[]{:S(2)}, u32[]{:S(2)}) %collective-permute-start.19) | collective-permute-done | bytes 1572896 | tf_op jit(solution)/shard_map/ppermute | solution.py:854
  304.2 12.5 %middle.1 = (f32[512,2048]{1,0:T(8,128)}, bf16[512,2048]{1,0:T(8,128)(2,1)}, bf16[512,2048]{1,0:T(8,128)(2,1)}, bf16[512,2048]{1,0:T(8,128)(2,1)}) custom-call(bf16[8,512,128]{2,1,0:T(8,128)(2,1)} %all-to-all-done.2.refs_0_, bf16[8,512,128]{2,1,0:T(8,128)(2,1)} %copy-done.20, bf16[2048,2048]{1,0:T(8,128)(2,1)} %all-gather.3.cloned.1.call-done.refs_2_.refs_4_, ...), custom_call_target="tpu_custom_call" | custom-call | flops 4294967296 | bytes 20971520 | tf_op jit(solution)/shard_map/middle/pallas_call | solution.py:143
  321.3 18.0 %feed_forward.4 = (bf16[4096,768]{1,0:T(8,128)(2,1)}, bf16[4096,1536]{1,0:T(8,128)(2,1)}, bf16[4096,2048]{1,0:T(8,128)(2,1)}, bf16[4096,2048]{1,0:T(8,128)(2,1)}) custom-call(bf16[512,2048]{1,0:T(8,128)(2,1)} %get-tuple-element.66.refs_0_, bf16[512,2048]{1,0:T(8,128)(2,1)} %collective-permute-done.21.refs_1_, bf16[512,2048]{1,0:T(8,128)(2,1)} %held.32.refs_2_.refs_3_, ...), custom_call_target="tpu_custom_call" | custom-call | flops 9663676416 | bytes 26214400 | tf_op jit(solution)/shard_map/feed_forward/pallas_call | solution.py:143
  348.9 18.0 %feed_forward.5 = (bf16[4096,768]{1,0:T(8,128)(2,1)}, bf16[4096,1536]{1,0:T(8,128)(2,1)}, bf16[4096,2048]{1,0:T(8,128)(2,1)}, bf16[4096,2048]{1,0:T(8,128)(2,1)}) custom-call(bf16[512,2048]{1,0:T(8,128)(2,1)} %held.39.refs_1_.refs_0_, ...), custom_call_target="tpu_custom_call", output_to_operand_aliasing={{0}: (6, {}), {1}: (7, {}), {2}: (8, {}), {3}: (9, {})} | custom-call | flops 9663676416 | bytes 26214400 | tf_op jit(solution)/shard_map/feed_forward/pallas_call | solution.py:143
  376.5 18.1 %feed_forward.6 = (bf16[4096,768]{1,0:T(8,128)(2,1)}, bf16[4096,1536]{1,0:T(8,128)(2,1)}, bf16[4096,2048]{1,0:T(8,128)(2,1)}, bf16[4096,2048]{1,0:T(8,128)(2,1)}) custom-call(bf16[512,2048]{1,0:T(8,128)(2,1)} %held.41.refs_1_.refs_0_, ...), custom_call_target="tpu_custom_call", output_to_operand_aliasing={{0}: (6, {}), {1}: (7, {}), {2}: (8, {}), {3}: (9, {})} | custom-call | flops 9663676416 | bytes 26214400 | tf_op jit(solution)/shard_map/feed_forward/pallas_call | solution.py:143
  405.3 18.2 %feed_forward.7 = (bf16[4096,768]{1,0:T(8,128)(2,1)}, bf16[4096,1536]{1,0:T(8,128)(2,1)}, bf16[4096,2048]{1,0:T(8,128)(2,1)}, bf16[4096,2048]{1,0:T(8,128)(2,1)}) custom-call(bf16[512,2048]{1,0:T(8,128)(2,1)} %held.43.refs_0_, bf16[512,2048]{1,0:T(8,128)(2,1)} %copy-done.26, ...), custom_call_target="tpu_custom_call", output_to_operand_aliasing={{0}: (6, {}), {1}: (7, {}), {2}: (8, {}), {3}: (9, {})} | custom-call | flops 9663676416 | bytes 26214400 | tf_op jit(solution)/shard_map/feed_forward/pallas_call | solution.py:143
  423.5 10.8 %block_product.15.refs_2_ = bf16[2,512,2048]{2,1,0:T(8,128)(2,1)} custom-call(bf16[4096,1536]{1,0:T(8,128)(2,1)} %get-tuple-element.81.refs_0_, bf16[2048,1536]{1,0:T(8,128)(2,1)} %constant_dynamic-update-slice_fusion.refs_6_.refs_4_.refs_1_), custom_call_target="tpu_custom_call" | custom-call | flops 6442450944 | bytes 17825792 | tf_op jit(solution)/shard_map/block_product/pallas_call | solution.py:143
  434.4 10.8 %block_product.16.refs_3_ = bf16[2,512,2048]{2,1,0:T(8,128)(2,1)} custom-call(bf16[4096,1536]{1,0:T(8,128)(2,1)} %get-tuple-element.81.refs_0_, bf16[2048,1536]{1,0:T(8,128)(2,1)} %constant_dynamic-update-slice_fusion.refs_6_.refs_4_.refs_1_, bf16[2,512,2048]{2,1,0:T(8,128)(2,1)} %block_product.15.refs_2_), custom_call_target="tpu_custom_call" | custom-call | flops 6442450944 | bytes 17825792 | tf_op jit(solution)/shard_map/block_product/pallas_call | solution.py:143
  445.5 11.1 %block_product.17 = (bf16[1,512,2048]{2,1,0:T(8,128)(2,1)}, bf16[1,512,2048]{2,1,0:T(8,128)(2,1)}) custom-call(bf16[4096,1536]{1,0:T(8,128)(2,1)} %get-tuple-element.81.refs_0_, bf16[2048,1536]{1,0:T(8,128)(2,1)} %constant_dynamic-update-slice_fusion.refs_6_.refs_4_.refs_1_, bf16[2,512,2048]{2,1,0:T(8,128)(2,1)} %collective-permute-done.31.refs_2_, ...), custom_call_target="tpu_custom_call" | custom-call | flops 6442450944 | bytes 17825792 | tf_op jit(solution)/shard_map/block_product/pallas_call | solution.py:143
  458.1 19.9 %convolution_convert_fusion.2.refs_4_.refs_0_ = bf16[768,2048]{1,0:T(8,128)(2,1)} fusion(bf16[4096,768]{1,0:T(8,128)(2,1)} %get-tuple-element.80.refs_0_, bf16[4096,2048]{1,0:T(8,128)(2,1)} %held.45), kind=kOutput, calls=%fused_computation.7 | convolution fusion | flops 12886474752 | bytes 26214400 | tf_op jit(solution)/shard_map/dot_general | solution.py:28
  495.0 34.0 %convolution_convert_fusion.1.refs_5_.refs_0_ = bf16[2048,1536]{1,0:T(8,128)(2,1)} fusion(bf16[4096,2048]{1,0:T(8,128)(2,1)} %held.46, bf16[4096,1536]{1,0:T(8,128)(2,1)} %get-tuple-element.81.refs_0_), kind=kOutput, calls=%fused_computation.1 | convolution fusion | flops 25772949504 | bytes 35651584 | tf_op jit(solution)/shard_map/dot_general | solution.py:28
  529.0 12.3 %collective-permute-done.34.refs_4_ = bf16[1,512,2048]{2,1,0:T(8,128)(2,1)S(1)} collective-permute-done((bf16[1,512,2048]{2,1,0:T(8,128)(2,1)}, bf16[1,512,2048]{2,1,0:T(8,128)(2,1)S(1)}, u32[]{:S(2)}, u32[]{:S(2)}) %collective-permute-start.34) | collective-permute-done | bytes 2097184 | tf_op jit(solution)/shard_map/ppermute | solution.py:80
  542.6 9.0 block_product.19
  551.6 16.8 %norm_back.2 = (f32[512,2048]{1,0:T(8,128)}, f32[8,2048]{1,0:T(8,128)}, bf16[512,2048]{1,0:T(8,128)(2,1)}, bf16[8,512,128]{2,1,0:T(8,128)(2,1)}, bf16[8,512,128]{2,1,0:T(8,128)(2,1)}) custom-call(bf16[512,2048]{1,0:T(8,128)(2,1)} %bitcast.61, f32[512,2048]{1,0:T(8,128)} %get-tuple-element.65.refs_1_, f32[1,2048]{1,0:T(1,128)} %reshape.132.refs_4_.refs_2_, ...), custom_call_target="tpu_custom_call" | custom-call | flops 4315938816 | bytes 25165824 | tf_op jit(solution)/shard_map/norm_back/pallas_call | solution.py:143
  631.4 63.0 %attend_back.2.refs_0_ = bf16[4096,384]{1,0:T(8,128)(2,1)} custom-call(s32[8]{0:T(128)} %fusion.2.refs_0_, bf16[4096,128]{1,0:T(8,128)(2,1)} %get-tuple-element.55.refs_0_.refs_1_, bf16[4096,128]{1,0:T(8,128)(2,1)} %get-tuple-element.56.refs_1_.refs_2_, bf16[4096,128]{1,0:T(8,128)(2,1)} %get-tuple-element.57.refs_2_.refs_3_, bf16[4096,128]{1,0:T(8,128)(2,1)} %bitcast.73, ...), custom_call_target="tpu_custom_call" | custom-call | flops 25769803776 | bytes 8388608 | tf_op jit(solution)/shard_map/attend_back/pallas_call | solution.py:143
  694.4 14.3 %convolution_convert_fusion.4.refs_10_.refs_3_.refs_6_ = bf16[2048,384]{1,0:T(8,128)(2,1)} fusion(bf16[4096,2048]{1,0:T(8,128)(2,1)} %first_norm.15.x_ref.refs_0_, bf16[4096,384]{1,0:T(8,128)(2,1)} %attend_back.2.refs_0_), kind=kOutput, calls=%fused_computation.9 | convolution fusion | flops 6443237376 | bytes 21495808 | tf_op jit(solution)/shard_map/dot_general | solution.py:28
  726.0 63.2 %attend_back.3.refs_1_ = bf16[4096,384]{1,0:T(8,128)(2,1)} custom-call(s32[8]{0:T(128)} %fusion.2.refs_0_, bf16[4096,128]{1,0:T(8,128)(2,1)} %get-tuple-element.59.refs_0_.refs_1_, bf16[4096,128]{1,0:T(8,128)(2,1)} %get-tuple-element.60.refs_1_.refs_2_, bf16[4096,128]{1,0:T(8,128)(2,1)} %get-tuple-element.61.refs_2_.refs_3_, bf16[4096,128]{1,0:T(8,128)(2,1)} %bitcast.72, ...), custom_call_target="tpu_custom_call" | custom-call | flops 25769803776 | bytes 8388608 | tf_op jit(solution)/shard_map/attend_back/pallas_call | solution.py:143
  819.4 13.3 %convolution_convert_fusion.3.refs_7_ = bf16[2048,384]{1,0:T(8,128)(2,1)} fusion(bf16[4096,2048]{1,0:T(8,128)(2,1)} %held.50, bf16[4096,384]{1,0:T(8,128)(2,1)S(1)} %copy-done.2), kind=kOutput, calls=%fused_computation.8 | convolution fusion | flops 6443237376 | bytes 21495808 | tf_op jit(solution)/shard_map/dot_general | solution.py:28
  877.2 25.6 %all-to-all-done.9.refs_0_ = bf16[8,64,384]{2,1,0:T(8,128)(2,1)S(1)} async-done(((bf16[8,64,384]{2,1,0:T(8,128)(2,1)}), bf16[8,64,384]{2,1,0:T(8,128)(2,1)S(1)}, u32[]{:S(2)}, u32[]{:S(2)}) %all-to-all-start.9) | async-done | bytes 393248 | tf_op jit(solution)/shard_map/all_to_all | solution.py:752
  (341 shorter events, 384.4 us)
Async XLA Ops:
  19.5 64.8 %collective-permute-start.1 = (bf16[512,2048]{1,0:T(8,128)(2,1)S(1)}, bf16[512,2048]{1,0:T(8,128)(2,1)}, u32[]{:S(2)}, u32[]{:S(2)}) collective-permute-start(bf16[512,2048]{1,0:T(8,128)(2,1)S(1)} %bitcast.57), channel_id=1, source_target_pairs={{0,1},{1,0},{2,3},{3,2},{4,5},{5,4},{6,7},{7,6},{8,9},{9,8},{10,11... | collective-permute-start | bytes 6291464 | tf_op jit(solution)/shard_map/ppermute | solution.py:76
  22.1 65.9 %collective-permute-start = (bf16[512,2048]{1,0:T(8,128)(2,1)S(1)}, bf16[512,2048]{1,0:T(8,128)(2,1)}, u32[]{:S(2)}, u32[]{:S(2)}) collective-permute-start(bf16[512,2048]{1,0:T(8,128)(2,1)S(1)} %bitcast.58), channel_id=1, source_target_pairs={{0,2},{1,5},{2,0},{3,7},{4,6},{5,1},{6,4},{7,3},{8,10},{9,13},{10,... | collective-permute-start | bytes 6291464 | tf_op jit(solution)/shard_map/ppermute | solution.py:76
  23.6 65.3 %collective-permute-start.8 = (bf16[512,2048]{1,0:T(8,128)(2,1)S(1)}, bf16[512,2048]{1,0:T(8,128)(2,1)}, u32[]{:S(2)}, u32[]{:S(2)}) collective-permute-start(bf16[512,2048]{1,0:T(8,128)(2,1)S(1)} %bitcast.59), channel_id=1, source_target_pairs={{0,4},{1,3},{2,6},{3,1},{4,0},{5,7},{6,2},{7,5},{8,12},{9,11},{10,... | collective-permute-start | bytes 6291464 | tf_op jit(solution)/shard_map/ppermute | solution.py:76
  66.6 236.6 %all-gather.5.cloned.1.call-start = ((), (), s32[]{:S(2)}) async-start(), calls=%async_computation.17 | async-start | bytes 3932160 | tf_op jit(solution)/shard_map/all_gather | solution.py:840
  121.4 181.9 %all-gather.3.cloned.1.call-start = ((), (), s32[]{:S(2)}) async-start(), calls=%async_computation.16 | async-start | bytes 9437184 | tf_op jit(solution)/shard_map/all_gather | solution.py:839
  160.9 56.8 %collective-permute-start.14 = (bf16[512,2048]{1,0:T(8,128)(2,1)}, bf16[512,2048]{1,0:T(8,128)(2,1)}, u32[]{:S(2)}, u32[]{:S(2)}) collective-permute-start(bf16[512,2048]{1,0:T(8,128)(2,1)} %held.32.refs_2_.refs_3_), channel_id=1, source_target_pairs={{0,2},{1,5},{2,0},{3,7},{4,6},{5,1},{6,4},{7,3},{8,10},{9,13},{10,... | collective-permute-start | bytes 6291464 | tf_op jit(solution)/shard_map/ppermute | solution.py:76
  162.9 56.3 %collective-permute-start.13 = (bf16[512,2048]{1,0:T(8,128)(2,1)}, bf16[512,2048]{1,0:T(8,128)(2,1)}, u32[]{:S(2)}, u32[]{:S(2)}) collective-permute-start(bf16[512,2048]{1,0:T(8,128)(2,1)} %held.32.refs_2_.refs_3_), channel_id=1, source_target_pairs={{0,1},{1,0},{2,3},{3,2},{4,5},{5,4},{6,7},{7,6},{8,9},{9,8},{10,11... | collective-permute-start | bytes 6291464 | tf_op jit(solution)/shard_map/ppermute | solution.py:76
  206.6 70.0 %all-to-all-start.2 = ((bf16[8,512,128]{2,1,0:T(8,128)(2,1)}), bf16[8,512,128]{2,1,0:T(8,128)(2,1)}, u32[]{:S(2)}, u32[]{:S(2)}) async-start(bf16[8,512,128]{2,1,0:T(8,128)(2,1)} %bitcast.71), calls=%async_computation.2 | async-start | bytes 2097152 | tf_op jit(solution)/shard_map/all_to_all | solution.py:752
  217.7 58.9 %collective-permute-start.17 = (bf16[512,2048]{1,0:T(8,128)(2,1)}, bf16[512,2048]{1,0:T(8,128)(2,1)}, u32[]{:S(2)}, u32[]{:S(2)}) collective-permute-start(bf16[512,2048]{1,0:T(8,128)(2,1)} %held.33.refs_4_.refs_2_), channel_id=1, source_target_pairs={{0,4},{1,3},{2,6},{3,1},{4,0},{5,7},{6,2},{7,5},{8,12},{9,11},{10,... | collective-permute-start | bytes 6291464 | tf_op jit(solution)/shard_map/ppermute | solution.py:76
  281.0 441.4 %reduce-scatter.10.cloned.1.call-start = ((), (), s32[]{:S(2)}) async-start(), calls=%async_computation.20 | async-start | bytes 7864320 | tf_op jit(solution)/shard_map/reduce_scatter | solution.py:900
  551.6 237.7 %reduce-scatter.8.cloned.1.call-start = ((), (), s32[]{:S(2)}) async-start(), calls=%async_computation.19 | async-start | bytes 3932160 | tf_op jit(solution)/shard_map/reduce_scatter | solution.py:898
  607.5 118.6 %collective-permute-start.40 = (bf16[2,256,2048]{2,1,0:T(8,128)(2,1)}, bf16[2,256,2048]{2,1,0:T(8,128)(2,1)}, u32[]{:S(2)}, u32[]{:S(2)}) collective-permute-start(bf16[2,256,2048]{2,1,0:T(8,128)(2,1)} %pad_maximum_fusion.1), channel_id=1, source_target_pairs={{0,1},{1,0},{2,3},{3,2},{4,5},{5,4},{6,7},{7,6},{8,9},{9,8},{10,11... | collective-permute-start | bytes 6291464 | tf_op jit(solution)/shard_map/ppermute | solution.py:76
  609.4 99.3 %collective-permute-start.39 = (bf16[2,256,2048]{2,1,0:T(8,128)(2,1)}, bf16[2,256,2048]{2,1,0:T(8,128)(2,1)}, u32[]{:S(2)}, u32[]{:S(2)}) collective-permute-start(bf16[2,256,2048]{2,1,0:T(8,128)(2,1)} %pad_maximum_fusion), channel_id=1, source_target_pairs={{0,1},{1,0},{2,3},{3,2},{4,5},{5,4},{6,7},{7,6},{8,9},{9,8},{10,11... | collective-permute-start | bytes 6291464 | tf_op jit(solution)/shard_map/ppermute | solution.py:76
  616.7 97.7 %collective-permute-start.35 = (bf16[2,512,2048]{2,1,0:T(8,128)(2,1)}, bf16[2,512,2048]{2,1,0:T(8,128)(2,1)}, u32[]{:S(2)}, u32[]{:S(2)}) collective-permute-start(bf16[2,512,2048]{2,1,0:T(8,128)(2,1)} %block_product.21.refs_3_), channel_id=1, source_target_pairs={{0,1},{1,0},{2,3},{3,2},{4,5},{5,4},{6,7},{7,6},{8,9},{9,8},{10,11... | collective-permute-start | bytes 12582920 | tf_op jit(solution)/shard_map/ppermute | solution.py:76
  625.2 89.3 %collective-permute-start.37 = (bf16[2,512,2048]{2,1,0:T(8,128)(2,1)}, bf16[2,512,2048]{2,1,0:T(8,128)(2,1)}, u32[]{:S(2)}, u32[]{:S(2)}) collective-permute-start(bf16[2,512,2048]{2,1,0:T(8,128)(2,1)} %block_product.22.refs_10_), channel_id=1, source_target_pairs={{4,0},{3,1},{6,2},{1,3},{0,4},{7,5},{2,6},{5,7},{12,8},{11,9},{14,... | collective-permute-start | bytes 12582920 | tf_op jit(solution)/shard_map/ppermute | solution.py:80
  627.7 94.6 %all-to-all-start.6 = ((bf16[8,512,128]{2,1,0:T(8,128)(2,1)}), bf16[8,512,128]{2,1,0:T(8,128)(2,1)S(1)}, u32[]{:S(2)}, u32[]{:S(2)}) async-start(bf16[8,512,128]{2,1,0:T(8,128)(2,1)} %get-tuple-element.88), calls=%async_computation.6 | async-start | bytes 2097152 | tf_op jit(solution)/shard_map/all_to_all | solution.py:752
  631.3 158.0 %reduce-scatter.6.cloned.1.call-start = ((), (), s32[]{:S(2)}) async-start(), calls=%async_computation.18 | async-start | bytes 1966080 | tf_op jit(solution)/shard_map/reduce_scatter | solution.py:919
  712.4 76.8 %collective-permute-start.41 = (bf16[2,256,2048]{2,1,0:T(8,128)(2,1)}, bf16[2,256,2048]{2,1,0:T(8,128)(2,1)}, u32[]{:S(2)}, u32[]{:S(2)}) collective-permute-start(bf16[2,256,2048]{2,1,0:T(8,128)(2,1)} %add_convert_fusion.refs_12_), channel_id=1, source_target_pairs={{4,0},{3,1},{6,2},{1,3},{0,4},{7,5},{2,6},{5,7},{12,8},{11,9},{14,... | collective-permute-start | bytes 6291464 | tf_op jit(solution)/shard_map/ppermute | solution.py:80
  720.9 68.4 %collective-permute-start.38 = (bf16[1,512,2048]{2,1,0:T(8,128)(2,1)}, bf16[1,512,2048]{2,1,0:T(8,128)(2,1)}, u32[]{:S(2)}, u32[]{:S(2)}) collective-permute-start(bf16[1,512,2048]{2,1,0:T(8,128)(2,1)} %block_product.23.refs_11_), channel_id=1, source_target_pairs={{2,0},{5,1},{0,2},{7,3},{6,4},{1,5},{4,6},{3,7},{10,8},{13,9},{8,1... | collective-permute-start | bytes 6291464 | tf_op jit(solution)/shard_map/ppermute | solution.py:80
  722.4 66.9 %all-to-all-start.7 = ((bf16[8,64,1536]{2,1,0:T(8,128)(2,1)}), bf16[8,64,1536]{2,1,0:T(8,128)(2,1)S(1)}, u32[]{:S(2)}, u32[]{:S(2)}) async-start(bf16[8,64,1536]{2,1,0:T(8,128)(2,1)} %bitcast.70), calls=%async_computation.10 | async-start | bytes 3145728 | tf_op jit(solution)/shard_map/all_to_all | solution.py:752
  726.0 140.2 %reduce-scatter.12.cloned.1.call-start = ((), (), s32[]{:S(2)}) async-start(), calls=%async_computation.21 | async-start | bytes 1966080 | tf_op jit(solution)/shard_map/reduce_scatter | solution.py:936
  850.1 65.0 %collective-permute-start.46 = (bf16[1,512,2048]{2,1,0:T(8,128)(2,1)}, bf16[1,512,2048]{2,1,0:T(8,128)(2,1)}, u32[]{:S(2)}, u32[]{:S(2)}) collective-permute-start(bf16[1,512,2048]{2,1,0:T(8,128)(2,1)} %block_product.28), channel_id=1, source_target_pairs={{2,0},{5,1},{0,2},{7,3},{6,4},{1,5},{4,6},{3,7},{10,8},{13,9},{8,1... | collective-permute-start | bytes 6291464 | tf_op jit(solution)/shard_map/ppermute | solution.py:80
  853.5 61.6 %collective-permute-start.45 = (bf16[1,512,2048]{2,1,0:T(8,128)(2,1)}, bf16[1,512,2048]{2,1,0:T(8,128)(2,1)}, u32[]{:S(2)}, u32[]{:S(2)}) collective-permute-start(bf16[1,512,2048]{2,1,0:T(8,128)(2,1)} %held.49), channel_id=1, source_target_pairs={{4,0},{3,1},{6,2},{1,3},{0,4},{7,5},{2,6},{5,7},{12,8},{11,9},{14,... | collective-permute-start | bytes 6291464 | tf_op jit(solution)/shard_map/ppermute | solution.py:80
  866.1 77.8 %reduce-scatter.14.cloned.1.call-start = ((), (), s32[]{:S(2)}) async-start(), calls=%async_computation.22 | async-start | bytes 1310720 | tf_op jit(solution)/shard_map/reduce_scatter | solution.py:943
  (87 other events, 1463.3 us)
Sparse Core Ops, SparseCore 0:
  121.5 73.6 all-gather.4
  197.1 77.0 all-gather.2
  551.7 108.2 reduce-scatter.9
  662.2 60.7 reduce-scatter.7
  725.7 35.2 reduce-scatter.5
  832.9 32.5 reduce-scatter.11
  869.2 25.7 reduce-scatter.13

commit v5 on v4

--- a/solution.py
+++ b/solution.py
@@ -223,6 +223,36 @@
         return values if apart else values[0]
 
     return product
+
+
+def part_kernel(table_ref, sum_ref, *refs):
+    total = sum_ref[...].astype(f32)
+    for ref in refs[:-1]:
+        total += ref[...].astype(f32)
+    refs[-1][...] = total.astype(refs[-1].dtype)
+
+
+def parts_of(sums, order):
+    rows = sums.shape[1]
+
+    def part(start, stop, addends, dtype, deps=()):
+        def block(at):
+            return pl.BlockSpec((1, rows, D), lambda b, t: (at + b, 0, 0))
+
+        return launch(
+            part_kernel,
+            [order, sums, *(value for value, _ in addends)],
+            [pl.BlockSpec((1, rows, D), lambda b, t: (t[start + b], 0, 0))] + [block(at) for _, at in addends],
+            [shape_of((stop - start, rows, D), dtype)],
+            [block(0)],
+            grid=(stop - start,),
+            prefetch=1,
+            deps=deps,
+            cost=((stop - start) * rows * D, (stop - start) * rows * D * 4, 0),
+            name="part",
+        )[0]
+
+    return part
 
 
 def norm_kernel(x_ref, gain_ref, shift_ref, *rest):
@@ -273,21 +303,20 @@
     )[0]
 
 
-def join_joint_kernel(n_sp, groups, group, *refs):
-    out_ref = refs[-1]
+def join_joint_kernel(n_sp, groups, group, in_ref, out_ref):
     for j in range(n_sp):
         for g in range(groups):
             for m in range(3):
                 start = m * D + (j * groups + g) * group
-                out_ref[:, start : start + group] = refs[g][j, :, m * group : (m + 1) * group].astype(f32)
-
-
-def join_joint(parts, n_sp):
-    groups = len(parts)
-    depth = parts[0].shape[1]
+                to = (g * 3 + m) * group
+                out_ref[:, start : start + group] = in_ref[j, :, to : to + group].astype(f32)
+
+
+def join_joint(value, groups):
+    n_sp, depth, width = value.shape
     return launch(
-        functools.partial(join_joint_kernel, n_sp, groups, parts[0].shape[2] // 3),
-        parts, [whole(p.shape) for p in parts], [shape_of((depth, 3 * D), f32)], [whole((depth, 3 * D))],
+        functools.partial(join_joint_kernel, n_sp, groups, width // 3 // groups),
+        [value], [whole(value.shape)], [shape_of((depth, 3 * D), f32)], [whole((depth, 3 * D))],
         grid=(1,), cost=(0, depth * D * 18, 0), name="join_joint",
     )[0]
 
@@ -904,13 +933,6 @@
     dos = [swap_sp(part).reshape(n_sp * span, group) for part in parts]
     out_sum = dot(attended_all, branch_grad, TN).astype(bf16).reshape(n_sp, n_z * depth, D)
 
-    def out_weight_part(start, stop, addends, dtype, deps=()):
-        parts = [lax.dynamic_index_in_dim(out_sum, order[b], 0, False) for b in range(start, stop)]
-        total = jnp.stack(parts).astype(f32)
-        for addend, at in addends:
-            total += addend[at : at + stop - start].astype(f32)
-        return total.astype(dtype)
-
     out_sums, out_theirs = plane.reduce_sums(out_product, branch_grad)
     out_got = plane.reduce_leg(out_sums)
     rows = attend_back(place, *heads[:3], dos[0], *results[0], tables, span, out_sums)
@@ -918,6 +940,7 @@
     joint_sums = [dot(normed, rows, TN).astype(bf16)]
     joint_parts = [lax.psum_scatter(joint_sums[0], "fsdp", scatter_dimension=0, tiled=True)]
     out_one, out_last = plane.reduce_next(out_product, out_got, out_theirs)
+    out_weight_part = parts_of(out_sum, order)
     weight_sums, weight_theirs = plane.reduce_sums(out_weight_part)
     weight_got = plane.reduce_leg(weight_sums)
     gate_up_own = swap_sp(gate_up_part)
@@ -934,7 +957,6 @@
     for g in range(1, groups):
         joint_sums.append(dot(last_normed, joint_rows[g], TN).astype(bf16))
         joint_parts.append(lax.psum_scatter(joint_sums[g], "fsdp", scatter_dimension=0, tiled=True))
-    joint_own = [swap_sp(j).reshape(n_sp, depth, 3 * group) for j in joint_parts]
     normed_one, normed_last = plane.legs_next(
         normed_product, further, normed_theirs, joint_sums
     )
@@ -946,12 +968,12 @@
     bias_sum = jnp.stack([jnp.sum(r.astype(f32), axis=0).reshape(3, group) for r in joint_rows], 1)
     bias_sum = bias_sum.reshape(3, 1, width)
     bias_sum = lax.dynamic_update_slice(jnp.zeros((3, n_sp, width), f32), bias_sum, (0, me, 0))
-    fill = (output, out_own, gate_grad, up_grad, bias_sum)
+    joint_own = jnp.concatenate(joint_parts, axis=1)
+    joint_grad = join_joint(swap_sp(joint_own).reshape(n_sp, depth, 3 * width), groups)
+    fill = (output, out_own, gate_grad, up_grad, bias_sum, joint_grad)
     normed_grad = plane.legs_own(normed_product, nearer, normed_theirs, normed_last, fill)
     tokens_grad, one_sums = norm_back(normed_grad, x, gain_one, middle_grad)
     tokens_grad = tokens_grad.reshape(tokens.shape)
-
-    joint_grad = join_joint(joint_own, n_sp)
 
     sums = [one_sums[0], one_sums[1], two_sums[0], two_sums[1]]
     sums = jnp.concatenate([s.reshape(n_all, n_gain) for s in sums] + [bias_sum.reshape(n_all, -1)], axis=1)

time: 962 us -> 947 us (0.984)
  Pallas kernels: 509 us -> 528 us
  between operations: 30.3 us -> 15.2 us
  other arithmetic: 25 us -> 11.5 us
    pallas_call x64 -> x69, Pallas kernels: 488 us -> 506 us  [launch(): pl.pallas_call(body, grid_spec=pltpu.PrefetchScalarGridSpec(num_scalar_pr...]
    all_to_all x9 -> x8, waiting for transfers between devices: 26.6 us -> 22.6 us  [swap_sp(): return lax.all_to_all(value, 'sp', split_axis=0, concat_axis=0, tiled=True)]
    all_to_all x9 -> x8, starting transfers between devices: 34.1 us -> 31.7 us  [swap_sp(): return lax.all_to_all(value, 'sp', split_axis=0, concat_axis=0, tiled=True)]
    unnamed x95 -> x93, local copies, waits for them, and re-layouts: 26.6 us -> 27.8 us
  transfers between devices with their start and end apart: 66 -> 65, of which waited for: 22 -> 23; matrix products, arithmetic and copies ran while one was open for 16% -> 14% of each run, Pallas kernels for 46% -> 49%
where the time goes in v5:
time: 947 us; the launch traced here: 938 us
  Pallas kernels  528 us (56%)
  waiting for transfers between devices  159 us (17%)
  matrix products  89.9 us (9%)
  starting transfers between devices  77.4 us (8%)
  local copies, waits for them, and re-layouts  56.9 us (6%)
  between operations  15.2 us (2%)
  other arithmetic  11.5 us (1%)
    pallas_call x69, Pallas kernels, launch(): pl.pallas_call(body, grid_spec=pltpu.PrefetchScalarGridSpec(num_scalar_pr...  506 us
    dot_general x5, matrix products, dot(): return lax.dot_general(a, b, dims, preferred_element_type=f32)  89.9 us
    ppermute x29, waiting for transfers between devices, send(): return lax.ppermute(value, 'sp', perm)  37 us
    all_to_all x8, starting transfers between devices, swap_sp(): return lax.all_to_all(value, 'sp', split_axis=0, concat_axis=0, tiled=True)  31.7 us
    ppermute x3, waiting for transfers between devices, per_device(): joint_blocks.append(lax.ppermute(joint_blocks[-1], 'fsdp', ring))  27.9 us
    unnamed x93, local copies, waits for them, and re-layouts  27.8 us
    ppermute x10, waiting for transfers between devices, back(): return lax.ppermute(value, 'sp', [(b, a) for a, b in perm])  23.3 us
    all_to_all x8, waiting for transfers between devices, swap_sp(): return lax.all_to_all(value, 'sp', split_axis=0, concat_axis=0, tiled=True)  22.6 us
  transfers between devices with their start and end apart: 65, of which 23 were waited for; matrix products, arithmetic and copies ran while one was open for 14% of the time, Pallas kernels for 49%

profile of v5, /device:TPU:0, one launch (start us, length us, event | category | flops | bytes accessed | tf_op | source)
XLA Modules:
  0.0 937.5 jit_solution(1197284876868215976)
XLA Ops:
  40.2 19.0 %collective-permute-done.5.refs_2_ = bf16[512,768]{1,0:T(8,128)(2,1)} collective-permute-done((bf16[512,768]{1,0:T(8,128)(2,1)}, bf16[512,768]{1,0:T(8,128)(2,1)}, u32[]{:S(2)}, u32[]{:S(2)}) %collective-permute-start.5) | collective-permute-done | bytes 786464 | tf_op jit(solution)/shard_map/ppermute | solution.py:837
  138.2 21.4 %joint_projection.1 = (bf16[4096,128]{1,0:T(8,128)(2,1)}, bf16[4096,128]{1,0:T(8,128)(2,1)}, bf16[4096,128]{1,0:T(8,128)(2,1)}, bf16[4096,128]{1,0:T(8,128)(2,1)...) custom-call(s32[8]{0:T(128)} %fusion.1.table_ref.refs_0_, bf16[4096,2048]{1,0:T(8,128)(2,1)} %first_norm.15.x_ref.refs_0_, ...), custom_call_target="tpu_custom_call" | custom-call | flops 12884901888 | bytes 23068672 | tf_op jit(solution)/shard_map/joint_projection/pallas_call | solution.py:489
  164.2 42.2 %attend.2 = (bf16[4096,128]{1,0:T(8,128)(2,1)}, f32[8,4096]{1,0:T(8,128)}) custom-call(bf16[4096,128]{1,0:T(8,128)(2,1)} %get-tuple-element.55.refs_0_.refs_1_, bf16[4096,128]{1,0:T(8,128)(2,1)} %get-tuple-element.56.refs_1_.refs_2_, bf16[4096,128]{1,0:T(8,128)(2,1)} %get-tuple-element.57.refs_2_.refs_3_), custom_call_target="tpu_custom_call" | custom-call | flops 17179869184 | bytes 4194304 | tf_op jit(solution)/shard_map/attend/pallas_call | solution.py:143
  219.1 42.2 %attend.3 = (bf16[4096,128]{1,0:T(8,128)(2,1)}, f32[8,4096]{1,0:T(8,128)}) custom-call(bf16[4096,128]{1,0:T(8,128)(2,1)} %get-tuple-element.59.refs_0_.refs_1_, bf16[4096,128]{1,0:T(8,128)(2,1)} %get-tuple-element.60.refs_1_.refs_2_, bf16[4096,128]{1,0:T(8,128)(2,1)} %get-tuple-element.61.refs_2_.refs_3_, bf16[512,2048]{1,0:T(8,128)(2,1)} %collective-permute-done.13.refs_3_, ...), custom_call_target="tpu_custom_call" | custom-call | flops 17179869184 | bytes 4194304 | tf_op jit(solution)/shard_map/attend/pallas_call | solution.py:143
  263.8 12.6 %collective-permute-done.17.refs_1_.refs_2_ = bf16[512,2048]{1,0:T(8,128)(2,1)} collective-permute-done((bf16[512,2048]{1,0:T(8,128)(2,1)}, bf16[512,2048]{1,0:T(8,128)(2,1)}, u32[]{:S(2)}, u32[]{:S(2)}) %collective-permute-start.17) | collective-permute-done | bytes 2097184 | tf_op jit(solution)/shard_map/ppermute | solution.py:76
  288.5 11.9 %collective-permute-done.19 = bf16[512,1536]{1,0:T(8,128)(2,1)} collective-permute-done((bf16[512,1536]{1,0:T(8,128)(2,1)}, bf16[512,1536]{1,0:T(8,128)(2,1)}, u32[]{:S(2)}, u32[]{:S(2)}) %collective-permute-start.19) | collective-permute-done | bytes 1572896 | tf_op jit(solution)/shard_map/ppermute | solution.py:883
  304.1 12.5 %middle.1 = (f32[512,2048]{1,0:T(8,128)}, bf16[512,2048]{1,0:T(8,128)(2,1)}, bf16[512,2048]{1,0:T(8,128)(2,1)}, bf16[512,2048]{1,0:T(8,128)(2,1)}) custom-call(bf16[8,512,128]{2,1,0:T(8,128)(2,1)} %all-to-all-done.2.refs_0_, bf16[8,512,128]{2,1,0:T(8,128)(2,1)} %copy-done.19, bf16[2048,2048]{1,0:T(8,128)(2,1)} %all-gather.3.cloned.1.call-done.refs_2_.refs_4_, ...), custom_call_target="tpu_custom_call" | custom-call | flops 4294967296 | bytes 20971520 | tf_op jit(solution)/shard_map/middle/pallas_call | solution.py:143
  321.1 18.0 %feed_forward.4 = (bf16[4096,768]{1,0:T(8,128)(2,1)}, bf16[4096,1536]{1,0:T(8,128)(2,1)}, bf16[4096,2048]{1,0:T(8,128)(2,1)}, bf16[4096,2048]{1,0:T(8,128)(2,1)}) custom-call(bf16[512,2048]{1,0:T(8,128)(2,1)} %get-tuple-element.66.refs_0_, bf16[512,2048]{1,0:T(8,128)(2,1)} %collective-permute-done.21.refs_1_, bf16[512,2048]{1,0:T(8,128)(2,1)} %held.32.refs_2_.refs_3_, ...), custom_call_target="tpu_custom_call" | custom-call | flops 9663676416 | bytes 26214400 | tf_op jit(solution)/shard_map/feed_forward/pallas_call | solution.py:143
  348.7 18.0 %feed_forward.5 = (bf16[4096,768]{1,0:T(8,128)(2,1)}, bf16[4096,1536]{1,0:T(8,128)(2,1)}, bf16[4096,2048]{1,0:T(8,128)(2,1)}, bf16[4096,2048]{1,0:T(8,128)(2,1)}) custom-call(bf16[512,2048]{1,0:T(8,128)(2,1)} %held.39.refs_1_.refs_0_, ...), custom_call_target="tpu_custom_call", output_to_operand_aliasing={{0}: (6, {}), {1}: (7, {}), {2}: (8, {}), {3}: (9, {})} | custom-call | flops 9663676416 | bytes 26214400 | tf_op jit(solution)/shard_map/feed_forward/pallas_call | solution.py:143
  376.4 18.0 %feed_forward.6 = (bf16[4096,768]{1,0:T(8,128)(2,1)}, bf16[4096,1536]{1,0:T(8,128)(2,1)}, bf16[4096,2048]{1,0:T(8,128)(2,1)}, bf16[4096,2048]{1,0:T(8,128)(2,1)}) custom-call(bf16[512,2048]{1,0:T(8,128)(2,1)} %held.41.refs_1_.refs_0_, ...), custom_call_target="tpu_custom_call", output_to_operand_aliasing={{0}: (6, {}), {1}: (7, {}), {2}: (8, {}), {3}: (9, {})} | custom-call | flops 9663676416 | bytes 26214400 | tf_op jit(solution)/shard_map/feed_forward/pallas_call | solution.py:143
  405.2 18.2 %feed_forward.7 = (bf16[4096,768]{1,0:T(8,128)(2,1)}, bf16[4096,1536]{1,0:T(8,128)(2,1)}, bf16[4096,2048]{1,0:T(8,128)(2,1)}, bf16[4096,2048]{1,0:T(8,128)(2,1)}) custom-call(bf16[512,2048]{1,0:T(8,128)(2,1)} %held.43.refs_0_, bf16[512,2048]{1,0:T(8,128)(2,1)} %copy-done.27, ...), custom_call_target="tpu_custom_call", output_to_operand_aliasing={{0}: (6, {}), {1}: (7, {}), {2}: (8, {}), {3}: (9, {})} | custom-call | flops 9663676416 | bytes 26214400 | tf_op jit(solution)/shard_map/feed_forward/pallas_call | solution.py:143
  423.4 10.8 %block_product.15.refs_2_ = bf16[2,512,2048]{2,1,0:T(8,128)(2,1)} custom-call(bf16[4096,1536]{1,0:T(8,128)(2,1)} %get-tuple-element.81.refs_0_, bf16[2048,1536]{1,0:T(8,128)(2,1)} %constant_dynamic-update-slice_fusion.refs_6_.refs_4_.refs_1_), custom_call_target="tpu_custom_call" | custom-call | flops 6442450944 | bytes 17825792 | tf_op jit(solution)/shard_map/block_product/pallas_call | solution.py:143
  434.3 10.8 %block_product.16.refs_3_ = bf16[2,512,2048]{2,1,0:T(8,128)(2,1)} custom-call(bf16[4096,1536]{1,0:T(8,128)(2,1)} %get-tuple-element.81.refs_0_, bf16[2048,1536]{1,0:T(8,128)(2,1)} %constant_dynamic-update-slice_fusion.refs_6_.refs_4_.refs_1_, bf16[2,512,2048]{2,1,0:T(8,128)(2,1)} %block_product.15.refs_2_), custom_call_target="tpu_custom_call" | custom-call | flops 6442450944 | bytes 17825792 | tf_op jit(solution)/shard_map/block_product/pallas_call | solution.py:143
  445.4 11.1 %block_product.17 = (bf16[1,512,2048]{2,1,0:T(8,128)(2,1)}, bf16[1,512,2048]{2,1,0:T(8,128)(2,1)}) custom-call(bf16[4096,1536]{1,0:T(8,128)(2,1)} %get-tuple-element.81.refs_0_, bf16[2048,1536]{1,0:T(8,128)(2,1)} %constant_dynamic-update-slice_fusion.refs_6_.refs_4_.refs_1_, bf16[2,512,2048]{2,1,0:T(8,128)(2,1)} %collective-permute-done.31.refs_2_, ...), custom_call_target="tpu_custom_call" | custom-call | flops 6442450944 | bytes 17825792 | tf_op jit(solution)/shard_map/block_product/pallas_call | solution.py:143
  458.0 19.9 %convolution_convert_fusion.2.refs_4_.refs_0_ = bf16[768,2048]{1,0:T(8,128)(2,1)} fusion(bf16[4096,768]{1,0:T(8,128)(2,1)} %get-tuple-element.80.refs_0_, bf16[4096,2048]{1,0:T(8,128)(2,1)} %held.45), kind=kOutput, calls=%fused_computation.6 | convolution fusion | flops 12886474752 | bytes 26214400 | tf_op jit(solution)/shard_map/dot_general | solution.py:28
  494.9 34.0 %convolution_convert_fusion.1.refs_5_.refs_0_ = bf16[2048,1536]{1,0:T(8,128)(2,1)} fusion(bf16[4096,2048]{1,0:T(8,128)(2,1)} %held.46, bf16[4096,1536]{1,0:T(8,128)(2,1)} %get-tuple-element.81.refs_0_), kind=kOutput, calls=%fused_computation.1 | convolution fusion | flops 25772949504 | bytes 35651584 | tf_op jit(solution)/shard_map/dot_general | solution.py:28
  528.9 12.3 %collective-permute-done.34.refs_4_ = bf16[1,512,2048]{2,1,0:T(8,128)(2,1)S(1)} collective-permute-done((bf16[1,512,2048]{2,1,0:T(8,128)(2,1)}, bf16[1,512,2048]{2,1,0:T(8,128)(2,1)S(1)}, u32[]{:S(2)}, u32[]{:S(2)}) %collective-permute-start.34) | collective-permute-done | bytes 2097184 | tf_op jit(solution)/shard_map/ppermute | solution.py:80
  542.5 9.0 block_product.19
  551.5 16.6 %norm_back.2 = (f32[512,2048]{1,0:T(8,128)}, f32[8,2048]{1,0:T(8,128)}, bf16[512,2048]{1,0:T(8,128)(2,1)}, bf16[8,512,128]{2,1,0:T(8,128)(2,1)}, bf16[8,512,128]{2,1,0:T(8,128)(2,1)}) custom-call(bf16[512,2048]{1,0:T(8,128)(2,1)} %bitcast.56, f32[512,2048]{1,0:T(8,128)} %get-tuple-element.65.refs_1_, f32[1,2048]{1,0:T(1,128)} %reshape.112.refs_4_.refs_2_, ...), custom_call_target="tpu_custom_call" | custom-call | flops 4315938816 | bytes 25165824 | tf_op jit(solution)/shard_map/norm_back/pallas_call | solution.py:143
  618.1 62.8 %attend_back.2.refs_0_ = bf16[4096,384]{1,0:T(8,128)(2,1)} custom-call(s32[8]{0:T(128)} %fusion.2.refs_0_, bf16[4096,128]{1,0:T(8,128)(2,1)} %get-tuple-element.55.refs_0_.refs_1_, bf16[4096,128]{1,0:T(8,128)(2,1)} %get-tuple-element.56.refs_1_.refs_2_, bf16[4096,128]{1,0:T(8,128)(2,1)} %get-tuple-element.57.refs_2_.refs_3_, bf16[4096,128]{1,0:T(8,128)(2,1)} %bitcast.66, ...), custom_call_target="tpu_custom_call" | custom-call | flops 25769803776 | bytes 8388608 | tf_op jit(solution)/shard_map/attend_back/pallas_call | solution.py:143
  680.8 14.2 %convolution_convert_fusion.4.refs_10_.refs_3_.refs_6_ = bf16[2048,384]{1,0:T(8,128)(2,1)} fusion(bf16[4096,2048]{1,0:T(8,128)(2,1)} %first_norm.15.x_ref.refs_0_, bf16[4096,384]{1,0:T(8,128)(2,1)} %attend_back.2.refs_0_), kind=kOutput, calls=%fused_computation.8 | convolution fusion | flops 6443237376 | bytes 21495808 | tf_op jit(solution)/shard_map/dot_general | solution.py:28
  714.9 62.8 %attend_back.3.refs_1_ = bf16[4096,384]{1,0:T(8,128)(2,1)} custom-call(s32[8]{0:T(128)} %fusion.2.refs_0_, bf16[4096,128]{1,0:T(8,128)(2,1)} %get-tuple-element.59.refs_0_.refs_1_, bf16[4096,128]{1,0:T(8,128)(2,1)} %get-tuple-element.60.refs_1_.refs_2_, bf16[4096,128]{1,0:T(8,128)(2,1)} %get-tuple-element.61.refs_2_.refs_3_, bf16[4096,128]{1,0:T(8,128)(2,1)} %bitcast.65, ...), custom_call_target="tpu_custom_call" | custom-call | flops 25769803776 | bytes 8388608 | tf_op jit(solution)/shard_map/attend_back/pallas_call | solution.py:143
  808.2 13.3 %convolution_convert_fusion.3.refs_7_ = bf16[2048,384]{1,0:T(8,128)(2,1)} fusion(bf16[4096,2048]{1,0:T(8,128)(2,1)} %held.50, bf16[4096,384]{1,0:T(8,128)(2,1)S(1)} %copy-done.2), kind=kOutput, calls=%fused_computation.7 | convolution fusion | flops 6443237376 | bytes 21495808 | tf_op jit(solution)/shard_map/dot_general | solution.py:28
  875.6 21.5 %all-to-all-done.8.refs_0_ = bf16[8,64,768]{2,1,0:T(8,128)(2,1)S(1)} async-done(((bf16[8,64,768]{2,1,0:T(8,128)(2,1)}), bf16[8,64,768]{2,1,0:T(8,128)(2,1)S(1)}, u32[]{:S(2)}, u32[]{:S(2)}) %all-to-all-start.8) | async-done | bytes 786464 | tf_op jit(solution)/shard_map/all_to_all | solution.py:781
  (336 shorter events, 389.2 us)
Async XLA Ops:
  19.5 64.8 %collective-permute-start.1 = (bf16[512,2048]{1,0:T(8,128)(2,1)S(1)}, bf16[512,2048]{1,0:T(8,128)(2,1)}, u32[]{:S(2)}, u32[]{:S(2)}) collective-permute-start(bf16[512,2048]{1,0:T(8,128)(2,1)S(1)} %bitcast.52), channel_id=1, source_target_pairs={{0,1},{1,0},{2,3},{3,2},{4,5},{5,4},{6,7},{7,6},{8,9},{9,8},{10,11... | collective-permute-start | bytes 6291464 | tf_op jit(solution)/shard_map/ppermute | solution.py:76
  22.1 65.8 %collective-permute-start = (bf16[512,2048]{1,0:T(8,128)(2,1)S(1)}, bf16[512,2048]{1,0:T(8,128)(2,1)}, u32[]{:S(2)}, u32[]{:S(2)}) collective-permute-start(bf16[512,2048]{1,0:T(8,128)(2,1)S(1)} %bitcast.53), channel_id=1, source_target_pairs={{0,2},{1,5},{2,0},{3,7},{4,6},{5,1},{6,4},{7,3},{8,10},{9,13},{10,... | collective-permute-start | bytes 6291464 | tf_op jit(solution)/shard_map/ppermute | solution.py:76
  23.6 65.3 %collective-permute-start.8 = (bf16[512,2048]{1,0:T(8,128)(2,1)S(1)}, bf16[512,2048]{1,0:T(8,128)(2,1)}, u32[]{:S(2)}, u32[]{:S(2)}) collective-permute-start(bf16[512,2048]{1,0:T(8,128)(2,1)S(1)} %bitcast.54), channel_id=1, source_target_pairs={{0,4},{1,3},{2,6},{3,1},{4,0},{5,7},{6,2},{7,5},{8,12},{9,11},{10,... | collective-permute-start | bytes 6291464 | tf_op jit(solution)/shard_map/ppermute | solution.py:76
  66.6 236.5 %all-gather.5.cloned.1.call-start = ((), (), s32[]{:S(2)}) async-start(), calls=%async_computation.16 | async-start | bytes 3932160 | tf_op jit(solution)/shard_map/all_gather | solution.py:869
  121.3 181.8 %all-gather.3.cloned.1.call-start = ((), (), s32[]{:S(2)}) async-start(), calls=%async_computation.15 | async-start | bytes 9437184 | tf_op jit(solution)/shard_map/all_gather | solution.py:868
  160.7 56.8 %collective-permute-start.14 = (bf16[512,2048]{1,0:T(8,128)(2,1)}, bf16[512,2048]{1,0:T(8,128)(2,1)}, u32[]{:S(2)}, u32[]{:S(2)}) collective-permute-start(bf16[512,2048]{1,0:T(8,128)(2,1)} %held.32.refs_2_.refs_3_), channel_id=1, source_target_pairs={{0,2},{1,5},{2,0},{3,7},{4,6},{5,1},{6,4},{7,3},{8,10},{9,13},{10,... | collective-permute-start | bytes 6291464 | tf_op jit(solution)/shard_map/ppermute | solution.py:76
  162.7 56.3 %collective-permute-start.13 = (bf16[512,2048]{1,0:T(8,128)(2,1)}, bf16[512,2048]{1,0:T(8,128)(2,1)}, u32[]{:S(2)}, u32[]{:S(2)}) collective-permute-start(bf16[512,2048]{1,0:T(8,128)(2,1)} %held.32.refs_2_.refs_3_), channel_id=1, source_target_pairs={{0,1},{1,0},{2,3},{3,2},{4,5},{5,4},{6,7},{7,6},{8,9},{9,8},{10,11... | collective-permute-start | bytes 6291464 | tf_op jit(solution)/shard_map/ppermute | solution.py:76
  206.5 70.0 %all-to-all-start.2 = ((bf16[8,512,128]{2,1,0:T(8,128)(2,1)}), bf16[8,512,128]{2,1,0:T(8,128)(2,1)}, u32[]{:S(2)}, u32[]{:S(2)}) async-start(bf16[8,512,128]{2,1,0:T(8,128)(2,1)} %bitcast.64), calls=%async_computation.2 | async-start | bytes 2097152 | tf_op jit(solution)/shard_map/all_to_all | solution.py:781
  217.5 59.0 %collective-permute-start.17 = (bf16[512,2048]{1,0:T(8,128)(2,1)}, bf16[512,2048]{1,0:T(8,128)(2,1)}, u32[]{:S(2)}, u32[]{:S(2)}) collective-permute-start(bf16[512,2048]{1,0:T(8,128)(2,1)} %held.33.refs_4_.refs_2_), channel_id=1, source_target_pairs={{0,4},{1,3},{2,6},{3,1},{4,0},{5,7},{6,2},{7,5},{8,12},{9,11},{10,... | collective-permute-start | bytes 6291464 | tf_op jit(solution)/shard_map/ppermute | solution.py:76
  280.9 429.4 %reduce-scatter.10.cloned.1.call-start = ((), (), s32[]{:S(2)}) async-start(), calls=%async_computation.19 | async-start | bytes 7864320 | tf_op jit(solution)/shard_map/reduce_scatter | solution.py:929
  551.5 226.3 %reduce-scatter.8.cloned.1.call-start = ((), (), s32[]{:S(2)}) async-start(), calls=%async_computation.18 | async-start | bytes 3932160 | tf_op jit(solution)/shard_map/reduce_scatter | solution.py:927
  592.3 102.8 %collective-permute-start.39 = (bf16[2,256,2048]{2,1,0:T(8,128)(2,1)}, bf16[2,256,2048]{2,1,0:T(8,128)(2,1)S(1)}, u32[]{:S(2)}, u32[]{:S(2)}) collective-permute-start(bf16[2,256,2048]{2,1,0:T(8,128)(2,1)} %part.5.refs_2_), channel_id=1, source_target_pairs={{0,1},{1,0},{2,3},{3,2},{4,5},{5,4},{6,7},{7,6},{8,9},{9,8},{10,11... | collective-permute-start | bytes 6291464 | tf_op jit(solution)/shard_map/ppermute | solution.py:76
  596.1 118.8 %collective-permute-start.40 = (bf16[2,256,2048]{2,1,0:T(8,128)(2,1)}, bf16[2,256,2048]{2,1,0:T(8,128)(2,1)}, u32[]{:S(2)}, u32[]{:S(2)}) collective-permute-start(bf16[2,256,2048]{2,1,0:T(8,128)(2,1)} %part.6.refs_3_), channel_id=1, source_target_pairs={{0,1},{1,0},{2,3},{3,2},{4,5},{5,4},{6,7},{7,6},{8,9},{9,8},{10,11... | collective-permute-start | bytes 6291464 | tf_op jit(solution)/shard_map/ppermute | solution.py:76
  603.4 99.1 %collective-permute-start.35 = (bf16[2,512,2048]{2,1,0:T(8,128)(2,1)}, bf16[2,512,2048]{2,1,0:T(8,128)(2,1)}, u32[]{:S(2)}, u32[]{:S(2)}) collective-permute-start(bf16[2,512,2048]{2,1,0:T(8,128)(2,1)} %block_product.21.refs_3_), channel_id=1, source_target_pairs={{0,1},{1,0},{2,3},{3,2},{4,5},{5,4},{6,7},{7,6},{8,9},{9,8},{10,11... | collective-permute-start | bytes 12582920 | tf_op jit(solution)/shard_map/ppermute | solution.py:76
  611.8 90.6 %collective-permute-start.37 = (bf16[2,512,2048]{2,1,0:T(8,128)(2,1)}, bf16[2,512,2048]{2,1,0:T(8,128)(2,1)}, u32[]{:S(2)}, u32[]{:S(2)}) collective-permute-start(bf16[2,512,2048]{2,1,0:T(8,128)(2,1)} %block_product.22.refs_10_), channel_id=1, source_target_pairs={{4,0},{3,1},{6,2},{1,3},{0,4},{7,5},{2,6},{5,7},{12,8},{11,9},{14,... | collective-permute-start | bytes 12582920 | tf_op jit(solution)/shard_map/ppermute | solution.py:80
  614.5 95.9 %all-to-all-start.6 = ((bf16[8,512,128]{2,1,0:T(8,128)(2,1)}), bf16[8,512,128]{2,1,0:T(8,128)(2,1)S(1)}, u32[]{:S(2)}, u32[]{:S(2)}) async-start(bf16[8,512,128]{2,1,0:T(8,128)(2,1)} %get-tuple-element.88), calls=%async_computation.6 | async-start | bytes 2097152 | tf_op jit(solution)/shard_map/all_to_all | solution.py:781
  618.0 159.8 %reduce-scatter.6.cloned.1.call-start = ((), (), s32[]{:S(2)}) async-start(), calls=%async_computation.17 | async-start | bytes 1966080 | tf_op jit(solution)/shard_map/reduce_scatter | solution.py:941
  700.5 77.3 %collective-permute-start.41 = (bf16[2,256,2048]{2,1,0:T(8,128)(2,1)}, bf16[2,256,2048]{2,1,0:T(8,128)(2,1)S(1)}, u32[]{:S(2)}, u32[]{:S(2)}) collective-permute-start(bf16[2,256,2048]{2,1,0:T(8,128)(2,1)} %part.7.refs_12_), channel_id=1, source_target_pairs={{4,0},{3,1},{6,2},{1,3},{0,4},{7,5},{2,6},{5,7},{12,8},{11,9},{14,... | collective-permute-start | bytes 6291464 | tf_op jit(solution)/shard_map/ppermute | solution.py:80
  708.9 68.9 %collective-permute-start.38 = (bf16[1,512,2048]{2,1,0:T(8,128)(2,1)}, bf16[1,512,2048]{2,1,0:T(8,128)(2,1)}, u32[]{:S(2)}, u32[]{:S(2)}) collective-permute-start(bf16[1,512,2048]{2,1,0:T(8,128)(2,1)} %block_product.23.refs_11_), channel_id=1, source_target_pairs={{2,0},{5,1},{0,2},{7,3},{6,4},{1,5},{4,6},{3,7},{10,8},{13,9},{8,1... | collective-permute-start | bytes 6291464 | tf_op jit(solution)/shard_map/ppermute | solution.py:80
  710.3 67.5 %all-to-all-start.7 = ((bf16[8,64,1536]{2,1,0:T(8,128)(2,1)}), bf16[8,64,1536]{2,1,0:T(8,128)(2,1)}, u32[]{:S(2)}, u32[]{:S(2)}) async-start(bf16[8,64,1536]{2,1,0:T(8,128)(2,1)} %bitcast.63), calls=%async_computation.10 | async-start | bytes 3145728 | tf_op jit(solution)/shard_map/all_to_all | solution.py:781
  714.9 139.5 %reduce-scatter.12.cloned.1.call-start = ((), (), s32[]{:S(2)}) async-start(), calls=%async_computation.20 | async-start | bytes 1966080 | tf_op jit(solution)/shard_map/reduce_scatter | solution.py:959
  821.6 106.9 %reduce-scatter.14.cloned.1.call-start = ((), (), s32[]{:S(2)}) async-start(), calls=%async_computation.21 | async-start | bytes 1310720 | tf_op jit(solution)/shard_map/reduce_scatter | solution.py:965
  840.1 60.4 %collective-permute-start.46 = (bf16[1,512,2048]{2,1,0:T(8,128)(2,1)}, bf16[1,512,2048]{2,1,0:T(8,128)(2,1)}, u32[]{:S(2)}, u32[]{:S(2)}) collective-permute-start(bf16[1,512,2048]{2,1,0:T(8,128)(2,1)} %block_product.28), channel_id=1, source_target_pairs={{2,0},{5,1},{0,2},{7,3},{6,4},{1,5},{4,6},{3,7},{10,8},{13,9},{8,1... | collective-permute-start | bytes 6291464 | tf_op jit(solution)/shard_map/ppermute | solution.py:80
  843.7 56.7 %collective-permute-start.45 = (bf16[1,512,2048]{2,1,0:T(8,128)(2,1)}, bf16[1,512,2048]{2,1,0:T(8,128)(2,1)}, u32[]{:S(2)}, u32[]{:S(2)}) collective-permute-start(bf16[1,512,2048]{2,1,0:T(8,128)(2,1)} %held.49), channel_id=1, source_target_pairs={{4,0},{3,1},{6,2},{1,3},{0,4},{7,5},{2,6},{5,7},{12,8},{11,9},{14,... | collective-permute-start | bytes 6291464 | tf_op jit(solution)/shard_map/ppermute | solution.py:80
  (85 other events, 1414.7 us)
Sparse Core Ops, SparseCore 0:
  121.5 73.8 all-gather.4
  197.2 76.9 all-gather.2
  551.6 108.2 reduce-scatter.9
  662.1 60.7 reduce-scatter.7
  725.6 35.3 reduce-scatter.5
  821.7 32.6 reduce-scatter.11
  856.7 26.1 reduce-scatter.13

commit v6 on v5

--- a/solution.py
+++ b/solution.py
@@ -321,7 +321,8 @@
     )[0]
 
 
-def cut_feed_kernel(n_sp, n_z, size, padded, gate_ref, up_ref, out_ref):
+def cut_feed_kernel(n_sp, n_z, size, padded, gate_ref, up_ref, beside_ref, out_ref, copy_ref):
+    copy_ref[...] = beside_ref[...]
     out_ref[...] = jnp.zeros_like(out_ref)
     for j in range(n_sp):
         for p, ref in enumerate((gate_ref, up_ref)):
@@ -331,15 +332,18 @@
                 out_ref[j, :, to : to + size] = ref[:, start : start + size]
 
 
-def cut_feed(gate_weight, up_weight, n_sp, n_z, padded, deps):
+def cut_feed(gate_weight, up_weight, beside, n_sp, n_z, padded):
     depth, total = gate_weight.shape
     size = total // (n_sp * n_z)
     shape = (n_sp, depth, 2 * n_z * padded)
     return launch(
         functools.partial(cut_feed_kernel, n_sp, n_z, size, padded),
-        [gate_weight, up_weight], [whole(gate_weight.shape)] * 2, [shape_of(shape, bf16)], [whole(shape)],
-        grid=(1,), cost=(0, gate_weight.size * 8, 0), name="cut_feed", deps=deps,
-    )[0]
+        [gate_weight, up_weight, beside],
+        [whole(gate_weight.shape)] * 2 + [whole(beside.shape)],
+        [shape_of(shape, bf16), shape_of(beside.shape, beside.dtype)],
+        [whole(shape), whole(beside.shape)],
+        grid=(1,), cost=(0, gate_weight.size * 8, 0), name="cut_feed",
+    )
 
 
 def join_feed_kernel(n_sp, n_z, size, padded, in_ref, gate_ref, up_ref):
@@ -393,7 +397,7 @@
             parts[g][j, :, columns] = full[:, place]
 
 
-def norm_back(grad, x, gain, beside, weight=None, depth=0, n_sp=0, groups=0):
+def norm_back(grad, x, gain, beside, weight=None, depth=0, n_sp=0, groups=0, deps=()):
     rows = x.shape[0]
     tile = min(256, rows)
     row = pl.BlockSpec((1, D), lambda i: (0, 0))
@@ -414,6 +418,7 @@
         out_specs,
         grid=(rows // tile,),
         cost=(rows * D * (20 + 2 * D * len(extra)), rows * D * 16 + 2 * D * D * len(extra), rows),
+        deps=deps,
         name="norm_back",
     )
 
@@ -472,13 +477,17 @@
 
 
 def joint_kernel(width, table_ref, x_ref, w_ref, bias_ref, cos_ref, up_ref, down_ref, *outs):
-    projected = dot(x_ref[...], w_ref[...], NN) + bias_ref[...]
-    tables = (cos_ref[...], up_ref[...], down_ref[...])
-    for g in range(len(outs) // 3):
-        part = projected[:, 3 * g * width : 3 * (g + 1) * width]
-        outs[3 * g][...] = turn(part[:, :width], *tables).astype(bf16)
-        outs[3 * g + 1][...] = turn(part[:, width : 2 * width], *tables).astype(bf16)
-        outs[3 * g + 2][...] = part[:, 2 * width :].astype(bf16)
+    rows = x_ref.shape[0]
+    tile = min(256, rows)
+    for start in range(0, rows, tile):
+        at = slice(start, start + tile)
+        projected = dot(x_ref[at], w_ref[...], NN) + bias_ref[...]
+        tables = (cos_ref[at], up_ref[at], down_ref[at])
+        for g in range(len(outs) // 3):
+            part = projected[:, 3 * g * width : 3 * (g + 1) * width]
+            outs[3 * g][at] = turn(part[:, :width], *tables).astype(bf16)
+            outs[3 * g + 1][at] = turn(part[:, width : 2 * width], *tables).astype(bf16)
+            outs[3 * g + 2][at] = part[:, 2 * width :].astype(bf16)
 
 
 def joint_projection(table, normed, weight, bias, tables, span, groups):
@@ -837,7 +846,7 @@
         joint_blocks.append(lax.ppermute(joint_blocks[-1], "fsdp", ring))
     joint_mine = in_line(joint_blocks, my_z)
 
-    gate_up_cols = cut_feed(gate_weight, up_weight, n_sp, n_z, ff_pad, ())
+    gate_up_cols, cot = cut_feed(gate_weight, up_weight, cotangent.reshape(span, D), n_sp, n_z, ff_pad)
     down_rows = jnp.pad(down_weight, ((0, ff_pad - ff_rows), (0, 0)))
     x = tokens.reshape(span, D)
     normed = None
@@ -848,7 +857,6 @@
     partner, one, twos = plane.gather_first(x)
     normed = norm_next(None, x, 0)
     normed = norm_next(normed, partner, half)
-    cot = held(cotangent.reshape(span, D), small_all)
     one = held(one, (normed, joint_blocks[1:3], gate_up_cols, cot))
     one_other, two_others, threes = plane.gather_second(one, twos)
     normed = norm_next(normed, one, 1)
@@ -969,10 +977,11 @@
     bias_sum = bias_sum.reshape(3, 1, width)
     bias_sum = lax.dynamic_update_slice(jnp.zeros((3, n_sp, width), f32), bias_sum, (0, me, 0))
     joint_own = jnp.concatenate(joint_parts, axis=1)
-    joint_grad = join_joint(swap_sp(joint_own).reshape(n_sp, depth, 3 * width), groups)
-    fill = (output, out_own, gate_grad, up_grad, bias_sum, joint_grad)
+    joint_own = swap_sp(joint_own).reshape(n_sp, depth, 3 * width)
+    fill = (output, out_own, gate_grad, up_grad, bias_sum)
     normed_grad = plane.legs_own(normed_product, nearer, normed_theirs, normed_last, fill)
-    tokens_grad, one_sums = norm_back(normed_grad, x, gain_one, middle_grad)
+    joint_grad = join_joint(held(joint_own, normed_grad), groups)
+    tokens_grad, one_sums = norm_back(normed_grad, x, gain_one, middle_grad, deps=joint_grad)
     tokens_grad = tokens_grad.reshape(tokens.shape)
 
     sums = [one_sums[0], one_sums[1], two_sums[0], two_sums[1]]

time: 947 us -> 938 us (level)
    all_to_all x8, waiting for transfers between devices: 22.6 us -> 1.06 us  [swap_sp(): return lax.all_to_all(value, 'sp', split_axis=0, concat_axis=0, tiled=True)]
    ppermute x10, waiting for transfers between devices: 23.3 us -> 38.4 us  [back(): return lax.ppermute(value, 'sp', [(b, a) for a, b in perm])]
    unnamed x93 -> x90, local copies, waits for them, and re-layouts: 27.8 us -> 25.3 us
  transfers between devices with their start and end apart: 65 -> 65, of which waited for: 23 -> 24; matrix products, arithmetic and copies ran while one was open for 14% -> 14% of each run, Pallas kernels for 49% -> 50%
where the time goes in v6:
time: 938 us; the launch traced here: 928 us
  Pallas kernels  528 us (56%)
  waiting for transfers between devices  153 us (16%)
  matrix products  89.9 us (10%)
  starting transfers between devices  77.4 us (8%)
  local copies, waits for them, and re-layouts  53.4 us (6%)
  between operations  15.3 us (2%)
  other arithmetic  11.5 us (1%)
    pallas_call x69, Pallas kernels, launch(): pl.pallas_call(body, grid_spec=pltpu.PrefetchScalarGridSpec(num_scalar_pr...  508 us
    dot_general x5, matrix products, dot(): return lax.dot_general(a, b, dims, preferred_element_type=f32)  89.9 us
    ppermute x10, waiting for transfers between devices, back(): return lax.ppermute(value, 'sp', [(b, a) for a, b in perm])  38.4 us
    ppermute x29, waiting for transfers between devices, send(): return lax.ppermute(value, 'sp', perm)  36.9 us
    all_to_all x8, starting transfers between devices, swap_sp(): return lax.all_to_all(value, 'sp', split_axis=0, concat_axis=0, tiled=True)  31 us
    ppermute x3, waiting for transfers between devices, per_device(): joint_blocks.append(lax.ppermute(joint_blocks[-1], 'fsdp', ring))  27.9 us
    unnamed x90, local copies, waits for them, and re-layouts  25.3 us
    pallas_call x1, Pallas kernels, joint_projection(): pl.pallas_call(functools.partial(joint_kernel, width), grid_spec=pltpu.Pr...  20.8 us
  transfers between devices with their start and end apart: 65, of which 24 were waited for; matrix products, arithmetic and copies ran while one was open for 14% of the time, Pallas kernels for 50%

profile of v6, /device:TPU:0, one launch (start us, length us, event | category | flops | bytes accessed | tf_op | source)
XLA Modules:
  0.0 928.5 jit_solution(2715100274527315344)
XLA Ops:
  37.0 19.0 %collective-permute-done.5.refs_2_ = bf16[512,768]{1,0:T(8,128)(2,1)} collective-permute-done((bf16[512,768]{1,0:T(8,128)(2,1)}, bf16[512,768]{1,0:T(8,128)(2,1)}, u32[]{:S(2)}, u32[]{:S(2)}) %collective-permute-start.5) | collective-permute-done | bytes 786464 | tf_op jit(solution)/shard_map/ppermute | solution.py:846
  134.7 20.8 %joint_projection.1 = (bf16[4096,128]{1,0:T(8,128)(2,1)}, bf16[4096,128]{1,0:T(8,128)(2,1)}, bf16[4096,128]{1,0:T(8,128)(2,1)}, bf16[4096,128]{1,0:T(8,128)(2,1)...) custom-call(s32[8]{0:T(128)} %fusion.1.table_ref.refs_0_, bf16[4096,2048]{1,0:T(8,128)(2,1)} %first_norm.15.x_ref.refs_0_, ...), custom_call_target="tpu_custom_call" | custom-call | flops 12884901888 | bytes 23068672 | tf_op jit(solution)/shard_map/joint_projection/pallas_call | solution.py:498
  160.2 42.2 %attend.2 = (bf16[4096,128]{1,0:T(8,128)(2,1)}, f32[8,4096]{1,0:T(8,128)}) custom-call(bf16[4096,128]{1,0:T(8,128)(2,1)} %get-tuple-element.59.refs_0_.refs_1_, bf16[4096,128]{1,0:T(8,128)(2,1)} %get-tuple-element.60.refs_1_.refs_2_, bf16[4096,128]{1,0:T(8,128)(2,1)} %get-tuple-element.61.refs_2_.refs_3_), custom_call_target="tpu_custom_call" | custom-call | flops 17179869184 | bytes 4194304 | tf_op jit(solution)/shard_map/attend/pallas_call | solution.py:143
  215.8 42.2 %attend.3 = (bf16[4096,128]{1,0:T(8,128)(2,1)}, f32[8,4096]{1,0:T(8,128)}) custom-call(bf16[4096,128]{1,0:T(8,128)(2,1)} %get-tuple-element.63.refs_0_.refs_1_, bf16[4096,128]{1,0:T(8,128)(2,1)} %get-tuple-element.64.refs_1_.refs_2_, bf16[4096,128]{1,0:T(8,128)(2,1)} %get-tuple-element.65.refs_2_.refs_3_, bf16[512,2048]{1,0:T(8,128)(2,1)} %collective-permute-done.13.refs_3_, ...), custom_call_target="tpu_custom_call" | custom-call | flops 17179869184 | bytes 4194304 | tf_op jit(solution)/shard_map/attend/pallas_call | solution.py:143
  260.5 12.5 %collective-permute-done.17.refs_1_.refs_2_ = bf16[512,2048]{1,0:T(8,128)(2,1)} collective-permute-done((bf16[512,2048]{1,0:T(8,128)(2,1)}, bf16[512,2048]{1,0:T(8,128)(2,1)}, u32[]{:S(2)}, u32[]{:S(2)}) %collective-permute-start.17) | collective-permute-done | bytes 2097184 | tf_op jit(solution)/shard_map/ppermute | solution.py:76
  284.5 12.7 %collective-permute-done.19 = bf16[512,1536]{1,0:T(8,128)(2,1)} collective-permute-done((bf16[512,1536]{1,0:T(8,128)(2,1)}, bf16[512,1536]{1,0:T(8,128)(2,1)}, u32[]{:S(2)}, u32[]{:S(2)}) %collective-permute-start.19) | collective-permute-done | bytes 1572896 | tf_op jit(solution)/shard_map/ppermute | solution.py:891
  300.8 12.5 %middle.1 = (f32[512,2048]{1,0:T(8,128)}, bf16[512,2048]{1,0:T(8,128)(2,1)}, bf16[512,2048]{1,0:T(8,128)(2,1)}, bf16[512,2048]{1,0:T(8,128)(2,1)}) custom-call(bf16[8,512,128]{2,1,0:T(8,128)(2,1)} %all-to-all-done.2.refs_0_, bf16[8,512,128]{2,1,0:T(8,128)(2,1)} %copy-done.20, bf16[2048,2048]{1,0:T(8,128)(2,1)} %all-gather.3.cloned.1.call-done.refs_2_.refs_4_, ...), custom_call_target="tpu_custom_call" | custom-call | flops 4294967296 | bytes 20971520 | tf_op jit(solution)/shard_map/middle/pallas_call | solution.py:143
  317.8 18.0 %feed_forward.4 = (bf16[4096,768]{1,0:T(8,128)(2,1)}, bf16[4096,1536]{1,0:T(8,128)(2,1)}, bf16[4096,2048]{1,0:T(8,128)(2,1)}, bf16[4096,2048]{1,0:T(8,128)(2,1)}) custom-call(bf16[512,2048]{1,0:T(8,128)(2,1)} %get-tuple-element.70.refs_0_, bf16[512,2048]{1,0:T(8,128)(2,1)} %collective-permute-done.21.refs_1_, bf16[512,2048]{1,0:T(8,128)(2,1)} %held.31.refs_2_.refs_3_, ...), custom_call_target="tpu_custom_call" | custom-call | flops 9663676416 | bytes 26214400 | tf_op jit(solution)/shard_map/feed_forward/pallas_call | solution.py:143
  345.4 18.0 %feed_forward.5 = (bf16[4096,768]{1,0:T(8,128)(2,1)}, bf16[4096,1536]{1,0:T(8,128)(2,1)}, bf16[4096,2048]{1,0:T(8,128)(2,1)}, bf16[4096,2048]{1,0:T(8,128)(2,1)}) custom-call(bf16[512,2048]{1,0:T(8,128)(2,1)} %held.38.refs_1_.refs_0_, ...), custom_call_target="tpu_custom_call", output_to_operand_aliasing={{0}: (6, {}), {1}: (7, {}), {2}: (8, {}), {3}: (9, {})} | custom-call | flops 9663676416 | bytes 26214400 | tf_op jit(solution)/shard_map/feed_forward/pallas_call | solution.py:143
  373.1 18.0 %feed_forward.6 = (bf16[4096,768]{1,0:T(8,128)(2,1)}, bf16[4096,1536]{1,0:T(8,128)(2,1)}, bf16[4096,2048]{1,0:T(8,128)(2,1)}, bf16[4096,2048]{1,0:T(8,128)(2,1)}) custom-call(bf16[512,2048]{1,0:T(8,128)(2,1)} %held.40.refs_1_.refs_0_, ...), custom_call_target="tpu_custom_call", output_to_operand_aliasing={{0}: (6, {}), {1}: (7, {}), {2}: (8, {}), {3}: (9, {})} | custom-call | flops 9663676416 | bytes 26214400 | tf_op jit(solution)/shard_map/feed_forward/pallas_call | solution.py:143
  401.9 18.2 %feed_forward.7 = (bf16[4096,768]{1,0:T(8,128)(2,1)}, bf16[4096,1536]{1,0:T(8,128)(2,1)}, bf16[4096,2048]{1,0:T(8,128)(2,1)}, bf16[4096,2048]{1,0:T(8,128)(2,1)}) custom-call(bf16[512,2048]{1,0:T(8,128)(2,1)} %held.42.refs_0_, bf16[512,2048]{1,0:T(8,128)(2,1)} %copy-done.27, ...), custom_call_target="tpu_custom_call", output_to_operand_aliasing={{0}: (6, {}), {1}: (7, {}), {2}: (8, {}), {3}: (9, {})} | custom-call | flops 9663676416 | bytes 26214400 | tf_op jit(solution)/shard_map/feed_forward/pallas_call | solution.py:143
  420.1 10.8 %block_product.15.refs_2_ = bf16[2,512,2048]{2,1,0:T(8,128)(2,1)} custom-call(bf16[4096,1536]{1,0:T(8,128)(2,1)} %get-tuple-element.85.refs_0_, bf16[2048,1536]{1,0:T(8,128)(2,1)} %constant_dynamic-update-slice_fusion.refs_6_.refs_4_.refs_1_), custom_call_target="tpu_custom_call" | custom-call | flops 6442450944 | bytes 17825792 | tf_op jit(solution)/shard_map/block_product/pallas_call | solution.py:143
  431.0 10.8 %block_product.16.refs_3_ = bf16[2,512,2048]{2,1,0:T(8,128)(2,1)} custom-call(bf16[4096,1536]{1,0:T(8,128)(2,1)} %get-tuple-element.85.refs_0_, bf16[2048,1536]{1,0:T(8,128)(2,1)} %constant_dynamic-update-slice_fusion.refs_6_.refs_4_.refs_1_, bf16[2,512,2048]{2,1,0:T(8,128)(2,1)} %block_product.15.refs_2_), custom_call_target="tpu_custom_call" | custom-call | flops 6442450944 | bytes 17825792 | tf_op jit(solution)/shard_map/block_product/pallas_call | solution.py:143
  442.1 11.1 %block_product.17 = (bf16[1,512,2048]{2,1,0:T(8,128)(2,1)}, bf16[1,512,2048]{2,1,0:T(8,128)(2,1)}) custom-call(bf16[4096,1536]{1,0:T(8,128)(2,1)} %get-tuple-element.85.refs_0_, bf16[2048,1536]{1,0:T(8,128)(2,1)} %constant_dynamic-update-slice_fusion.refs_6_.refs_4_.refs_1_, bf16[2,512,2048]{2,1,0:T(8,128)(2,1)} %collective-permute-done.31.refs_2_, ...), custom_call_target="tpu_custom_call" | custom-call | flops 6442450944 | bytes 17825792 | tf_op jit(solution)/shard_map/block_product/pallas_call | solution.py:143
  454.8 19.9 %convolution_convert_fusion.2.refs_4_.refs_0_ = bf16[768,2048]{1,0:T(8,128)(2,1)} fusion(bf16[4096,768]{1,0:T(8,128)(2,1)} %get-tuple-element.84.refs_0_, bf16[4096,2048]{1,0:T(8,128)(2,1)} %held.44), kind=kOutput, calls=%fused_computation.6 | convolution fusion | flops 12886474752 | bytes 26214400 | tf_op jit(solution)/shard_map/dot_general | solution.py:28
  491.6 34.0 %convolution_convert_fusion.1.refs_5_.refs_0_ = bf16[2048,1536]{1,0:T(8,128)(2,1)} fusion(bf16[4096,2048]{1,0:T(8,128)(2,1)} %held.45, bf16[4096,1536]{1,0:T(8,128)(2,1)} %get-tuple-element.85.refs_0_), kind=kOutput, calls=%fused_computation.1 | convolution fusion | flops 25772949504 | bytes 35651584 | tf_op jit(solution)/shard_map/dot_general | solution.py:28
  525.6 12.3 %collective-permute-done.34.refs_4_ = bf16[1,512,2048]{2,1,0:T(8,128)(2,1)S(1)} collective-permute-done((bf16[1,512,2048]{2,1,0:T(8,128)(2,1)}, bf16[1,512,2048]{2,1,0:T(8,128)(2,1)S(1)}, u32[]{:S(2)}, u32[]{:S(2)}) %collective-permute-start.34) | collective-permute-done | bytes 2097184 | tf_op jit(solution)/shard_map/ppermute | solution.py:80
  539.2 9.0 block_product.19
  548.3 16.6 %norm_back.2 = (f32[512,2048]{1,0:T(8,128)}, f32[8,2048]{1,0:T(8,128)}, bf16[512,2048]{1,0:T(8,128)(2,1)}, bf16[8,512,128]{2,1,0:T(8,128)(2,1)}, bf16[8,512,128]{2,1,0:T(8,128)(2,1)}) custom-call(bf16[512,2048]{1,0:T(8,128)(2,1)} %bitcast.49, f32[512,2048]{1,0:T(8,128)} %get-tuple-element.69.refs_1_, f32[1,2048]{1,0:T(1,128)} %reshape.114.refs_4_.refs_2_, ...), custom_call_target="tpu_custom_call" | custom-call | flops 4315938816 | bytes 25165824 | tf_op jit(solution)/shard_map/norm_back/pallas_call | solution.py:143
  614.8 62.8 %attend_back.2.refs_0_ = bf16[4096,384]{1,0:T(8,128)(2,1)} custom-call(s32[8]{0:T(128)} %fusion.2.refs_0_, bf16[4096,128]{1,0:T(8,128)(2,1)} %get-tuple-element.59.refs_0_.refs_1_, bf16[4096,128]{1,0:T(8,128)(2,1)} %get-tuple-element.60.refs_1_.refs_2_, bf16[4096,128]{1,0:T(8,128)(2,1)} %get-tuple-element.61.refs_2_.refs_3_, bf16[4096,128]{1,0:T(8,128)(2,1)} %bitcast.67, ...), custom_call_target="tpu_custom_call" | custom-call | flops 25769803776 | bytes 8388608 | tf_op jit(solution)/shard_map/attend_back/pallas_call | solution.py:143
  677.6 14.2 %convolution_convert_fusion.4.refs_10_.refs_3_.refs_6_ = bf16[2048,384]{1,0:T(8,128)(2,1)} fusion(bf16[4096,2048]{1,0:T(8,128)(2,1)} %first_norm.15.x_ref.refs_0_, bf16[4096,384]{1,0:T(8,128)(2,1)} %attend_back.2.refs_0_), kind=kOutput, calls=%fused_computation.8 | convolution fusion | flops 6443237376 | bytes 21495808 | tf_op jit(solution)/shard_map/dot_general | solution.py:28
  711.6 62.8 %attend_back.3.refs_1_ = bf16[4096,384]{1,0:T(8,128)(2,1)} custom-call(s32[8]{0:T(128)} %fusion.2.refs_0_, bf16[4096,128]{1,0:T(8,128)(2,1)} %get-tuple-element.63.refs_0_.refs_1_, bf16[4096,128]{1,0:T(8,128)(2,1)} %get-tuple-element.64.refs_1_.refs_2_, bf16[4096,128]{1,0:T(8,128)(2,1)} %get-tuple-element.65.refs_2_.refs_3_, bf16[4096,128]{1,0:T(8,128)(2,1)} %bitcast.66, ...), custom_call_target="tpu_custom_call" | custom-call | flops 25769803776 | bytes 8388608 | tf_op jit(solution)/shard_map/attend_back/pallas_call | solution.py:143
  805.0 13.3 %convolution_convert_fusion.3.refs_7_ = bf16[2048,384]{1,0:T(8,128)(2,1)} fusion(bf16[4096,2048]{1,0:T(8,128)(2,1)} %held.49, bf16[4096,384]{1,0:T(8,128)(2,1)S(1)} %copy-done.2), kind=kOutput, calls=%fused_computation.7 | convolution fusion | flops 6443237376 | bytes 21495808 | tf_op jit(solution)/shard_map/dot_general | solution.py:28
  872.3 15.0 %collective-permute-done.46.refs_6_ = bf16[1,512,2048]{2,1,0:T(8,128)(2,1)} collective-permute-done((bf16[1,512,2048]{2,1,0:T(8,128)(2,1)}, bf16[1,512,2048]{2,1,0:T(8,128)(2,1)}, u32[]{:S(2)}, u32[]{:S(2)}) %collective-permute-start.46) | collective-permute-done | bytes 2097184 | tf_op jit(solution)/shard_map/ppermute | solution.py:80
  (333 shorter events, 386.6 us)
Async XLA Ops:
  16.2 64.7 %collective-permute-start.1 = (bf16[512,2048]{1,0:T(8,128)(2,1)S(1)}, bf16[512,2048]{1,0:T(8,128)(2,1)}, u32[]{:S(2)}, u32[]{:S(2)}) collective-permute-start(bf16[512,2048]{1,0:T(8,128)(2,1)S(1)} %bitcast.53), channel_id=1, source_target_pairs={{0,1},{1,0},{2,3},{3,2},{4,5},{5,4},{6,7},{7,6},{8,9},{9,8},{10,11... | collective-permute-start | bytes 6291464 | tf_op jit(solution)/shard_map/ppermute | solution.py:76
  18.9 65.8 %collective-permute-start = (bf16[512,2048]{1,0:T(8,128)(2,1)S(1)}, bf16[512,2048]{1,0:T(8,128)(2,1)}, u32[]{:S(2)}, u32[]{:S(2)}) collective-permute-start(bf16[512,2048]{1,0:T(8,128)(2,1)S(1)} %bitcast.54), channel_id=1, source_target_pairs={{0,2},{1,5},{2,0},{3,7},{4,6},{5,1},{6,4},{7,3},{8,10},{9,13},{10,... | collective-permute-start | bytes 6291464 | tf_op jit(solution)/shard_map/ppermute | solution.py:76
  20.4 65.2 %collective-permute-start.8 = (bf16[512,2048]{1,0:T(8,128)(2,1)S(1)}, bf16[512,2048]{1,0:T(8,128)(2,1)}, u32[]{:S(2)}, u32[]{:S(2)}) collective-permute-start(bf16[512,2048]{1,0:T(8,128)(2,1)S(1)} %bitcast.55), channel_id=1, source_target_pairs={{0,4},{1,3},{2,6},{3,1},{4,0},{5,7},{6,2},{7,5},{8,12},{9,11},{10,... | collective-permute-start | bytes 6291464 | tf_op jit(solution)/shard_map/ppermute | solution.py:76
  63.3 236.5 %all-gather.5.cloned.1.call-start = ((), (), s32[]{:S(2)}) async-start(), calls=%async_computation.16 | async-start | bytes 3932160 | tf_op jit(solution)/shard_map/all_gather | solution.py:877
  118.1 181.8 %all-gather.3.cloned.1.call-start = ((), (), s32[]{:S(2)}) async-start(), calls=%async_computation.15 | async-start | bytes 9437184 | tf_op jit(solution)/shard_map/all_gather | solution.py:876
  156.7 57.5 %collective-permute-start.14 = (bf16[512,2048]{1,0:T(8,128)(2,1)}, bf16[512,2048]{1,0:T(8,128)(2,1)}, u32[]{:S(2)}, u32[]{:S(2)}) collective-permute-start(bf16[512,2048]{1,0:T(8,128)(2,1)} %held.31.refs_2_.refs_3_), channel_id=1, source_target_pairs={{0,2},{1,5},{2,0},{3,7},{4,6},{5,1},{6,4},{7,3},{8,10},{9,13},{10,... | collective-permute-start | bytes 6291464 | tf_op jit(solution)/shard_map/ppermute | solution.py:76
  158.7 57.1 %collective-permute-start.13 = (bf16[512,2048]{1,0:T(8,128)(2,1)}, bf16[512,2048]{1,0:T(8,128)(2,1)}, u32[]{:S(2)}, u32[]{:S(2)}) collective-permute-start(bf16[512,2048]{1,0:T(8,128)(2,1)} %held.31.refs_2_.refs_3_), channel_id=1, source_target_pairs={{0,1},{1,0},{2,3},{3,2},{4,5},{5,4},{6,7},{7,6},{8,9},{9,8},{10,11... | collective-permute-start | bytes 6291464 | tf_op jit(solution)/shard_map/ppermute | solution.py:76
  158.7 57.1 %collective-permute-start.15 = (bf16[512,2048]{1,0:T(8,128)(2,1)}, bf16[512,2048]{1,0:T(8,128)(2,1)}, u32[]{:S(2)}, u32[]{:S(2)}) collective-permute-start(bf16[512,2048]{1,0:T(8,128)(2,1)} %held.31.refs_2_.refs_3_), channel_id=1, source_target_pairs={{0,4},{1,3},{2,6},{3,1},{4,0},{5,7},{6,2},{7,5},{8,12},{9,11},{10,... | collective-permute-start | bytes 6291464 | tf_op jit(solution)/shard_map/ppermute | solution.py:76
  160.2 52.5 %collective-permute-start.16 = (bf16[512,1536]{1,0:T(8,128)(2,1)S(1)}, bf16[512,1536]{1,0:T(8,128)(2,1)S(1)}, u32[]{:S(2)}, u32[]{:S(2)}) collective-permute-start(bf16[512,1536]{1,0:T(8,128)(2,1)S(1)} %copy-done.6), channel_id=1, source_target_pairs={{0,8},{8,16},{16,24},{24,0},{1,9},{9,17},{17,25},{25,1},{2,10},{10... | collective-permute-start | bytes 4718600 | tf_op jit(solution)/shard_map/ppermute | solution.py:879
  202.4 70.7 %all-to-all-start.2 = ((bf16[8,512,128]{2,1,0:T(8,128)(2,1)}), bf16[8,512,128]{2,1,0:T(8,128)(2,1)}, u32[]{:S(2)}, u32[]{:S(2)}) async-start(bf16[8,512,128]{2,1,0:T(8,128)(2,1)} %bitcast.65), calls=%async_computation.2 | async-start | bytes 2097152 | tf_op jit(solution)/shard_map/all_to_all | solution.py:790
  214.2 58.9 %collective-permute-start.17 = (bf16[512,2048]{1,0:T(8,128)(2,1)}, bf16[512,2048]{1,0:T(8,128)(2,1)}, u32[]{:S(2)}, u32[]{:S(2)}) collective-permute-start(bf16[512,2048]{1,0:T(8,128)(2,1)} %held.32.refs_4_.refs_2_), channel_id=1, source_target_pairs={{0,4},{1,3},{2,6},{3,1},{4,0},{5,7},{6,2},{7,5},{8,12},{9,11},{10,... | collective-permute-start | bytes 6291464 | tf_op jit(solution)/shard_map/ppermute | solution.py:76
  276.8 430.2 %reduce-scatter.10.cloned.1.call-start = ((), (), s32[]{:S(2)}) async-start(), calls=%async_computation.19 | async-start | bytes 7864320 | tf_op jit(solution)/shard_map/reduce_scatter | solution.py:937
  548.2 226.2 %reduce-scatter.8.cloned.1.call-start = ((), (), s32[]{:S(2)}) async-start(), calls=%async_computation.18 | async-start | bytes 3932160 | tf_op jit(solution)/shard_map/reduce_scatter | solution.py:935
  589.1 102.8 %collective-permute-start.39 = (bf16[2,256,2048]{2,1,0:T(8,128)(2,1)}, bf16[2,256,2048]{2,1,0:T(8,128)(2,1)S(1)}, u32[]{:S(2)}, u32[]{:S(2)}) collective-permute-start(bf16[2,256,2048]{2,1,0:T(8,128)(2,1)} %part.5.refs_2_), channel_id=1, source_target_pairs={{0,1},{1,0},{2,3},{3,2},{4,5},{5,4},{6,7},{7,6},{8,9},{9,8},{10,11... | collective-permute-start | bytes 6291464 | tf_op jit(solution)/shard_map/ppermute | solution.py:76
  592.8 118.8 %collective-permute-start.40 = (bf16[2,256,2048]{2,1,0:T(8,128)(2,1)}, bf16[2,256,2048]{2,1,0:T(8,128)(2,1)}, u32[]{:S(2)}, u32[]{:S(2)}) collective-permute-start(bf16[2,256,2048]{2,1,0:T(8,128)(2,1)} %part.6.refs_3_), channel_id=1, source_target_pairs={{0,1},{1,0},{2,3},{3,2},{4,5},{5,4},{6,7},{7,6},{8,9},{9,8},{10,11... | collective-permute-start | bytes 6291464 | tf_op jit(solution)/shard_map/ppermute | solution.py:76
  600.1 99.1 %collective-permute-start.35 = (bf16[2,512,2048]{2,1,0:T(8,128)(2,1)}, bf16[2,512,2048]{2,1,0:T(8,128)(2,1)}, u32[]{:S(2)}, u32[]{:S(2)}) collective-permute-start(bf16[2,512,2048]{2,1,0:T(8,128)(2,1)} %block_product.21.refs_3_), channel_id=1, source_target_pairs={{0,1},{1,0},{2,3},{3,2},{4,5},{5,4},{6,7},{7,6},{8,9},{9,8},{10,11... | collective-permute-start | bytes 12582920 | tf_op jit(solution)/shard_map/ppermute | solution.py:76
  608.5 90.6 %collective-permute-start.37 = (bf16[2,512,2048]{2,1,0:T(8,128)(2,1)}, bf16[2,512,2048]{2,1,0:T(8,128)(2,1)}, u32[]{:S(2)}, u32[]{:S(2)}) collective-permute-start(bf16[2,512,2048]{2,1,0:T(8,128)(2,1)} %block_product.22.refs_10_), channel_id=1, source_target_pairs={{4,0},{3,1},{6,2},{1,3},{0,4},{7,5},{2,6},{5,7},{12,8},{11,9},{14,... | collective-permute-start | bytes 12582920 | tf_op jit(solution)/shard_map/ppermute | solution.py:80
  611.2 95.9 %all-to-all-start.6 = ((bf16[8,512,128]{2,1,0:T(8,128)(2,1)}), bf16[8,512,128]{2,1,0:T(8,128)(2,1)S(1)}, u32[]{:S(2)}, u32[]{:S(2)}) async-start(bf16[8,512,128]{2,1,0:T(8,128)(2,1)} %get-tuple-element.92), calls=%async_computation.6 | async-start | bytes 2097152 | tf_op jit(solution)/shard_map/all_to_all | solution.py:790
  614.7 159.7 %reduce-scatter.6.cloned.1.call-start = ((), (), s32[]{:S(2)}) async-start(), calls=%async_computation.17 | async-start | bytes 1966080 | tf_op jit(solution)/shard_map/reduce_scatter | solution.py:949
  697.2 77.2 %collective-permute-start.41 = (bf16[2,256,2048]{2,1,0:T(8,128)(2,1)}, bf16[2,256,2048]{2,1,0:T(8,128)(2,1)S(1)}, u32[]{:S(2)}, u32[]{:S(2)}) collective-permute-start(bf16[2,256,2048]{2,1,0:T(8,128)(2,1)} %part.7.refs_12_), channel_id=1, source_target_pairs={{4,0},{3,1},{6,2},{1,3},{0,4},{7,5},{2,6},{5,7},{12,8},{11,9},{14,... | collective-permute-start | bytes 6291464 | tf_op jit(solution)/shard_map/ppermute | solution.py:80
  705.6 68.9 %collective-permute-start.38 = (bf16[1,512,2048]{2,1,0:T(8,128)(2,1)}, bf16[1,512,2048]{2,1,0:T(8,128)(2,1)}, u32[]{:S(2)}, u32[]{:S(2)}) collective-permute-start(bf16[1,512,2048]{2,1,0:T(8,128)(2,1)} %block_product.23.refs_11_), channel_id=1, source_target_pairs={{2,0},{5,1},{0,2},{7,3},{6,4},{1,5},{4,6},{3,7},{10,8},{13,9},{8,1... | collective-permute-start | bytes 6291464 | tf_op jit(solution)/shard_map/ppermute | solution.py:80
  707.0 67.5 %all-to-all-start.7 = ((bf16[8,64,1536]{2,1,0:T(8,128)(2,1)}), bf16[8,64,1536]{2,1,0:T(8,128)(2,1)}, u32[]{:S(2)}, u32[]{:S(2)}) async-start(bf16[8,64,1536]{2,1,0:T(8,128)(2,1)} %bitcast.64), calls=%async_computation.10 | async-start | bytes 3145728 | tf_op jit(solution)/shard_map/all_to_all | solution.py:790
  711.6 139.6 %reduce-scatter.12.cloned.1.call-start = ((), (), s32[]{:S(2)}) async-start(), calls=%async_computation.20 | async-start | bytes 1966080 | tf_op jit(solution)/shard_map/reduce_scatter | solution.py:967
  818.3 101.1 %reduce-scatter.14.cloned.1.call-start = ((), (), s32[]{:S(2)}) async-start(), calls=%async_computation.21 | async-start | bytes 1310720 | tf_op jit(solution)/shard_map/reduce_scatter | solution.py:973
  (84 other events, 1396.7 us)
Sparse Core Ops, SparseCore 0:
  118.2 74.4 all-gather.4
  194.6 77.8 all-gather.2
  548.3 108.2 reduce-scatter.9
  658.8 60.7 reduce-scatter.7
  722.3 35.3 reduce-scatter.5
  818.4 32.6 reduce-scatter.11
  853.4 26.0 reduce-scatter.13

commit v7 on v6

--- a/solution.py
+++ b/solution.py
@@ -540,30 +540,31 @@
     m_s[...] = jnp.full_like(m_s, masked_value)
     l_s[...] = jnp.zeros_like(l_s)
 
-    def body(j, masked):
+    def body(j, masked, start=0):
+        at = slice(start, bq)
         rows = pl.ds(pl.multiple_of(j * bk, bk), bk)
         k = k_ref[rows, :]
-        scores = [dot(k, qm[h], NT) for h in range(heads)]
+        scores = [dot(k, qm[h, at], NT) for h in range(heads)]
         if masked:
             key_at = lax.broadcasted_iota(jnp.int32, scores[0].shape, 0) + j * bk
-            query_at = lax.broadcasted_iota(jnp.int32, scores[0].shape, 1) + i * bq
+            query_at = lax.broadcasted_iota(jnp.int32, scores[0].shape, 1) + (i * bq + start)
             scores = [jnp.where(key_at <= query_at, s, masked_value) for s in scores]
-        m0 = m_s[...]
-        l0 = l_s[...]
+        m0 = m_s[:, at]
+        l0 = l_s[:, at]
         m1 = jnp.maximum(m0, jnp.concatenate([jnp.max(s, axis=0, keepdims=True) for s in scores] + [m0[heads:]], 0))
-        m_s[...] = m1
+        m_s[:, at] = m1
         kept = jnp.exp2((m0 - m1) * LOG2E_SCALE)
         base = m1 * LOG2E_SCALE
         raised = [jnp.exp2(scores[h] * LOG2E_SCALE - base[h : h + 1]) for h in range(heads)]
-        l_s[...] = l0 * kept + jnp.concatenate([jnp.sum(p, axis=0, keepdims=True) for p in raised] + [l0[heads:]], 0)
+        l_s[:, at] = l0 * kept + jnp.concatenate([jnp.sum(p, axis=0, keepdims=True) for p in raised] + [l0[heads:]], 0)
         for h in range(heads):
             part = slice(h * HEAD, (h + 1) * HEAD)
-            acc[part, :] = acc[part, :] * kept[h : h + 1] + dot(vt[part, rows], raised[h].astype(bf16), NN)
+            acc[part, at] = acc[part, at] * kept[h : h + 1] + dot(vt[part, rows], raised[h].astype(bf16), NN)
 
     whole = (i * bq) // bk
     lax.fori_loop(0, whole, lambda j, c: (body(j, False), c)[1], 0)
     for d in range(max(1, bq // bk)):
-        body(whole + d, True)
+        body(whole + d, True, d * bk)
     for h in range(heads):
         part = slice(h * HEAD, (h + 1) * HEAD)
         acc[part, :] = acc[part, :] * (1.0 / l_s[h : h + 1])

time: 938 us -> 934 us (level)
  transfers between devices with their start and end apart: 65 -> 65, of which waited for: 24 -> 23; matrix products, arithmetic and copies ran while one was open for 14% -> 14% of each run, Pallas kernels for 50% -> 49%
where the time goes in v7:
time: 934 us; the launch traced here: 925 us
  Pallas kernels  522 us (56%)
  waiting for transfers between devices  156 us (17%)
  matrix products  89.9 us (10%)
  starting transfers between devices  77.2 us (8%)
  local copies, waits for them, and re-layouts  53.4 us (6%)
  between operations  15 us (2%)
  other arithmetic  11.5 us (1%)
    pallas_call x69, Pallas kernels, launch(): pl.pallas_call(body, grid_spec=pltpu.PrefetchScalarGridSpec(num_scalar_pr...  501 us
    dot_general x5, matrix products, dot(): return lax.dot_general(a, b, dims, preferred_element_type=f32)  89.9 us
    ppermute x29, waiting for transfers between devices, send(): return lax.ppermute(value, 'sp', perm)  40.6 us
    ppermute x10, waiting for transfers between devices, back(): return lax.ppermute(value, 'sp', [(b, a) for a, b in perm])  38.4 us
    all_to_all x8, starting transfers between devices, swap_sp(): return lax.all_to_all(value, 'sp', split_axis=0, concat_axis=0, tiled=True)  31.1 us
    ppermute x3, waiting for transfers between devices, per_device(): joint_blocks.append(lax.ppermute(joint_blocks[-1], 'fsdp', ring))  27.9 us
    unnamed x90, local copies, waits for them, and re-layouts  25.3 us
    pallas_call x1, Pallas kernels, joint_projection(): pl.pallas_call(functools.partial(joint_kernel, width), grid_spec=pltpu.Pr...  20.8 us
  transfers between devices with their start and end apart: 65, of which 23 were waited for; matrix products, arithmetic and copies ran while one was open for 14% of the time, Pallas kernels for 49%

profile of v7, /device:TPU:0, one launch (start us, length us, event | category | flops | bytes accessed | tf_op | source)
XLA Modules:
  0.0 924.7 jit_solution(5697261501611433715)
XLA Ops:
  37.0 19.0 %collective-permute-done.5.refs_2_ = bf16[512,768]{1,0:T(8,128)(2,1)} collective-permute-done((bf16[512,768]{1,0:T(8,128)(2,1)}, bf16[512,768]{1,0:T(8,128)(2,1)}, u32[]{:S(2)}, u32[]{:S(2)}) %collective-permute-start.5) | collective-permute-done | bytes 786464 | tf_op jit(solution)/shard_map/ppermute | solution.py:847
  134.7 20.8 %joint_projection.1 = (bf16[4096,128]{1,0:T(8,128)(2,1)}, bf16[4096,128]{1,0:T(8,128)(2,1)}, bf16[4096,128]{1,0:T(8,128)(2,1)}, bf16[4096,128]{1,0:T(8,128)(2,1)...) custom-call(s32[8]{0:T(128)} %fusion.1.table_ref.refs_0_, bf16[4096,2048]{1,0:T(8,128)(2,1)} %first_norm.15.x_ref.refs_0_, ...), custom_call_target="tpu_custom_call" | custom-call | flops 12884901888 | bytes 23068672 | tf_op jit(solution)/shard_map/joint_projection/pallas_call | solution.py:498
  160.1 38.9 %attend.2 = (bf16[4096,128]{1,0:T(8,128)(2,1)}, f32[8,4096]{1,0:T(8,128)}) custom-call(bf16[4096,128]{1,0:T(8,128)(2,1)} %get-tuple-element.59.refs_0_.refs_1_, bf16[4096,128]{1,0:T(8,128)(2,1)} %get-tuple-element.60.refs_1_.refs_2_, bf16[4096,128]{1,0:T(8,128)(2,1)} %get-tuple-element.61.refs_2_.refs_3_), custom_call_target="tpu_custom_call" | custom-call | flops 17179869184 | bytes 4194304 | tf_op jit(solution)/shard_map/attend/pallas_call | solution.py:143
  203.4 9.3 %collective-permute-done.16.refs_0_ = bf16[512,1536]{1,0:T(8,128)(2,1)S(1)} collective-permute-done((bf16[512,1536]{1,0:T(8,128)(2,1)S(1)}, bf16[512,1536]{1,0:T(8,128)(2,1)S(1)}, u32[]{:S(2)}, u32[]{:S(2)}) %collective-permute-start.16) | collective-permute-done | bytes 1572896 | tf_op jit(solution)/shard_map/ppermute | solution.py:880
  215.4 39.0 %attend.3 = (bf16[4096,128]{1,0:T(8,128)(2,1)}, f32[8,4096]{1,0:T(8,128)}) custom-call(bf16[4096,128]{1,0:T(8,128)(2,1)} %get-tuple-element.63.refs_0_.refs_1_, bf16[4096,128]{1,0:T(8,128)(2,1)} %get-tuple-element.64.refs_1_.refs_2_, bf16[4096,128]{1,0:T(8,128)(2,1)} %get-tuple-element.65.refs_2_.refs_3_, bf16[512,2048]{1,0:T(8,128)(2,1)} %collective-permute-done.13.refs_3_, ...), custom_call_target="tpu_custom_call" | custom-call | flops 17179869184 | bytes 4194304 | tf_op jit(solution)/shard_map/attend/pallas_call | solution.py:143
  256.9 16.2 %collective-permute-done.17.refs_1_.refs_2_ = bf16[512,2048]{1,0:T(8,128)(2,1)} collective-permute-done((bf16[512,2048]{1,0:T(8,128)(2,1)}, bf16[512,2048]{1,0:T(8,128)(2,1)}, u32[]{:S(2)}, u32[]{:S(2)}) %collective-permute-start.17) | collective-permute-done | bytes 2097184 | tf_op jit(solution)/shard_map/ppermute | solution.py:76
  284.5 9.0 collective-permute-done.19
  297.1 12.8 %middle.1 = (f32[512,2048]{1,0:T(8,128)}, bf16[512,2048]{1,0:T(8,128)(2,1)}, bf16[512,2048]{1,0:T(8,128)(2,1)}, bf16[512,2048]{1,0:T(8,128)(2,1)}) custom-call(bf16[8,512,128]{2,1,0:T(8,128)(2,1)} %all-to-all-done.2.refs_0_, bf16[8,512,128]{2,1,0:T(8,128)(2,1)} %copy-done.20, bf16[2048,2048]{1,0:T(8,128)(2,1)} %all-gather.3.cloned.1.call-done.refs_2_.refs_4_, ...), custom_call_target="tpu_custom_call" | custom-call | flops 4294967296 | bytes 20971520 | tf_op jit(solution)/shard_map/middle/pallas_call | solution.py:143
  314.4 18.0 %feed_forward.4 = (bf16[4096,768]{1,0:T(8,128)(2,1)}, bf16[4096,1536]{1,0:T(8,128)(2,1)}, bf16[4096,2048]{1,0:T(8,128)(2,1)}, bf16[4096,2048]{1,0:T(8,128)(2,1)}) custom-call(bf16[512,2048]{1,0:T(8,128)(2,1)} %get-tuple-element.70.refs_0_, bf16[512,2048]{1,0:T(8,128)(2,1)} %collective-permute-done.21.refs_1_, bf16[512,2048]{1,0:T(8,128)(2,1)} %held.31.refs_2_.refs_3_, ...), custom_call_target="tpu_custom_call" | custom-call | flops 9663676416 | bytes 26214400 | tf_op jit(solution)/shard_map/feed_forward/pallas_call | solution.py:143
  342.0 18.0 %feed_forward.5 = (bf16[4096,768]{1,0:T(8,128)(2,1)}, bf16[4096,1536]{1,0:T(8,128)(2,1)}, bf16[4096,2048]{1,0:T(8,128)(2,1)}, bf16[4096,2048]{1,0:T(8,128)(2,1)}) custom-call(bf16[512,2048]{1,0:T(8,128)(2,1)} %held.38.refs_1_.refs_0_, ...), custom_call_target="tpu_custom_call", output_to_operand_aliasing={{0}: (6, {}), {1}: (7, {}), {2}: (8, {}), {3}: (9, {})} | custom-call | flops 9663676416 | bytes 26214400 | tf_op jit(solution)/shard_map/feed_forward/pallas_call | solution.py:143
  369.6 18.0 %feed_forward.6 = (bf16[4096,768]{1,0:T(8,128)(2,1)}, bf16[4096,1536]{1,0:T(8,128)(2,1)}, bf16[4096,2048]{1,0:T(8,128)(2,1)}, bf16[4096,2048]{1,0:T(8,128)(2,1)}) custom-call(bf16[512,2048]{1,0:T(8,128)(2,1)} %held.40.refs_1_.refs_0_, ...), custom_call_target="tpu_custom_call", output_to_operand_aliasing={{0}: (6, {}), {1}: (7, {}), {2}: (8, {}), {3}: (9, {})} | custom-call | flops 9663676416 | bytes 26214400 | tf_op jit(solution)/shard_map/feed_forward/pallas_call | solution.py:143
  398.4 18.2 %feed_forward.7 = (bf16[4096,768]{1,0:T(8,128)(2,1)}, bf16[4096,1536]{1,0:T(8,128)(2,1)}, bf16[4096,2048]{1,0:T(8,128)(2,1)}, bf16[4096,2048]{1,0:T(8,128)(2,1)}) custom-call(bf16[512,2048]{1,0:T(8,128)(2,1)} %held.42.refs_0_, bf16[512,2048]{1,0:T(8,128)(2,1)} %copy-done.27, ...), custom_call_target="tpu_custom_call", output_to_operand_aliasing={{0}: (6, {}), {1}: (7, {}), {2}: (8, {}), {3}: (9, {})} | custom-call | flops 9663676416 | bytes 26214400 | tf_op jit(solution)/shard_map/feed_forward/pallas_call | solution.py:143
  416.6 10.8 %block_product.15.refs_2_ = bf16[2,512,2048]{2,1,0:T(8,128)(2,1)} custom-call(bf16[4096,1536]{1,0:T(8,128)(2,1)} %get-tuple-element.85.refs_0_, bf16[2048,1536]{1,0:T(8,128)(2,1)} %constant_dynamic-update-slice_fusion.refs_6_.refs_4_.refs_1_), custom_call_target="tpu_custom_call" | custom-call | flops 6442450944 | bytes 17825792 | tf_op jit(solution)/shard_map/block_product/pallas_call | solution.py:143
  427.5 10.8 %block_product.16.refs_3_ = bf16[2,512,2048]{2,1,0:T(8,128)(2,1)} custom-call(bf16[4096,1536]{1,0:T(8,128)(2,1)} %get-tuple-element.85.refs_0_, bf16[2048,1536]{1,0:T(8,128)(2,1)} %constant_dynamic-update-slice_fusion.refs_6_.refs_4_.refs_1_, bf16[2,512,2048]{2,1,0:T(8,128)(2,1)} %block_product.15.refs_2_), custom_call_target="tpu_custom_call" | custom-call | flops 6442450944 | bytes 17825792 | tf_op jit(solution)/shard_map/block_product/pallas_call | solution.py:143
  438.7 11.1 %block_product.17 = (bf16[1,512,2048]{2,1,0:T(8,128)(2,1)}, bf16[1,512,2048]{2,1,0:T(8,128)(2,1)}) custom-call(bf16[4096,1536]{1,0:T(8,128)(2,1)} %get-tuple-element.85.refs_0_, bf16[2048,1536]{1,0:T(8,128)(2,1)} %constant_dynamic-update-slice_fusion.refs_6_.refs_4_.refs_1_, bf16[2,512,2048]{2,1,0:T(8,128)(2,1)} %collective-permute-done.31.refs_2_, ...), custom_call_target="tpu_custom_call" | custom-call | flops 6442450944 | bytes 17825792 | tf_op jit(solution)/shard_map/block_product/pallas_call | solution.py:143
  451.3 19.9 %convolution_convert_fusion.2.refs_4_.refs_0_ = bf16[768,2048]{1,0:T(8,128)(2,1)} fusion(bf16[4096,768]{1,0:T(8,128)(2,1)} %get-tuple-element.84.refs_0_, bf16[4096,2048]{1,0:T(8,128)(2,1)} %held.44), kind=kOutput, calls=%fused_computation.6 | convolution fusion | flops 12886474752 | bytes 26214400 | tf_op jit(solution)/shard_map/dot_general | solution.py:28
  488.0 34.0 %convolution_convert_fusion.1.refs_5_.refs_0_ = bf16[2048,1536]{1,0:T(8,128)(2,1)} fusion(bf16[4096,2048]{1,0:T(8,128)(2,1)} %held.45, bf16[4096,1536]{1,0:T(8,128)(2,1)} %get-tuple-element.85.refs_0_), kind=kOutput, calls=%fused_computation.1 | convolution fusion | flops 25772949504 | bytes 35651584 | tf_op jit(solution)/shard_map/dot_general | solution.py:28
  521.9 12.3 %collective-permute-done.34.refs_4_ = bf16[1,512,2048]{2,1,0:T(8,128)(2,1)S(1)} collective-permute-done((bf16[1,512,2048]{2,1,0:T(8,128)(2,1)}, bf16[1,512,2048]{2,1,0:T(8,128)(2,1)S(1)}, u32[]{:S(2)}, u32[]{:S(2)}) %collective-permute-start.34) | collective-permute-done | bytes 2097184 | tf_op jit(solution)/shard_map/ppermute | solution.py:80
  544.6 16.6 %norm_back.2 = (f32[512,2048]{1,0:T(8,128)}, f32[8,2048]{1,0:T(8,128)}, bf16[512,2048]{1,0:T(8,128)(2,1)}, bf16[8,512,128]{2,1,0:T(8,128)(2,1)}, bf16[8,512,128]{2,1,0:T(8,128)(2,1)}) custom-call(bf16[512,2048]{1,0:T(8,128)(2,1)} %bitcast.49, f32[512,2048]{1,0:T(8,128)} %get-tuple-element.69.refs_1_, f32[1,2048]{1,0:T(1,128)} %reshape.114.refs_4_.refs_2_, ...), custom_call_target="tpu_custom_call" | custom-call | flops 4315938816 | bytes 25165824 | tf_op jit(solution)/shard_map/norm_back/pallas_call | solution.py:143
  611.4 62.8 %attend_back.2.refs_0_ = bf16[4096,384]{1,0:T(8,128)(2,1)} custom-call(s32[8]{0:T(128)} %fusion.2.refs_0_, bf16[4096,128]{1,0:T(8,128)(2,1)} %get-tuple-element.59.refs_0_.refs_1_, bf16[4096,128]{1,0:T(8,128)(2,1)} %get-tuple-element.60.refs_1_.refs_2_, bf16[4096,128]{1,0:T(8,128)(2,1)} %get-tuple-element.61.refs_2_.refs_3_, bf16[4096,128]{1,0:T(8,128)(2,1)} %bitcast.67, ...), custom_call_target="tpu_custom_call" | custom-call | flops 25769803776 | bytes 8388608 | tf_op jit(solution)/shard_map/attend_back/pallas_call | solution.py:143
  674.1 14.2 %convolution_convert_fusion.4.refs_10_.refs_3_.refs_6_ = bf16[2048,384]{1,0:T(8,128)(2,1)} fusion(bf16[4096,2048]{1,0:T(8,128)(2,1)} %first_norm.15.x_ref.refs_0_, bf16[4096,384]{1,0:T(8,128)(2,1)} %attend_back.2.refs_0_), kind=kOutput, calls=%fused_computation.8 | convolution fusion | flops 6443237376 | bytes 21495808 | tf_op jit(solution)/shard_map/dot_general | solution.py:28
  708.2 62.8 %attend_back.3.refs_1_ = bf16[4096,384]{1,0:T(8,128)(2,1)} custom-call(s32[8]{0:T(128)} %fusion.2.refs_0_, bf16[4096,128]{1,0:T(8,128)(2,1)} %get-tuple-element.63.refs_0_.refs_1_, bf16[4096,128]{1,0:T(8,128)(2,1)} %get-tuple-element.64.refs_1_.refs_2_, bf16[4096,128]{1,0:T(8,128)(2,1)} %get-tuple-element.65.refs_2_.refs_3_, bf16[4096,128]{1,0:T(8,128)(2,1)} %bitcast.66, ...), custom_call_target="tpu_custom_call" | custom-call | flops 25769803776 | bytes 8388608 | tf_op jit(solution)/shard_map/attend_back/pallas_call | solution.py:143
  801.6 13.3 %convolution_convert_fusion.3.refs_7_ = bf16[2048,384]{1,0:T(8,128)(2,1)} fusion(bf16[4096,2048]{1,0:T(8,128)(2,1)} %held.49, bf16[4096,384]{1,0:T(8,128)(2,1)S(1)} %copy-done.2), kind=kOutput, calls=%fused_computation.7 | convolution fusion | flops 6443237376 | bytes 21495808 | tf_op jit(solution)/shard_map/dot_general | solution.py:28
  868.8 15.0 %collective-permute-done.46.refs_6_ = bf16[1,512,2048]{2,1,0:T(8,128)(2,1)} collective-permute-done((bf16[1,512,2048]{2,1,0:T(8,128)(2,1)}, bf16[1,512,2048]{2,1,0:T(8,128)(2,1)}, u32[]{:S(2)}, u32[]{:S(2)}) %collective-permute-start.46) | collective-permute-done | bytes 2097184 | tf_op jit(solution)/shard_map/ppermute | solution.py:80
  (333 shorter events, 389.0 us)
Async XLA Ops:
  16.2 64.7 %collective-permute-start.1 = (bf16[512,2048]{1,0:T(8,128)(2,1)S(1)}, bf16[512,2048]{1,0:T(8,128)(2,1)}, u32[]{:S(2)}, u32[]{:S(2)}) collective-permute-start(bf16[512,2048]{1,0:T(8,128)(2,1)S(1)} %bitcast.53), channel_id=1, source_target_pairs={{0,1},{1,0},{2,3},{3,2},{4,5},{5,4},{6,7},{7,6},{8,9},{9,8},{10,11... | collective-permute-start | bytes 6291464 | tf_op jit(solution)/shard_map/ppermute | solution.py:76
  18.9 65.8 %collective-permute-start = (bf16[512,2048]{1,0:T(8,128)(2,1)S(1)}, bf16[512,2048]{1,0:T(8,128)(2,1)}, u32[]{:S(2)}, u32[]{:S(2)}) collective-permute-start(bf16[512,2048]{1,0:T(8,128)(2,1)S(1)} %bitcast.54), channel_id=1, source_target_pairs={{0,2},{1,5},{2,0},{3,7},{4,6},{5,1},{6,4},{7,3},{8,10},{9,13},{10,... | collective-permute-start | bytes 6291464 | tf_op jit(solution)/shard_map/ppermute | solution.py:76
  20.4 65.2 %collective-permute-start.8 = (bf16[512,2048]{1,0:T(8,128)(2,1)S(1)}, bf16[512,2048]{1,0:T(8,128)(2,1)}, u32[]{:S(2)}, u32[]{:S(2)}) collective-permute-start(bf16[512,2048]{1,0:T(8,128)(2,1)S(1)} %bitcast.55), channel_id=1, source_target_pairs={{0,4},{1,3},{2,6},{3,1},{4,0},{5,7},{6,2},{7,5},{8,12},{9,11},{10,... | collective-permute-start | bytes 6291464 | tf_op jit(solution)/shard_map/ppermute | solution.py:76
  63.3 232.8 %all-gather.5.cloned.1.call-start = ((), (), s32[]{:S(2)}) async-start(), calls=%async_computation.16 | async-start | bytes 3932160 | tf_op jit(solution)/shard_map/all_gather | solution.py:878
  118.1 178.1 %all-gather.3.cloned.1.call-start = ((), (), s32[]{:S(2)}) async-start(), calls=%async_computation.15 | async-start | bytes 9437184 | tf_op jit(solution)/shard_map/all_gather | solution.py:877
  156.7 57.2 %collective-permute-start.14 = (bf16[512,2048]{1,0:T(8,128)(2,1)}, bf16[512,2048]{1,0:T(8,128)(2,1)}, u32[]{:S(2)}, u32[]{:S(2)}) collective-permute-start(bf16[512,2048]{1,0:T(8,128)(2,1)} %held.31.refs_2_.refs_3_), channel_id=1, source_target_pairs={{0,2},{1,5},{2,0},{3,7},{4,6},{5,1},{6,4},{7,3},{8,10},{9,13},{10,... | collective-permute-start | bytes 6291464 | tf_op jit(solution)/shard_map/ppermute | solution.py:76
  158.6 56.7 %collective-permute-start.13 = (bf16[512,2048]{1,0:T(8,128)(2,1)}, bf16[512,2048]{1,0:T(8,128)(2,1)}, u32[]{:S(2)}, u32[]{:S(2)}) collective-permute-start(bf16[512,2048]{1,0:T(8,128)(2,1)} %held.31.refs_2_.refs_3_), channel_id=1, source_target_pairs={{0,1},{1,0},{2,3},{3,2},{4,5},{5,4},{6,7},{7,6},{8,9},{9,8},{10,11... | collective-permute-start | bytes 6291464 | tf_op jit(solution)/shard_map/ppermute | solution.py:76
  158.6 56.7 %collective-permute-start.15 = (bf16[512,2048]{1,0:T(8,128)(2,1)}, bf16[512,2048]{1,0:T(8,128)(2,1)}, u32[]{:S(2)}, u32[]{:S(2)}) collective-permute-start(bf16[512,2048]{1,0:T(8,128)(2,1)} %held.31.refs_2_.refs_3_), channel_id=1, source_target_pairs={{0,4},{1,3},{2,6},{3,1},{4,0},{5,7},{6,2},{7,5},{8,12},{9,11},{10,... | collective-permute-start | bytes 6291464 | tf_op jit(solution)/shard_map/ppermute | solution.py:76
  160.1 52.5 %collective-permute-start.16 = (bf16[512,1536]{1,0:T(8,128)(2,1)S(1)}, bf16[512,1536]{1,0:T(8,128)(2,1)S(1)}, u32[]{:S(2)}, u32[]{:S(2)}) collective-permute-start(bf16[512,1536]{1,0:T(8,128)(2,1)S(1)} %copy-done.6), channel_id=1, source_target_pairs={{0,8},{8,16},{16,24},{24,0},{1,9},{9,17},{17,25},{25,1},{2,10},{10... | collective-permute-start | bytes 4718600 | tf_op jit(solution)/shard_map/ppermute | solution.py:880
  199.1 74.0 %all-to-all-start.2 = ((bf16[8,512,128]{2,1,0:T(8,128)(2,1)}), bf16[8,512,128]{2,1,0:T(8,128)(2,1)}, u32[]{:S(2)}, u32[]{:S(2)}) async-start(bf16[8,512,128]{2,1,0:T(8,128)(2,1)} %bitcast.65), calls=%async_computation.2 | async-start | bytes 2097152 | tf_op jit(solution)/shard_map/all_to_all | solution.py:791
  213.8 59.3 %collective-permute-start.17 = (bf16[512,2048]{1,0:T(8,128)(2,1)}, bf16[512,2048]{1,0:T(8,128)(2,1)}, u32[]{:S(2)}, u32[]{:S(2)}) collective-permute-start(bf16[512,2048]{1,0:T(8,128)(2,1)} %held.32.refs_4_.refs_2_), channel_id=1, source_target_pairs={{0,4},{1,3},{2,6},{3,1},{4,0},{5,7},{6,2},{7,5},{8,12},{9,11},{10,... | collective-permute-start | bytes 6291464 | tf_op jit(solution)/shard_map/ppermute | solution.py:76
  276.8 426.9 %reduce-scatter.10.cloned.1.call-start = ((), (), s32[]{:S(2)}) async-start(), calls=%async_computation.19 | async-start | bytes 7864320 | tf_op jit(solution)/shard_map/reduce_scatter | solution.py:938
  544.5 226.6 %reduce-scatter.8.cloned.1.call-start = ((), (), s32[]{:S(2)}) async-start(), calls=%async_computation.18 | async-start | bytes 3932160 | tf_op jit(solution)/shard_map/reduce_scatter | solution.py:936
  585.6 102.8 %collective-permute-start.39 = (bf16[2,256,2048]{2,1,0:T(8,128)(2,1)}, bf16[2,256,2048]{2,1,0:T(8,128)(2,1)S(1)}, u32[]{:S(2)}, u32[]{:S(2)}) collective-permute-start(bf16[2,256,2048]{2,1,0:T(8,128)(2,1)} %part.5.refs_2_), channel_id=1, source_target_pairs={{0,1},{1,0},{2,3},{3,2},{4,5},{5,4},{6,7},{7,6},{8,9},{9,8},{10,11... | collective-permute-start | bytes 6291464 | tf_op jit(solution)/shard_map/ppermute | solution.py:76
  589.4 118.9 %collective-permute-start.40 = (bf16[2,256,2048]{2,1,0:T(8,128)(2,1)}, bf16[2,256,2048]{2,1,0:T(8,128)(2,1)}, u32[]{:S(2)}, u32[]{:S(2)}) collective-permute-start(bf16[2,256,2048]{2,1,0:T(8,128)(2,1)} %part.6.refs_3_), channel_id=1, source_target_pairs={{0,1},{1,0},{2,3},{3,2},{4,5},{5,4},{6,7},{7,6},{8,9},{9,8},{10,11... | collective-permute-start | bytes 6291464 | tf_op jit(solution)/shard_map/ppermute | solution.py:76
  596.6 99.1 %collective-permute-start.35 = (bf16[2,512,2048]{2,1,0:T(8,128)(2,1)}, bf16[2,512,2048]{2,1,0:T(8,128)(2,1)}, u32[]{:S(2)}, u32[]{:S(2)}) collective-permute-start(bf16[2,512,2048]{2,1,0:T(8,128)(2,1)} %block_product.21.refs_3_), channel_id=1, source_target_pairs={{0,1},{1,0},{2,3},{3,2},{4,5},{5,4},{6,7},{7,6},{8,9},{9,8},{10,11... | collective-permute-start | bytes 12582920 | tf_op jit(solution)/shard_map/ppermute | solution.py:76
  605.1 90.7 %collective-permute-start.37 = (bf16[2,512,2048]{2,1,0:T(8,128)(2,1)}, bf16[2,512,2048]{2,1,0:T(8,128)(2,1)}, u32[]{:S(2)}, u32[]{:S(2)}) collective-permute-start(bf16[2,512,2048]{2,1,0:T(8,128)(2,1)} %block_product.22.refs_10_), channel_id=1, source_target_pairs={{4,0},{3,1},{6,2},{1,3},{0,4},{7,5},{2,6},{5,7},{12,8},{11,9},{14,... | collective-permute-start | bytes 12582920 | tf_op jit(solution)/shard_map/ppermute | solution.py:80
  607.7 95.9 %all-to-all-start.6 = ((bf16[8,512,128]{2,1,0:T(8,128)(2,1)}), bf16[8,512,128]{2,1,0:T(8,128)(2,1)S(1)}, u32[]{:S(2)}, u32[]{:S(2)}) async-start(bf16[8,512,128]{2,1,0:T(8,128)(2,1)} %get-tuple-element.92), calls=%async_computation.6 | async-start | bytes 2097152 | tf_op jit(solution)/shard_map/all_to_all | solution.py:791
  611.3 159.8 %reduce-scatter.6.cloned.1.call-start = ((), (), s32[]{:S(2)}) async-start(), calls=%async_computation.17 | async-start | bytes 1966080 | tf_op jit(solution)/shard_map/reduce_scatter | solution.py:950
  693.8 77.3 %collective-permute-start.41 = (bf16[2,256,2048]{2,1,0:T(8,128)(2,1)}, bf16[2,256,2048]{2,1,0:T(8,128)(2,1)S(1)}, u32[]{:S(2)}, u32[]{:S(2)}) collective-permute-start(bf16[2,256,2048]{2,1,0:T(8,128)(2,1)} %part.7.refs_12_), channel_id=1, source_target_pairs={{4,0},{3,1},{6,2},{1,3},{0,4},{7,5},{2,6},{5,7},{12,8},{11,9},{14,... | collective-permute-start | bytes 6291464 | tf_op jit(solution)/shard_map/ppermute | solution.py:80
  702.2 68.9 %collective-permute-start.38 = (bf16[1,512,2048]{2,1,0:T(8,128)(2,1)}, bf16[1,512,2048]{2,1,0:T(8,128)(2,1)}, u32[]{:S(2)}, u32[]{:S(2)}) collective-permute-start(bf16[1,512,2048]{2,1,0:T(8,128)(2,1)} %block_product.23.refs_11_), channel_id=1, source_target_pairs={{2,0},{5,1},{0,2},{7,3},{6,4},{1,5},{4,6},{3,7},{10,8},{13,9},{8,1... | collective-permute-start | bytes 6291464 | tf_op jit(solution)/shard_map/ppermute | solution.py:80
  703.7 67.4 %all-to-all-start.7 = ((bf16[8,64,1536]{2,1,0:T(8,128)(2,1)}), bf16[8,64,1536]{2,1,0:T(8,128)(2,1)}, u32[]{:S(2)}, u32[]{:S(2)}) async-start(bf16[8,64,1536]{2,1,0:T(8,128)(2,1)} %bitcast.64), calls=%async_computation.10 | async-start | bytes 3145728 | tf_op jit(solution)/shard_map/all_to_all | solution.py:791
  708.2 139.4 %reduce-scatter.12.cloned.1.call-start = ((), (), s32[]{:S(2)}) async-start(), calls=%async_computation.20 | async-start | bytes 1966080 | tf_op jit(solution)/shard_map/reduce_scatter | solution.py:968
  814.9 101.0 %reduce-scatter.14.cloned.1.call-start = ((), (), s32[]{:S(2)}) async-start(), calls=%async_computation.21 | async-start | bytes 1310720 | tf_op jit(solution)/shard_map/reduce_scatter | solution.py:974
  (84 other events, 1389.9 us)
Sparse Core Ops, SparseCore 0:
  118.2 74.5 all-gather.4
  194.6 79.1 all-gather.2
  544.6 108.2 reduce-scatter.9
  655.1 60.7 reduce-scatter.7
  718.7 35.2 reduce-scatter.5
  815.0 32.5 reduce-scatter.11
  849.9 26.1 reduce-scatter.13
